TPU v7x, 32 devices: a whole 2x2x4 slice. The times are simulated.
32 devices in a mesh: sensor: 16 (over z, y, x), tm: 2 (over core).
Axes of the slice: x: 2, y: 2, z: 4, core: 2. Of those that a mesh axis runs over, the one named last changes fastest.
Arguments:
- inputs: bfloat16 [1024, 32, 128], P('sensor', 'tm'), may hold values from -6 to 6
- mask: int32 [1024, 32], P('sensor', 'tm'), may hold values 0 or 1
- projector: float32 [64, 128], replicated, may hold values from -6 to 6
- w_key: bfloat16 [128, 128], replicated, may hold values from -0.5 to 0.5
- w_value: bfloat16 [128, 128], replicated, may hold values from -0.5 to 0.5
- w_query: bfloat16 [128, 128], replicated, may hold values from -0.5 to 0.5
- w_out: bfloat16 [128, 128], replicated, may hold values from -0.5 to 0.5
- cotangent: bfloat16 [1024, 32, 128], P('sensor', 'tm'), may hold values from -6 to 6
Outputs:
- layer_out: bfloat16 [1024, 32, 128], P('sensor', 'tm')
- grad_inputs: bfloat16 [1024, 32, 128], P('sensor', 'tm')
- grad_projector: float32 [64, 128], P('tm')
- grad_key: float32 [128, 128], P('tm')
- grad_value: float32 [128, 128], P('tm')
- grad_query: float32 [128, 128], P('tm')
- grad_out: float32 [128, 128], P('tm')
All inputs are finite; a program needn't handle non-finite values. No bound on the sum of `mask` on one device may be relied on, other than what follows from the above.
Results may differ from a plain program's by a relative error of at most 0.0095.
Values sent between devices are 32-bit elements; how exact they have to be, the bound alone decides.
No kernel may reach another device: no remote copies, remote signals or barrier semaphores. Data moves between devices by JAX's collectives and lax.ppermute only.
A program may use at most 64 MiB of HBM per device.

v0:
```python
import jax
import jax.numpy as jnp
from jax import lax
from jax.sharding import PartitionSpec as P

sharpness_divisor = 12.0
epsilon = 1e-06
largest_energy = lax.Precision.HIGHEST


def normalize(vector):
    return vector * lax.rsqrt(jnp.mean(vector * vector, axis=-1, keepdims=True) + epsilon)


def attend_in(matched_plain_vector, values, projector):
    matched_unit_vector = normalize(matched_plain_vector)
    mapping_unit_vector = normalize(projector)
    attention_energies = (
        sharpness_divisor
        / matched_plain_vector.shape[-1]
        * jnp.dot(mapping_unit_vector, matched_unit_vector.T, precision=largest_energy)
    )
    weights = jnp.exp(attention_energies)
    numerator = jnp.dot(weights, values.astype(jnp.float32), precision=largest_energy)
    denominator = jnp.sum(weights, axis=1)
    return (numerator, denominator)


def make_summary(numerator, denominator):
    return numerator / denominator[..., None]


def attend_out(asking_plain_vector, summary):
    asking_unit_vector = normalize(asking_plain_vector)
    pooled_unit_vector = normalize(summary)
    attention_energies = (
        sharpness_divisor
        / asking_plain_vector.shape[-1]
        * jnp.dot(asking_unit_vector, pooled_unit_vector.T, precision=largest_energy)
    )
    weights = jnp.exp(attention_energies)
    weights = weights / jnp.sum(weights, axis=1, keepdims=True)
    blended = jnp.dot(weights, summary, precision=largest_energy)
    return normalize(blended).astype(jnp.bfloat16)


def contract_cells(left, right):
    return lax.dot_general(
        left, right, (((0, 1), (0, 1)), ((), ())), preferred_element_type=jnp.float32
    )


def back_project(left, weight):
    return lax.dot_general(
        left, weight, (((2,), (1,)), ((), ())), preferred_element_type=jnp.float32
    )


def per_device(inputs, mask, projector, w_key, w_value, w_query, w_out, cotangent):
    hidden = inputs * mask[..., None].astype(inputs.dtype)
    matched_plain_vector = jnp.dot(hidden, w_key, preferred_element_type=jnp.float32)
    values = jnp.dot(hidden, w_value, preferred_element_type=jnp.float32).astype(jnp.bfloat16)
    asking_plain_vector = jnp.dot(hidden, w_query, preferred_element_type=jnp.float32)
    batched_in = jax.vmap(attend_in, in_axes=(1, 1, None))
    (numerator, denominator), in_back = jax.vjp(batched_in, matched_plain_vector, values, projector)
    numerator, denominator = lax.psum((numerator, denominator), "sensor")
    summary, summary_back = jax.vjp(make_summary, numerator, denominator)
    batched_out = jax.vmap(attend_out, in_axes=(1, 0), out_axes=1)
    normed, out_back = jax.vjp(batched_out, asking_plain_vector, summary)
    output_rows = (
        hidden.astype(jnp.float32) + jnp.dot(normed, w_out, preferred_element_type=jnp.float32)
    ).astype(jnp.bfloat16)
    grad_out = contract_cells(normed, cotangent)
    d_normed = back_project(cotangent, w_out).astype(jnp.bfloat16)
    d_query, d_summary = out_back(d_normed)
    d_summary = lax.psum(d_summary, "sensor")
    d_numerator, d_denominator = summary_back(d_summary)
    d_key, d_values, d_projector = in_back((d_numerator, d_denominator))
    d_query = d_query.astype(jnp.bfloat16)
    d_key = d_key.astype(jnp.bfloat16)
    grad_key = contract_cells(hidden, d_key)
    grad_value = contract_cells(hidden, d_values)
    grad_query = contract_cells(hidden, d_query)
    d_hidden = cotangent.astype(jnp.float32)
    d_hidden = d_hidden + back_project(d_query, w_query)
    d_hidden = d_hidden + back_project(d_key, w_key)
    d_hidden = d_hidden + back_project(d_values, w_value)
    d_inputs = (d_hidden * mask[..., None].astype(jnp.float32)).astype(jnp.bfloat16)
    partials = (d_projector, grad_key, grad_value, grad_query, grad_out)
    summed = lax.psum((partials[0], partials[1], partials[2], partials[3], partials[4]), "sensor")
    owned_rows = (
        lax.psum_scatter(summed[0], "tm", scatter_dimension=0, tiled=True),
        lax.psum_scatter(summed[1], "tm", scatter_dimension=0, tiled=True),
        lax.psum_scatter(summed[2], "tm", scatter_dimension=0, tiled=True),
        lax.psum_scatter(summed[3], "tm", scatter_dimension=0, tiled=True),
        lax.psum_scatter(summed[4], "tm", scatter_dimension=0, tiled=True),
    )
    return (
        output_rows,
        d_inputs,
        owned_rows[0],
        owned_rows[1],
        owned_rows[2],
        owned_rows[3],
        owned_rows[4],
    )


def solution(mesh):
    placed = (
        P("sensor", "tm", None),
        P("sensor", "tm"),
        P(),
        P(),
        P(),
        P(),
        P(),
        P("sensor", "tm", None),
    )
    return jax.shard_map(
        per_device,
        mesh=mesh,
        in_specs=placed,
        out_specs=(
            P("sensor", "tm", None),
            P("sensor", "tm", None),
            P("tm", None),
            P("tm", None),
            P("tm", None),
            P("tm", None),
            P("tm", None),
        ),
        check_vma=False,
    )
```

profile of v0, /device:TPU:0, one launch (start us, length us, event | category | flops | bytes accessed | tf_op | source)
XLA Modules:
  0.0 422.1 jit_solution(13396379474754775781)
XLA Ops:
  7.2 0.8 fusion.69
  8.1 1.4 multiply_reduce_fusion.6
  9.6 0.6 copy-done.10
  10.5 0.6 copy-done.3
  11.2 0.5 copy-done.38
  12.4 0.7 fusion.25
  13.1 1.4 fusion.26
  14.6 44.2 %psum.57 = f32[16,64]{1,0:T(8,128)S(1)} all-reduce(f32[16,64]{1,0:T(8,128)S(1)} %bitcast.107), channel_id=1, replica_groups=mesh['sensor'=16,'tm'=2] {'sensor'}, use_global_device_ids=true, to_apply=%region_5.0 | all-reduce | flops 1024 | bytes 8192 | tf_op jit(solution)/shard_map/psum | solution.py:66
  58.8 0.4 multiply_reduce_fusion.7
  59.3 0.6 fusion.56
  59.9 0.6 multiply_divide_fusion
  60.9 1.0 bitcast_multiply_fusion.6
  61.9 63.8 %all-reduce.5.cloned.1.call-done = f32[16,64,128]{2,1,0:T(8,128)} async-done(((f32[16,64,128]{2,1,0:T(8,128)}), f32[16,64,128]{2,1,0:T(8,128)}) %all-reduce.5.cloned.1.call-update) | async-done | bytes 524304 | tf_op jit(solution)/shard_map/psum | solution.py:66
  125.7 1.5 multiply_reduce_fusion.5
  127.3 2.2 fusion.70
  129.5 1.4 multiply_reduce_fusion.3
  131.0 1.5 multiply_reduce_fusion.2
  132.5 1.0 multiply_reduce_fusion.1
  133.6 2.0 fusion.1
  135.6 0.6 copy-done.31
  136.3 2.5 fusion.22
  140.1 0.6 copy-done.12
  141.6 1.1 convolution_bitcast_fusion.2
  142.7 1.0 fusion.8
  144.2 0.9 convolution_bitcast_fusion.1
  145.1 97.9 %all-reduce.7.cloned.1.call-done = f32[16,64,128]{2,1,0:T(8,128)} async-done(((f32[16,64,128]{2,1,0:T(8,128)}), f32[16,64,128]{2,1,0:T(8,128)}) %all-reduce.7.cloned.1.call-update) | async-done | bytes 524304 | tf_op jit(solution)/shard_map/psum | solution.py:76
  243.0 1.5 multiply_reduce_fusion
  244.6 0.6 fusion.5
  245.2 1.2 multiply_reduce_fusion.8
  246.4 0.9 fusion.14
  247.4 0.6 copy-done.39
  248.0 0.7 add_add_fusion.5
  248.9 0.7 fusion.11
  249.8 1.1 convolution_bitcast_fusion.3
  251.3 1.1 convolution_bitcast_fusion.4
  252.5 0.7 copy-done.25
  253.4 8.9 %reduce-scatter.14.cloned.1.call-done = f32[64,128]{1,0:T(8,128)} async-done(((f32[128,128]{1,0:T(8,128)}), f32[64,128]{1,0:T(8,128)}) %reduce-scatter.14.cloned.1.call-update) | async-done | bytes 32784 | tf_op jit(solution)/shard_map/reduce_scatter | solution.py:96
  262.3 11.2 %reduce-scatter.6.cloned.1.call-done = f32[32,128]{1,0:T(8,128)} async-done(((f32[64,128]{1,0:T(8,128)}), f32[32,128]{1,0:T(8,128)}) %reduce-scatter.6.cloned.1.call-update) | async-done | bytes 16400 | tf_op jit(solution)/shard_map/reduce_scatter | solution.py:92
  273.6 10.7 %reduce-scatter.10.cloned.1.call-done = f32[64,128]{1,0:T(8,128)} async-done(((f32[128,128]{1,0:T(8,128)}), f32[64,128]{1,0:T(8,128)}) %reduce-scatter.10.cloned.1.call-update) | async-done | bytes 32784 | tf_op jit(solution)/shard_map/reduce_scatter | solution.py:94
  284.2 11.4 %reduce-scatter.8.cloned.1.call-done = f32[64,128]{1,0:T(8,128)} async-done(((f32[128,128]{1,0:T(8,128)}), f32[64,128]{1,0:T(8,128)}) %reduce-scatter.8.cloned.1.call-update) | async-done | bytes 32784 | tf_op jit(solution)/shard_map/reduce_scatter | solution.py:93
  295.7 0.7 copy-done.19
  296.4 1.0 fusion.7
  297.4 113.6 %all-reduce.9.cloned.1.call-done = (f32[32,128]{1,0:T(8,128)}, f32[64,128]{1,0:T(8,128)}, f32[64,128]{1,0:T(8,128)}, f32[64,128]{1,0:T(8,128)}, f32[64,128]{1,0:T(8,128)}) async-done(((f32[32,128]{1,0:T(8,128)}, f32[64,128]{1,0:T(8,128)}, f32[64,128]{1,0:T(8,128)}, f32[64,128]{1,0:T(8,128)}, f32[64,128]{1,0:T(8,128)}), (f32[32,128]{1,0:T(8,128)}, f32[64,128]{1,0:T(8,128)}, f32[64,128]{1,0:T(8,128)}, ...) | async-done | bytes 147472 | tf_op jit(solution)/shard_map/psum | solution.py:90
  411.0 1.3 copy.93
  412.3 0.6 copy.94
  413.1 0.6 copy.95
  413.8 0.6 copy.96
  414.6 0.6 copy.97
  (124 shorter events, 6.2 us)
Async XLA Ops:
  7.2 51.6 %copy-start = (bf16[128,128]{1,0:T(8,128)(2,1)S(1)}, bf16[128,128]{1,0:T(8,128)(2,1)}, u32[]{:S(2)}) copy-start(bf16[128,128]{1,0:T(8,128)(2,1)} %param.13) | copy-start | bytes 98308
  7.2 0.9 copy-start.24
  7.2 118.5 %all-reduce.5.cloned.1.call-start = ((), (), s32[]{:S(2)}) async-start(), calls=%async_computation.5 | async-start | bytes 1048576 | tf_op jit(solution)/shard_map/psum | solution.py:66
  8.1 50.7 %copy-start.26 = (bf16[64,16]{1,0:T(8,128)(2,1)}, bf16[64,16]{1,0:T(8,128)(2,1)S(1)}, u32[]{:S(2)}) copy-start(bf16[64,16]{1,0:T(8,128)(2,1)S(1)} %copy.15) | copy-start | bytes 6148
  10.3 0.8 copy-start.3
  10.4 1.4 copy-start.40
  11.1 0.8 copy-start.18
  12.2 0.9 copy-start.8
  14.5 228.5 %all-reduce.7.cloned.1.call-start = ((), (), s32[]{:S(2)}) async-start(), calls=%async_computation.6 | async-start | bytes 1048576 | tf_op jit(solution)/shard_map/psum | solution.py:76
  58.8 1.8 copy-start.2
  59.9 0.8 copy-start.16
  125.7 1.5 copy-start.1
  127.3 6.3 %copy-start.32 = (f32[16,64]{1,0:T(8,128)}, f32[16,64]{1,0:T(8,128)S(1)}, u32[]{:S(2)}) copy-start(f32[16,64]{1,0:T(8,128)S(1)} %fusion.60) | copy-start | bytes 12292
  129.5 4.1 copy-start.30
  129.5 4.1 copy-start.44
  130.9 2.7 copy-start.4
  130.9 1.6 copy-start.7
  132.5 1.1 copy-start.45
  132.5 1.0 copy-start.34
  135.6 0.7 copy-start.33
  135.6 0.7 copy-start.35
  135.6 117.8 %reduce-scatter.12.cloned.1.call-start = ((), (), s32[]{:S(2)}) async-start(), calls=%async_computation.10 | async-start | bytes 98304 | tf_op jit(solution)/shard_map/reduce_scatter | solution.py:95
  138.8 0.8 copy-start.14
  138.8 1.1 copy-start.5
  139.9 0.8 copy-start.12
  140.6 0.7 copy-start.27
  140.6 1.0 copy-start.41
  141.6 1.1 copy-start.17
  141.6 1.1 copy-start.28
  141.6 1.1 copy-start.42
  143.9 118.4 %reduce-scatter.14.cloned.1.call-start = ((), (), s32[]{:S(2)}) async-start(), calls=%async_computation.11 | async-start | bytes 98304 | tf_op jit(solution)/shard_map/reduce_scatter | solution.py:96
  145.1 97.9 %copy-start.15 = (f32[16,64]{1,0:T(8,128)S(1)}, f32[16,64]{1,0:T(8,128)}, u32[]{:S(2)}) copy-start(f32[16,64]{1,0:T(8,128)} %multiply_divide_fusion) | copy-start | bytes 12292
  145.1 99.5 %copy-start.9 = (bf16[64,16,128]{2,1,0:T(8,128)(2,1)S(1)}, bf16[64,16,128]{2,1,0:T(8,128)(2,1)}, u32[]{:S(2)}) copy-start(bf16[64,16,128]{2,1,0:T(8,128)(2,1)} %copy-done.8) | copy-start | bytes 786436
  145.1 128.5 %reduce-scatter.6.cloned.1.call-start = ((), (), s32[]{:S(2)}) async-start(), calls=%async_computation.7 | async-start | bytes 49152 | tf_op jit(solution)/shard_map/reduce_scatter | solution.py:92
  243.0 1.5 copy-start.6
  245.2 1.2 copy-start.37
  248.0 0.8 copy-start.11
  248.8 0.8 copy-start.29
  248.8 1.0 copy-start.43
  248.8 35.4 %reduce-scatter.10.cloned.1.call-start = ((), (), s32[]{:S(2)}) async-start(), calls=%async_computation.9 | async-start | bytes 98304 | tf_op jit(solution)/shard_map/reduce_scatter | solution.py:94
  250.9 44.7 %reduce-scatter.8.cloned.1.call-start = ((), (), s32[]{:S(2)}) async-start(), calls=%async_computation.8 | async-start | bytes 98304 | tf_op jit(solution)/shard_map/reduce_scatter | solution.py:93
  252.4 0.8 copy-start.25
  252.4 158.5 %all-reduce.9.cloned.1.call-start = ((), (), s32[]{:S(2)}) async-start(), calls=%async_computation.12 | async-start | bytes 294912 | tf_op jit(solution)/shard_map/psum | solution.py:90
  295.6 0.8 copy-start.19
  411.0 1.3 copy-start.23
  412.3 0.8 copy-start.22
  413.1 0.8 copy-start.21
  413.8 0.8 copy-start.20
  (6 other events, 3.6 us)
Sparse Core Ops, SparseCore 0:
  14.6 111.0 all-reduce.4
  135.7 107.2 all-reduce.6
  245.2 6.3 reduce-scatter.11
  253.7 8.6 reduce-scatter.13
  264.9 8.5 reduce-scatter.5
  275.6 8.5 reduce-scatter.9
  287.0 8.5 reduce-scatter.7
  301.7 109.1 all-reduce.8
where the time goes:
time: 423 us; the launch traced here: 422 us
  waiting for transfers between devices  318 us (75%)
  blocking collectives  44.2 us (10%)
  matrix products  25.2 us (6%)
  between operations  14.7 us (3%)
  local copies, waits for them, and re-layouts  11.4 us (3%)
  other arithmetic  8.5 us (2%)
    psum x1, waiting for transfers between devices, per_device(): lax.psum((partials[0], partials[1], partials[2], partials[3], partials[4]...  114 us
    psum x1, waiting for transfers between devices, per_device(): d_summary = lax.psum(d_summary, 'sensor')  97.9 us
    psum x1, waiting for transfers between devices, per_device(): numerator, denominator = lax.psum((numerator, denominator), 'sensor')  63.8 us
    psum x1, blocking collectives, per_device(): numerator, denominator = lax.psum((numerator, denominator), 'sensor')  44.2 us
    reduce_scatter x1, waiting for transfers between devices, per_device(): lax.psum_scatter(summed[1], 'tm', scatter_dimension=0, tiled=True)  11.4 us
    reduce_scatter x1, waiting for transfers between devices, per_device(): lax.psum_scatter(summed[0], 'tm', scatter_dimension=0, tiled=True)  11.2 us
    unnamed x97, local copies, waits for them, and re-layouts  11 us
    reduce_scatter x1, waiting for transfers between devices, per_device(): lax.psum_scatter(summed[2], 'tm', scatter_dimension=0, tiled=True)  10.7 us
  transfers between devices with their start and end apart: 8, of which 7 were waited for; matrix products, arithmetic and copies ran while one was open for 5% of the time, Pallas kernels for 0%

commit v1 on v0

v1 whole, which is shorter than its diff:
```python
import functools
import math

import jax
import jax.numpy as jnp
from jax import lax
from jax.experimental import pallas as pl
from jax.experimental.pallas import tpu as pltpu
from jax.sharding import PartitionSpec as P

sharpness_divisor = 12.0
epsilon = 1e-06
f32 = jnp.float32
bf16 = jnp.bfloat16


def params():
    return pltpu.CompilerParams(vmem_limit_bytes=48 * 1024 * 1024)


def dot(left, right, left_dim, right_dim):
    return lax.dot_general(
        left, right, (((left_dim,), (right_dim,)), ((), ())), preferred_element_type=f32
    )


def rounded_dot(left, right, left_dim, right_dim):
    return dot(left.astype(bf16), right.astype(bf16), left_dim, right_dim)


def inverse_norm(vector):
    return lax.rsqrt(jnp.mean(vector * vector, axis=-1, keepdims=True) + epsilon)


def normalize_back(inverse, unit, gradient):
    return inverse * (gradient - unit * jnp.mean(unit * gradient, axis=-1, keepdims=True))


def outward_kernel(rows_ref, mask_ref, out_ref, wide):
    wide[...] = rows_ref[...].astype(f32)
    marks = None if mask_ref is None else mask_ref[...].astype(f32)
    for t in range(out_ref.shape[0]):
        rows = wide[:, t, :]
        out_ref[t] = rows if marks is None else rows * marks[:, t : t + 1]


def outward(rows, mask):
    sensors, steps, width = rows.shape
    args = (rows,) if mask is None else (rows, mask)
    body = outward_kernel if mask is not None else (lambda r, o, w: outward_kernel(r, None, o, w))
    return pl.pallas_call(
        body,
        out_shape=jax.ShapeDtypeStruct((steps, sensors, width), f32),
        scratch_shapes=[pltpu.VMEM((sensors, steps, width), f32)],
        compiler_params=params(),
    )(*args)


def homeward_kernel(rows_ref, mask_ref, out_ref, wide):
    marks = None if mask_ref is None else mask_ref[...].astype(f32)
    for t in range(rows_ref.shape[0]):
        rows = rows_ref[t]
        wide[:, t, :] = rows if marks is None else rows * marks[:, t : t + 1]
    out_ref[...] = wide[...].astype(out_ref.dtype)


def homeward(rows, mask):
    steps, sensors, width = rows.shape
    args = (rows,) if mask is None else (rows, mask)
    body = homeward_kernel if mask is not None else (lambda r, o, w: homeward_kernel(r, None, o, w))
    return pl.pallas_call(
        body,
        out_shape=jax.ShapeDtypeStruct((sensors, steps, width), bf16),
        scratch_shapes=[pltpu.VMEM((sensors, steps, width), f32)],
        compiler_params=params(),
    )(*args)


def step_rows(ref, t):
    rows = ref[:, t]
    return rows.reshape(rows.shape[0] * rows.shape[1], rows.shape[2])


def project(ref, t, w_key, w_value, w_query):
    hidden = step_rows(ref, t).astype(bf16)
    width = w_key.shape[1]
    both = dot(hidden, jnp.concatenate([w_key, w_value, w_query], axis=1), 1, 0)
    return hidden, both[:, :width], both[:, width : 2 * width].astype(bf16), both[:, 2 * width :]


def scale_of(width):
    return sharpness_divisor / width


def weigh_in(key_raw, projector):
    inverse = inverse_norm(key_raw)
    unit = key_raw * inverse
    mapping = projector * inverse_norm(projector)
    scale = scale_of(key_raw.shape[-1])
    return inverse, unit, jnp.exp(scale * rounded_dot(mapping, unit, 1, 1))


def weigh_out(query_raw, summary):
    inverse = inverse_norm(query_raw)
    unit = query_raw * inverse
    pooled_inverse = inverse_norm(summary)
    pooled = summary * pooled_inverse
    scale = scale_of(query_raw.shape[-1])
    weights = jnp.exp(scale * rounded_dot(pooled, unit, 1, 1))
    attention = weights / jnp.sum(weights, axis=0, keepdims=True)
    return inverse, unit, pooled_inverse, pooled, attention


def in_part(refs, t, num_ref, den_ref):
    hidden, key_raw, values, _ = project(refs["hidden"], t, *refs["projections"])
    _, _, weights = weigh_in(key_raw, refs["projector"])
    num_ref[t] = rounded_dot(weights, values, 1, 0)
    den_ref[t] = jnp.broadcast_to(jnp.sum(weights, axis=1, keepdims=True), den_ref.shape[1:])


def out_part(refs, t, num, den, lay_ref, normed_ref):
    rows = step_rows(refs["hidden"], t)
    query_raw = dot(rows.astype(bf16), refs["projections"][2], 1, 0)
    summary = num / den
    _, _, _, _, attention = weigh_out(query_raw, summary)
    blended = rounded_dot(attention, summary, 0, 0)
    normed = (blended * inverse_norm(blended)).astype(bf16)
    layer = (rows + dot(normed, refs["w_out"], 1, 0)).astype(bf16).astype(f32)
    lay_ref[:, t] = layer.reshape(lay_ref.shape[0], *lay_ref.shape[2:])


def out_back_part(refs, t, num, den, ds_ref, dq_ref, go_ref):
    hidden = step_rows(refs["hidden"], t).astype(bf16)
    query_raw = dot(hidden, refs["projections"][2], 1, 0)
    cotangent = step_rows(refs["cotangent"], t).astype(bf16)
    summary = num / den
    inverse, unit, pooled_inverse, pooled, attention = weigh_out(query_raw, summary)
    scale = scale_of(query_raw.shape[-1])
    blended = rounded_dot(attention, summary, 0, 0)
    blended_inverse = inverse_norm(blended)
    normed = blended * blended_inverse
    go_ref[...] += dot(normed.astype(bf16), cotangent, 0, 0)
    d_normed = dot(cotangent, refs["w_out"], 1, 1).astype(bf16).astype(f32)
    d_blended = normalize_back(blended_inverse, normed, d_normed)
    d_attention = rounded_dot(summary, d_blended, 1, 1)
    d_scores = attention * (
        d_attention - jnp.sum(attention * d_attention, axis=0, keepdims=True)
    )
    d_unit = scale * rounded_dot(d_scores, pooled, 0, 0)
    d_pooled = scale * rounded_dot(d_scores, unit, 1, 0)
    ds_ref[t] = rounded_dot(attention, d_blended, 1, 0) + normalize_back(
        pooled_inverse, pooled, d_pooled
    )
    dq_ref[t] = normalize_back(inverse, unit, d_unit).astype(bf16)


def in_back_part(refs, t, num, den, d_summary, d_query, dh_ref, grads):
    hidden, key_raw, values, _ = project(refs["hidden"], t, *refs["projections"])
    cotangent = step_rows(refs["cotangent"], t)
    projector = refs["projector"]
    inverse, unit, weights = weigh_in(key_raw, projector)
    scale = scale_of(key_raw.shape[-1])
    d_num = d_summary / den
    d_den = -jnp.sum(d_summary * num, axis=1, keepdims=True) / (den * den)[:, :1]
    d_weights = rounded_dot(d_num, values, 1, 1) + d_den
    d_scores = d_weights * weights
    mapping_inverse = inverse_norm(projector)
    mapping = projector * mapping_inverse
    d_unit = scale * rounded_dot(d_scores, mapping, 0, 0)
    d_mapping = scale * rounded_dot(d_scores, unit, 1, 0)
    d_key = normalize_back(inverse, unit, d_unit).astype(bf16)
    d_values = rounded_dot(weights, d_num, 0, 0).astype(bf16)
    w_key, w_value, w_query = refs["projections"]
    together = jnp.concatenate([d_key, d_values, d_query], axis=1)
    turned = jnp.concatenate([w_key, w_value, w_query], axis=1)
    d_hidden = cotangent + dot(together, turned, 1, 1)
    dh_ref[:, t] = d_hidden.reshape(dh_ref.shape[0], *dh_ref.shape[2:])
    width = w_key.shape[1]
    gradients = dot(hidden, together, 0, 0)
    for i, grad in enumerate(grads[1:]):
        grad[...] += gradients[:, i * width : (i + 1) * width]
    grads[0][...] += normalize_back(mapping_inverse, mapping, d_mapping)


def read_refs(hidden, projector, wk, wv, wq, wo=None, cotangent=None):
    return {
        "hidden": hidden,
        "projector": projector[...],
        "projections": (wk[...], wv[...], wq[...]),
        "w_out": None if wo is None else wo[...],
        "cotangent": cotangent,
    }


def in_kernel(hidden, projector, wk, wv, wq, num_ref, den_ref):
    refs = read_refs(hidden, projector, wk, wv, wq)
    for t in range(hidden.shape[1]):
        in_part(refs, t, num_ref, den_ref)


def out_kernel(hidden, projector, wk, wv, wq, wo, num_ref, den_ref, lay_ref):
    refs = read_refs(hidden, projector, wk, wv, wq, wo)
    for t in range(hidden.shape[1]):
        out_part(refs, t, num_ref[t], den_ref[t], lay_ref, None)


def forward_kernel(hidden, projector, wk, wv, wq, wo, num_ref, den_ref, lay_ref):
    in_kernel(hidden, projector, wk, wv, wq, num_ref, den_ref)
    out_kernel(hidden, projector, wk, wv, wq, wo, num_ref, den_ref, lay_ref)


def out_back_kernel(hidden, projector, wk, wv, wq, wo, cot, num_ref, den_ref, ds_ref, dq_ref, go_ref):
    refs = read_refs(hidden, projector, wk, wv, wq, wo, cot)
    go_ref[...] = jnp.zeros_like(go_ref)
    for t in range(hidden.shape[1]):
        out_back_part(refs, t, num_ref[t], den_ref[t], ds_ref, dq_ref, go_ref)


def lay_partials(part_ref, grads):
    owners = part_ref.shape[0]
    for m in range(owners):
        at = 0
        for grad in grads:
            own = grad.shape[0] // owners
            part_ref[m, at : at + own, :] = grad[m * own : (m + 1) * own, :]
            at += own
        if at < part_ref.shape[1]:
            part_ref[m, at:, :] = jnp.zeros((part_ref.shape[1] - at, part_ref.shape[2]), f32)


def in_back_kernel(
    hidden, projector, wk, wv, wq, wo, cot, num_ref, den_ref, ds_ref, dq_ref, go_ref,
    dh_ref, part_ref, gp, gk, gv, gq,
):
    refs = read_refs(hidden, projector, wk, wv, wq, wo, cot)
    grads = (gp, gk, gv, gq)
    for grad in grads:
        grad[...] = jnp.zeros_like(grad)
    for t in range(hidden.shape[1]):
        in_back_part(refs, t, num_ref[t], den_ref[t], ds_ref[t], dq_ref[t], dh_ref, grads)
    lay_partials(part_ref, grads + (go_ref,))


def backward_kernel(
    hidden, projector, wk, wv, wq, wo, cot, num_ref, den_ref,
    dh_ref, part_ref, gp, gk, gv, gq, ds_ref, dq_ref, go_ref,
):
    out_back_kernel(
        hidden, projector, wk, wv, wq, wo, cot, num_ref, den_ref, ds_ref, dq_ref, go_ref
    )
    in_back_kernel(
        hidden, projector, wk, wv, wq, wo, cot, num_ref, den_ref, ds_ref, dq_ref, go_ref,
        dh_ref, part_ref, gp, gk, gv, gq,
    )


def fold_kernel(parts_ref, out_ref):
    total = parts_ref[0]
    for i in range(1, parts_ref.shape[0]):
        total = total + parts_ref[i]
    out_ref[...] = total


def fold(parts):
    return pl.pallas_call(
        fold_kernel,
        out_shape=jax.ShapeDtypeStruct(parts.shape[1:], f32),
        compiler_params=params(),
    )(parts)


def deal_kernel(rows_ref, *out_refs):
    at = 0
    for out in out_refs:
        out[...] = rows_ref[at : at + out.shape[0], :]
        at += out.shape[0]


def per_device(n_sensor, n_tm, inputs, mask, projector, w_key, w_value, w_query, w_out, cotangent):
    sensors, steps, width = inputs.shape
    tokens = projector.shape[0]
    group = math.gcd(n_sensor, steps)
    rest = n_sensor // group
    share = steps // group
    if rest == 1:
        swap = functools.partial(
            lax.all_to_all, axis_name="sensor", split_axis=0, concat_axis=0, tiled=True
        )
    else:
        blocks = [list(range(r * group, (r + 1) * group)) for r in range(rest)]
        swap = functools.partial(
            lax.all_to_all, axis_name="sensor", split_axis=0, concat_axis=0, tiled=True,
            axis_index_groups=blocks,
        )
        across = [list(range(i, n_sensor, group)) for i in range(group)]
    timed = (group, share, sensors, width)
    hidden = swap(outward(inputs, mask)).reshape(timed)
    cot = swap(outward(cotangent, None)).reshape(timed)
    weights = (projector, w_key, w_value, w_query)
    small = jax.ShapeDtypeStruct((share, tokens, width), f32)
    large = jax.ShapeDtypeStruct(timed, f32)
    square = jax.ShapeDtypeStruct((width, width), f32)
    query_shape = jax.ShapeDtypeStruct((share, group * sensors, width), bf16)
    owned = [tokens // n_tm] + [width // n_tm] * 4
    chunk = -(-sum(owned) // n_sensor)
    part_shape = jax.ShapeDtypeStruct((n_tm, chunk * n_sensor, width), f32)
    grad_scratch = [pltpu.VMEM((tokens, width), f32)] + [pltpu.VMEM((width, width), f32)] * 3
    if rest == 1:
        num, den, layer = pl.pallas_call(
            forward_kernel, out_shape=(small, small, large), compiler_params=params()
        )(hidden, *weights, w_out)
    else:
        num, den = pl.pallas_call(in_kernel, out_shape=(small, small), compiler_params=params())(
            hidden, *weights
        )
        num, den = lax.psum((num, den), "sensor", axis_index_groups=across)
        layer = pl.pallas_call(out_kernel, out_shape=large, compiler_params=params())(
            hidden, *weights, w_out, num, den
        )
    layer_home = swap(layer.reshape(steps, sensors, width))
    if rest == 1:
        d_hidden, part = pl.pallas_call(
            backward_kernel,
            out_shape=(large, part_shape),
            scratch_shapes=grad_scratch
            + [
                pltpu.VMEM(small.shape, f32),
                pltpu.VMEM(query_shape.shape, bf16),
                pltpu.VMEM((width, width), f32),
            ],
            compiler_params=params(),
        )(hidden, *weights, w_out, cot, num, den)
    else:
        d_summary, d_query, grad_out = pl.pallas_call(
            out_back_kernel, out_shape=(small, query_shape, square), compiler_params=params()
        )(hidden, *weights, w_out, cot, num, den)
        d_summary = lax.psum(d_summary, "sensor", axis_index_groups=across)
        d_hidden, part = pl.pallas_call(
            in_back_kernel,
            out_shape=(large, part_shape),
            scratch_shapes=grad_scratch,
            compiler_params=params(),
        )(hidden, *weights, w_out, cot, num, den, d_summary, d_query, grad_out)
    me = lax.axis_index("tm")
    terms = [lax.dynamic_index_in_dim(part, me, 0, keepdims=False)]
    for step in range(1, n_tm):
        gone = lax.dynamic_index_in_dim(part, lax.rem(me + step, n_tm), 0, keepdims=False)
        ring = [(i, (i + step) % n_tm) for i in range(n_tm)]
        terms.append(lax.ppermute(gone, "tm", ring))
    mine = sum(terms[1:], terms[0]).reshape(n_sensor, chunk, width)
    whole_swap = functools.partial(
        lax.all_to_all, axis_name="sensor", split_axis=0, concat_axis=0, tiled=True
    )
    total = fold(whole_swap(mine))
    gathered = whole_swap(jnp.broadcast_to(total[None], (n_sensor, chunk, width)))
    d_home = swap(d_hidden.reshape(steps, sensors, width))
    output_rows = homeward(layer_home, None)
    d_inputs = homeward(d_home, mask)
    outs = pl.pallas_call(
        deal_kernel,
        out_shape=tuple(jax.ShapeDtypeStruct((n, width), f32) for n in owned),
        compiler_params=params(),
    )(gathered.reshape(n_sensor * chunk, width))
    return (output_rows, d_inputs, *outs)


def solution(mesh):
    placed = (
        P("sensor", "tm", None),
        P("sensor", "tm"),
        P(),
        P(),
        P(),
        P(),
        P(),
        P("sensor", "tm", None),
    )
    return jax.shard_map(
        functools.partial(per_device, mesh.shape["sensor"], mesh.shape["tm"]),
        mesh=mesh,
        in_specs=placed,
        out_specs=(
            P("sensor", "tm", None),
            P("sensor", "tm", None),
            P("tm", None),
            P("tm", None),
            P("tm", None),
            P("tm", None),
            P("tm", None),
        ),
        check_vma=False,
    )
```

time: 423 us -> 113 us (0.27)
  waiting for transfers between devices: 318 us -> 40.8 us
  matrix products: 25.2 us -> 0 us
  starting transfers between devices: 0.51 us -> 16.4 us
  between operations: 14.7 us -> 0.78 us
  Pallas kernels: 0 us -> 10.4 us
  local copies, waits for them, and re-layouts: 11.4 us -> 1.81 us
  other arithmetic: 8.5 us -> 0.02 us
    psum x3 -> x0, waiting for transfers between devices: 275 us -> none  [the longest x1 114 us: per_device(): lax.psum((partials[0], partials[1], partials[2], partials[3], partials[4]...]
    psum x1 -> x0, blocking collectives: 44.2 us -> none  [per_device(): numerator, denominator = lax.psum((numerator, denominator), 'sensor')]
    reduce_scatter x5 -> x0, waiting for transfers between devices: 42.2 us -> none  [the longest x1 11.4 us: per_device(): lax.psum_scatter(summed[1], 'tm', scatter_dimension=0, tiled=True)]
    all_to_all x0 -> x3, blocking collectives: none -> 41.8 us  [the longest x1 17.9 us: per_device(): layer_home = swap(layer.reshape(steps, sensors, width))]
    all_to_all x0 -> x3, waiting for transfers between devices: none -> 39.5 us  [the longest x1 14 us: per_device(): hidden = swap(outward(inputs, mask)).reshape(timed)]
    dot_general x23 -> x0, matrix products: 24.5 us -> none  [the longest x3 5.75 us: attend_out(): jnp.dot(asking_unit_vector, pooled_unit_vector.T, precision=largest_energy)]
    all_to_all x0 -> x3, starting transfers between devices: none -> 16.4 us  [the longest x1 8.44 us: per_device(): hidden = swap(outward(inputs, mask)).reshape(timed)]
    pallas_call x0 -> x8, Pallas kernels: none -> 10.4 us  [the longest x1 3.7 us: per_device(): pl.pallas_call(backward_kernel, out_shape=(large, part_shape), scratch_sh...]
  transfers between devices with their start and end apart: 8 -> 4, of which waited for: 7 -> 4; matrix products, arithmetic and copies ran while one was open for 5% -> 0% of each run, Pallas kernels for 0% -> 4%
where the time goes in v1:
time: 113 us; the launch traced here: 112 us
  blocking collectives  41.8 us (37%)
  waiting for transfers between devices  40.8 us (36%)
  starting transfers between devices  16.4 us (15%)
  Pallas kernels  10.4 us (9%)
  local copies, waits for them, and re-layouts  1.81 us (2%)
    all_to_all x1, blocking collectives, per_device(): layer_home = swap(layer.reshape(steps, sensors, width))  17.9 us
    all_to_all x1, waiting for transfers between devices, per_device(): hidden = swap(outward(inputs, mask)).reshape(timed)  14 us
    all_to_all x1, waiting for transfers between devices, per_device(): cot = swap(outward(cotangent, None)).reshape(timed)  12.8 us
    all_to_all x1, waiting for transfers between devices, per_device(): d_home = swap(d_hidden.reshape(steps, sensors, width))  12.7 us
    all_to_all x1, blocking collectives, per_device(): total = fold(whole_swap(mine))  12.6 us
    all_to_all x1, blocking collectives, per_device(): whole_swap(jnp.broadcast_to(total[None], (n_sensor, chunk, width)))  11.3 us
    all_to_all x1, starting transfers between devices, per_device(): hidden = swap(outward(inputs, mask)).reshape(timed)  8.44 us
    all_to_all x1, starting transfers between devices, per_device(): cot = swap(outward(cotangent, None)).reshape(timed)  4.04 us
  transfers between devices with their start and end apart: 4, of which 4 were waited for; matrix products, arithmetic and copies ran while one was open for 0% of the time, Pallas kernels for 4%

profile of v1, /device:TPU:0, one launch (start us, length us, event | category | flops | bytes accessed | tf_op | source)
XLA Modules:
  0.0 112.0 jit_solution(17426907270206072888)
XLA Ops:
  0.6 0.8 copy.17.mask_ref
  1.4 0.0 copy-start
  1.4 0.9 copy-done
  2.4 1.1 shard_map.135
  3.5 0.0 copy-start.1
  3.5 8.4 %all-to-all-start = ((f32[16,64,128]{2,1,0:T(8,128)}), f32[16,64,128]{2,1,0:T(8,128)S(1)}, u32[]{:S(2)}, u32[]{:S(2)}) async-start(f32[16,64,128]{2,1,0:T(8,128)} %shard_map.135), calls=%async_computation | async-start | bytes 1048576 | tf_op jit(solution)/shard_map/all_to_all | solution.py:297
  11.9 0.0 copy-done.1
  11.9 1.1 shard_map.138
  13.0 14.0 %all-to-all-done = f32[16,64,128]{2,1,0:T(8,128)S(1)} async-done(((f32[16,64,128]{2,1,0:T(8,128)}), f32[16,64,128]{2,1,0:T(8,128)S(1)}, u32[]{:S(2)}, u32[]{:S(2)}) %all-to-all-start) | async-done | bytes 524320 | tf_op jit(solution)/shard_map/all_to_all | solution.py:297
  27.1 0.0 copy-start.2
  27.1 0.0 copy-start.3
  27.1 0.0 copy-start.4
  27.1 0.0 copy-start.5
  27.1 0.0 copy-start.6
  27.1 4.0 %all-to-all-start.2 = ((f32[16,64,128]{2,1,0:T(8,128)}), f32[16,64,128]{2,1,0:T(8,128)S(1)}, u32[]{:S(2)}, u32[]{:S(2)}) async-start(f32[16,64,128]{2,1,0:T(8,128)} %shard_map.138), calls=%async_computation.2 | async-start | bytes 1048576 | tf_op jit(solution)/shard_map/all_to_all | solution.py:298
  31.1 0.0 copy-done.2
  31.2 0.0 copy-done.3
  31.2 0.0 copy-done.4
  31.2 0.0 copy-done.5
  31.2 0.0 copy-done.6
  31.2 1.6 %shard_map.136 = (f32[1,64,128]{2,1,0:T(8,128)S(1)}, f32[1,64,128]{2,1,0:T(8,128)S(1)}, f32[16,1,64,128]{3,2,1,0:T(8,128)S(1)}) custom-call(f32[16,1,64,128]{3,2,1,0:T(8,128)S(1)} %bitcast.8, f32[64,128]{1,0:T(8,128)S(1)} %copy-done.2, bf16[128,128]{1,0:T(8,128)(2,1)S(1)} %copy-done.3, bf16[128,128]{1,0:T(8,128)(2,1)S(1)} %copy-done.4, ...), custom_call_target="tpu_custom_call" | custom-call | tf_op jit(solution)/shard_map/pallas_call | solution.py:309
  32.8 12.8 %all-to-all-done.2 = f32[16,64,128]{2,1,0:T(8,128)S(1)} async-done(((f32[16,64,128]{2,1,0:T(8,128)}), f32[16,64,128]{2,1,0:T(8,128)S(1)}, u32[]{:S(2)}, u32[]{:S(2)}) %all-to-all-start.2) | async-done | bytes 524320 | tf_op jit(solution)/shard_map/all_to_all | solution.py:298
  45.6 3.7 %shard_map.139 = (f32[16,1,64,128]{3,2,1,0:T(8,128)}, f32[2,288,128]{2,1,0:T(8,128)S(1)}) custom-call(f32[16,1,64,128]{3,2,1,0:T(8,128)S(1)} %bitcast.9, f32[64,128]{1,0:T(8,128)S(1)} %copy-done.2, bf16[128,128]{1,0:T(8,128)(2,1)S(1)} %copy-done.3, bf16[128,128]{1,0:T(8,128)(2,1)S(1)} %copy-done.4, bf16[128,128]{1,0:T(8,128)(2,1)S(1)} %copy-done.5, ...), custom_call_target="tpu_custom_call" | custom-call | tf_op jit(solution)/shard_map/pallas_call | solution.py:322
  49.3 0.1 collective-permute-start
  49.4 1.4 %collective-permute-done = f32[288,128]{1,0:T(8,128)S(1)} collective-permute-done((f32[288,128]{1,0:T(8,128)S(1)}, f32[288,128]{1,0:T(8,128)S(1)}, u32[]{:S(2)}, u32[]{:S(2)}) %collective-permute-start) | collective-permute-done | bytes 147488 | tf_op jit(solution)/shard_map/ppermute | solution.py:349
  50.8 12.6 %all_to_all.30.parts_ref = f32[16,18,128]{2,1,0:T(8,128)S(1)} all-to-all(f32[16,18,128]{2,1,0:T(8,128)S(1)} %reshape.37), channel_id=1, replica_groups=mesh['sensor'=16,'tm'=2] {'sensor'}, dimensions={0} | all-to-all | bytes 294912 | tf_op jit(solution)/shard_map/all_to_all | solution.py:354
  63.4 11.3 %all_to_all.31 = f32[16,18,128]{2,1,0:T(8,128)S(1)} all-to-all(f32[16,18,128]{2,1,0:T(8,128)S(1)} %broadcast_in_dim.2), channel_id=1, replica_groups=mesh['sensor'=16,'tm'=2] {'sensor'}, dimensions={0} | all-to-all | bytes 294912 | tf_op jit(solution)/shard_map/all_to_all | solution.py:355
  74.7 17.9 %all_to_all.32.r = f32[16,64,128]{2,1,0:T(8,128)S(1)} all-to-all(f32[16,64,128]{2,1,0:T(8,128)S(1)} %bitcast.11), channel_id=1, replica_groups=mesh['sensor'=16,'tm'=2] {'sensor'}, dimensions={0} | all-to-all | bytes 1048576 | tf_op jit(solution)/shard_map/all_to_all | solution.py:320
  92.6 3.9 %all-to-all-start.3 = ((f32[16,64,128]{2,1,0:T(8,128)}), f32[16,64,128]{2,1,0:T(8,128)S(1)}, u32[]{:S(2)}, u32[]{:S(2)}) async-start(f32[16,64,128]{2,1,0:T(8,128)} %bitcast.3), calls=%async_computation.3 | async-start | bytes 1048576 | tf_op jit(solution)/shard_map/all_to_all | solution.py:356
  96.5 0.7 shard_map.142
  97.1 1.1 shard_map.137
  98.2 12.7 %all-to-all-done.3.rows_ref = f32[16,64,128]{2,1,0:T(8,128)S(1)} async-done(((f32[16,64,128]{2,1,0:T(8,128)}), f32[16,64,128]{2,1,0:T(8,128)S(1)}, u32[]{:S(2)}, u32[]{:S(2)}) %all-to-all-start.3) | async-done | bytes 524320 | tf_op jit(solution)/shard_map/all_to_all | solution.py:356
  110.8 1.1 %shard_map.140 = bf16[64,16,128]{2,1,0:T(8,128)(2,1)} custom-call(f32[16,64,128]{2,1,0:T(8,128)S(1)} %all-to-all-done.3.rows_ref, s32[64,16]{1,0:T(8,128)S(1)} %copy.17.mask_ref), custom_call_target="tpu_custom_call" | custom-call | tf_op jit(solution)/shard_map/pallas_call | solution.py:71
  (6 shorter events, 0.1 us)
Async XLA Ops:
  1.4 1.0 copy-start
  3.5 8.5 %copy-start.1 = (bf16[64,16,128]{2,1,0:T(8,128)(2,1)S(1)}, bf16[64,16,128]{2,1,0:T(8,128)(2,1)}, u32[]{:S(2)}) copy-start(bf16[64,16,128]{2,1,0:T(8,128)(2,1)} %r.1) | copy-start | bytes 786436
  3.5 23.6 %all-to-all-start = ((f32[16,64,128]{2,1,0:T(8,128)}), f32[16,64,128]{2,1,0:T(8,128)S(1)}, u32[]{:S(2)}, u32[]{:S(2)}) async-start(f32[16,64,128]{2,1,0:T(8,128)} %shard_map.135), calls=%async_computation | async-start | bytes 1048576 | tf_op jit(solution)/shard_map/all_to_all | solution.py:297
  27.1 4.1 %copy-start.2 = (f32[64,128]{1,0:T(8,128)S(1)}, f32[64,128]{1,0:T(8,128)}, u32[]{:S(2)}) copy-start(f32[64,128]{1,0:T(8,128)} %projector.3) | copy-start | bytes 98308
  27.1 4.1 %copy-start.3 = (bf16[128,128]{1,0:T(8,128)(2,1)S(1)}, bf16[128,128]{1,0:T(8,128)(2,1)}, u32[]{:S(2)}) copy-start(bf16[128,128]{1,0:T(8,128)(2,1)} %wk.3) | copy-start | bytes 98308
  27.1 4.1 %copy-start.4 = (bf16[128,128]{1,0:T(8,128)(2,1)S(1)}, bf16[128,128]{1,0:T(8,128)(2,1)}, u32[]{:S(2)}) copy-start(bf16[128,128]{1,0:T(8,128)(2,1)} %wv.3) | copy-start | bytes 98308
  27.1 4.1 %copy-start.5 = (bf16[128,128]{1,0:T(8,128)(2,1)S(1)}, bf16[128,128]{1,0:T(8,128)(2,1)}, u32[]{:S(2)}) copy-start(bf16[128,128]{1,0:T(8,128)(2,1)} %wq.3) | copy-start | bytes 98308
  27.1 4.1 %copy-start.6 = (bf16[128,128]{1,0:T(8,128)(2,1)S(1)}, bf16[128,128]{1,0:T(8,128)(2,1)}, u32[]{:S(2)}) copy-start(bf16[128,128]{1,0:T(8,128)(2,1)} %wo.3) | copy-start | bytes 98308
  27.1 18.5 %all-to-all-start.2 = ((f32[16,64,128]{2,1,0:T(8,128)}), f32[16,64,128]{2,1,0:T(8,128)S(1)}, u32[]{:S(2)}, u32[]{:S(2)}) async-start(f32[16,64,128]{2,1,0:T(8,128)} %shard_map.138), calls=%async_computation.2 | async-start | bytes 1048576 | tf_op jit(solution)/shard_map/all_to_all | solution.py:298
  49.3 1.4 %collective-permute-start = (f32[288,128]{1,0:T(8,128)S(1)}, f32[288,128]{1,0:T(8,128)S(1)}, u32[]{:S(2)}, u32[]{:S(2)}) collective-permute-start(f32[288,128]{1,0:T(8,128)S(1)} %dynamic-slice_bitcast_fusion), channel_id=1, source_target_pairs={{0,1},{1,0},{2,3},{3,2},{4,5},{5,4},{6,7},{7,6},{8,9},{9,8},{10,11... | collective-permute-start | bytes 442376 | tf_op jit(solution)/shard_map/ppermute | solution.py:349
  92.6 18.3 %all-to-all-start.3 = ((f32[16,64,128]{2,1,0:T(8,128)}), f32[16,64,128]{2,1,0:T(8,128)S(1)}, u32[]{:S(2)}, u32[]{:S(2)}) async-start(f32[16,64,128]{2,1,0:T(8,128)} %bitcast.3), calls=%async_computation.3 | async-start | bytes 1048576 | tf_op jit(solution)/shard_map/all_to_all | solution.py:356

commit v2 on v0

v2 whole, which is shorter than its diff:
```python
import functools
import math

import jax
import jax.numpy as jnp
from jax import lax
from jax.experimental import pallas as pl
from jax.experimental.pallas import tpu as pltpu
from jax.sharding import PartitionSpec as P

sharpness_divisor = 12.0
epsilon = 1e-06
f32 = jnp.float32
bf16 = jnp.bfloat16


def params():
    return pltpu.CompilerParams(vmem_limit_bytes=48 * 1024 * 1024)


def dot(left, right, left_dim, right_dim):
    return lax.dot_general(
        left, right, (((left_dim,), (right_dim,)), ((), ())), preferred_element_type=f32
    )


def rounded_dot(left, right, left_dim, right_dim):
    return dot(left.astype(bf16), right.astype(bf16), left_dim, right_dim)


def inverse_norm(vector):
    return lax.rsqrt(jnp.mean(vector * vector, axis=-1, keepdims=True) + epsilon)


def normalize_back(inverse, unit, gradient):
    return inverse * (gradient - unit * jnp.mean(unit * gradient, axis=-1, keepdims=True))


def outward_kernel(inputs_ref, mask_ref, cotangent_ref, out_ref, wide, wide_cotangent):
    sensors, steps, _ = inputs_ref.shape
    share = steps // out_ref.shape[0]
    wide[...] = inputs_ref[...].astype(f32)
    wide_cotangent[...] = cotangent_ref[...].astype(f32)
    marks = mask_ref[...].astype(f32)
    for t in range(steps):
        place, own = divmod(t, share)
        out_ref[place, own * sensors : (own + 1) * sensors, :] = (
            wide[:, t, :] * marks[:, t : t + 1]
        )
        at = (share + own) * sensors
        out_ref[place, at : at + sensors, :] = wide_cotangent[:, t, :]


def homeward_kernel(rows_ref, mask_ref, layer_ref, d_inputs_ref, wide, wide_gradient):
    sensors, steps, _ = layer_ref.shape
    share = steps // rows_ref.shape[0]
    marks = mask_ref[...].astype(f32)
    for t in range(steps):
        place, own = divmod(t, share)
        wide[:, t, :] = rows_ref[place, own * sensors : (own + 1) * sensors, :]
        at = (share + own) * sensors
        wide_gradient[:, t, :] = rows_ref[place, at : at + sensors, :] * marks[:, t : t + 1]
    layer_ref[...] = wide[...].astype(bf16)
    d_inputs_ref[...] = wide_gradient[...].astype(bf16)


def rows_of(ref, block, sensors):
    rows = ref[:, block * sensors : (block + 1) * sensors, :]
    return rows.reshape(rows.shape[0] * sensors, rows.shape[2])


def put_rows(ref, block, sensors, rows):
    ref[:, block * sensors : (block + 1) * sensors, :] = rows.reshape(
        ref.shape[0], sensors, rows.shape[1]
    )


def scale_of(width):
    return sharpness_divisor / width


def weigh_in(key_raw, projector):
    inverse = inverse_norm(key_raw)
    unit = key_raw * inverse
    mapping = projector * inverse_norm(projector)
    scale = scale_of(key_raw.shape[-1])
    return inverse, unit, jnp.exp(scale * rounded_dot(mapping, unit, 1, 1))


def diagonal(tokens):
    rows = lax.broadcasted_iota(jnp.int32, (tokens, tokens), 0)
    return rows == lax.broadcasted_iota(jnp.int32, (tokens, tokens), 1)


def in_kernel(share, sensors, swapped, projector, wk, wv, sums_ref):
    tokens, width = projector.shape
    same = diagonal(tokens)
    tail = share * tokens
    sums_ref[tail:, :] = jnp.zeros((sums_ref.shape[0] - tail, width), f32)
    both_weights = jnp.concatenate([wk[...], wv[...]], axis=1)
    for t in range(share):
        hidden = rows_of(swapped, t, sensors).astype(bf16)
        both = dot(hidden, both_weights, 1, 0)
        _, _, weights = weigh_in(both[:, :width], projector[...])
        sums_ref[t * tokens : (t + 1) * tokens, :] = rounded_dot(weights, both[:, width:], 1, 0)
        den = jnp.sum(weights, axis=1, keepdims=True)
        sums_ref[tail + t : tail + t + 1, :tokens] = jnp.sum(
            jnp.where(same, den, 0.0), axis=0, keepdims=True
        )


def total_of(refs):
    total = refs[0][...]
    for ref in refs[1:]:
        total = total + ref[...]
    return total


def num_den(total, t, share, tokens):
    num = total[t * tokens : (t + 1) * tokens, :]
    at = share * tokens + t
    den = jnp.sum(
        jnp.where(diagonal(tokens), total[at : at + 1, :tokens], 0.0), axis=1, keepdims=True
    )
    return num, den


def out_kernel(share, sensors, terms, swapped, wq, wo, *refs):
    sums = refs[:terms]
    lay_ref, ds_ref, dq_ref, go_ref = refs[terms:]
    width = wq.shape[0]
    tokens = ds_ref.shape[0] // share
    scale = scale_of(width)
    total = total_of(sums)
    w_out = wo[...]
    for t in range(share):
        rows = rows_of(swapped, t, sensors)
        query_raw = dot(rows.astype(bf16), wq[...], 1, 0)
        cotangent = rows_of(swapped, share + t, sensors).astype(bf16)
        num, den = num_den(total, t, share, tokens)
        summary = num / den
        inverse = inverse_norm(query_raw)
        unit = query_raw * inverse
        pooled_inverse = inverse_norm(summary)
        pooled = summary * pooled_inverse
        weights = jnp.exp(scale * rounded_dot(pooled, unit, 1, 1))
        attention = weights / jnp.sum(weights, axis=0, keepdims=True)
        blended = rounded_dot(attention, summary, 0, 0)
        blended_inverse = inverse_norm(blended)
        normed = blended * blended_inverse
        rounded = normed.astype(bf16)
        layer = (rows + dot(rounded, w_out, 1, 0)).astype(bf16).astype(f32)
        put_rows(lay_ref, t, sensors, layer)
        grad_out = dot(rounded, cotangent, 0, 0)
        go_ref[...] = grad_out if t == 0 else go_ref[...] + grad_out
        d_normed = dot(cotangent, w_out, 1, 1).astype(bf16).astype(f32)
        d_blended = normalize_back(blended_inverse, normed, d_normed)
        d_attention = rounded_dot(summary, d_blended, 1, 1)
        d_scores = attention * (
            d_attention - jnp.sum(attention * d_attention, axis=0, keepdims=True)
        )
        d_unit = scale * rounded_dot(d_scores, pooled, 0, 0)
        d_pooled = scale * rounded_dot(d_scores, unit, 1, 0)
        ds_ref[t * tokens : (t + 1) * tokens, :] = rounded_dot(
            attention, d_blended, 1, 0
        ) + normalize_back(pooled_inverse, pooled, d_pooled)
        d_query = normalize_back(inverse, unit, d_unit).astype(bf16)
        dq_ref[t * d_query.shape[0] : (t + 1) * d_query.shape[0], :] = d_query


def put_partials(ref, base, owners, chunk, grads):
    for m in range(owners):
        at = 0
        for grad in grads:
            own = grad.shape[0] // owners
            done = 0
            while done < own:
                place, row = divmod(at, chunk)
                count = min(own - done, chunk - row)
                begin = base + m * chunk + row
                start = m * own + done
                ref[place, begin : begin + count, :] = grad[start : start + count, :]
                done += count
                at += count
        while at < ref.shape[0] * chunk:
            place, row = divmod(at, chunk)
            begin = base + m * chunk + row
            ref[place, begin : begin + chunk - row, :] = jnp.zeros((chunk - row, ref.shape[2]), f32)
            at += chunk - row


def in_back_kernel(share, sensors, terms, owners, chunk, swapped, projector, wk, wv, wq, lay_ref, dq_ref, go_ref, *refs):
    sums, d_sums = refs[:terms], refs[terms : 2 * terms]
    out_ref = refs[2 * terms]
    tokens, width = projector.shape
    scale = scale_of(width)
    total = total_of(sums)
    d_total = total_of(d_sums)
    mapping_inverse = inverse_norm(projector[...])
    mapping = projector[...] * mapping_inverse
    w_key, w_value, w_query = wk[...], wv[...], wq[...]
    both_weights = jnp.concatenate([w_key, w_value], axis=1)
    turned = jnp.concatenate([w_key, w_value, w_query], axis=1)
    out_ref[:, : share * sensors, :] = lay_ref[...]
    gradients = None
    for t in range(share):
        hidden = rows_of(swapped, t, sensors).astype(bf16)
        both = dot(hidden, both_weights, 1, 0)
        values = both[:, width:].astype(bf16)
        cotangent = rows_of(swapped, share + t, sensors)
        inverse, unit, weights = weigh_in(both[:, :width], projector[...])
        num, den = num_den(total, t, share, tokens)
        d_summary = d_total[t * tokens : (t + 1) * tokens, :]
        d_num = d_summary / den
        d_den = -jnp.sum(d_summary * num, axis=1, keepdims=True) / (den * den)
        d_scores = (rounded_dot(d_num, values, 1, 1) + d_den) * weights
        d_unit = scale * rounded_dot(d_scores, mapping, 0, 0)
        d_mapping = scale * rounded_dot(d_scores, unit, 1, 0)
        d_key = normalize_back(inverse, unit, d_unit).astype(bf16)
        d_values = rounded_dot(weights, d_num, 0, 0).astype(bf16)
        d_query = dq_ref[t * hidden.shape[0] : (t + 1) * hidden.shape[0], :]
        together = jnp.concatenate([d_key, d_values, d_query], axis=1)
        put_rows(out_ref, share + t, sensors, cotangent + dot(together, turned, 1, 1))
        more = (normalize_back(mapping_inverse, mapping, d_mapping), dot(hidden, together, 0, 0))
        gradients = more if t == 0 else tuple(a + b for a, b in zip(gradients, more))
    parts = [gradients[0]] + [gradients[1][:, i * width : (i + 1) * width] for i in range(3)]
    put_partials(out_ref, 2 * share * sensors, owners, chunk, parts + [go_ref[...]])


def fold_kernel(base, parts_ref, out_ref):
    total = parts_ref[0, base:, :]
    for i in range(1, parts_ref.shape[0]):
        total = total + parts_ref[i, base:, :]
    out_ref[...] = total.reshape(out_ref.shape)


def deal_kernel(rows_ref, *out_refs):
    at = 0
    for out in out_refs:
        out[...] = rows_ref[at : at + out.shape[0], :]
        at += out.shape[0]


def call(kernel, out_shape, *args, **more):
    return pl.pallas_call(kernel, out_shape=out_shape, compiler_params=params(), **more)(*args)


def group_size(n_sensor, steps):
    group = math.gcd(n_sensor, steps)
    return group // 2 if group % 2 == 0 and group > 8 else group


def per_device(n_sensor, n_tm, inputs, mask, projector, w_key, w_value, w_query, w_out, cotangent):
    sensors, steps, width = inputs.shape
    tokens = projector.shape[0]
    group = group_size(n_sensor, steps)
    rest = n_sensor // group
    share = steps // group
    blocks = [list(range(r * group, (r + 1) * group)) for r in range(rest)]

    def swap(rows):
        return lax.all_to_all(rows, "sensor", 0, 0, tiled=True, axis_index_groups=blocks)

    def others(rows):
        return [
            lax.ppermute(
                rows, "sensor", [(i, (i + step * group) % n_sensor) for i in range(n_sensor)]
            )
            for step in range(1, rest)
        ]

    def shape(*dims, kind=f32):
        return jax.ShapeDtypeStruct(dims, kind)

    wide = pltpu.VMEM(inputs.shape, f32)
    swapped = swap(
        call(
            outward_kernel,
            shape(group, 2 * share * sensors, width),
            inputs, mask, cotangent,
            scratch_shapes=[wide, wide],
        )
    )
    n_rows = group * sensors
    sums_rows = share * tokens + -(-share // 8) * 8
    sums = call(
        functools.partial(in_kernel, share, sensors),
        shape(sums_rows, width),
        swapped, projector, w_key, w_value,
    )
    sums = [sums] + others(sums)
    layer, d_sums, d_query, grad_out = call(
        functools.partial(out_kernel, share, sensors, rest),
        (
            shape(group, share * sensors, width),
            shape(share * tokens, width),
            shape(share * n_rows, width, kind=bf16),
            shape(width, width),
        ),
        swapped, w_query, w_out, *sums,
    )
    d_sums = [d_sums] + others(d_sums)
    owned = [tokens // n_tm] + [width // n_tm] * 4
    chunk = -(-sum(owned) // (8 * group)) * 8
    base = 2 * share * sensors
    back = call(
        functools.partial(in_back_kernel, share, sensors, rest, n_tm, chunk),
        shape(group, base + n_tm * chunk, width),
        swapped, projector, w_key, w_value, w_query, layer, d_query, grad_out, *sums, *d_sums,
    )
    home = swap(back)
    part = call(functools.partial(fold_kernel, base), shape(n_tm, chunk, width), home)
    me = lax.axis_index("tm")
    mine = lax.dynamic_index_in_dim(part, me, 0, keepdims=False)
    for step in range(1, n_tm):
        gone = lax.dynamic_index_in_dim(part, lax.rem(me + step, n_tm), 0, keepdims=False)
        ring = [(i, (i + step) % n_tm) for i in range(n_tm)]
        mine = mine + lax.ppermute(gone, "tm", ring)
    mine = sum(others(mine), mine)
    gathered = swap(jnp.broadcast_to(mine[None], (group, chunk, width)))
    output_rows, d_inputs = call(
        homeward_kernel,
        (shape(*inputs.shape, kind=bf16), shape(*inputs.shape, kind=bf16)),
        home, mask,
        scratch_shapes=[wide, wide],
    )
    outs = call(
        deal_kernel,
        tuple(shape(n, width) for n in owned),
        gathered.reshape(group * chunk, width),
    )
    return (output_rows, d_inputs, *outs)


def solution(mesh):
    placed = (
        P("sensor", "tm", None),
        P("sensor", "tm"),
        P(),
        P(),
        P(),
        P(),
        P(),
        P("sensor", "tm", None),
    )
    return jax.shard_map(
        functools.partial(per_device, mesh.shape["sensor"], mesh.shape["tm"]),
        mesh=mesh,
        in_specs=placed,
        out_specs=(
            P("sensor", "tm", None),
            P("sensor", "tm", None),
            P("tm", None),
            P("tm", None),
            P("tm", None),
            P("tm", None),
            P("tm", None),
        ),
        check_vma=False,
    )
```

time: 423 us -> 78.8 us (0.19)
  waiting for transfers between devices: 318 us -> 28.5 us
  matrix products: 25.2 us -> 0 us
  blocking collectives: 44.2 us -> 21.1 us
  starting transfers between devices: 0.51 us -> 14.8 us
  between operations: 14.7 us -> 0.74 us
  Pallas kernels: 0 us -> 9.77 us
  other arithmetic: 8.5 us -> 0.01 us
  local copies, waits for them, and re-layouts: 11.4 us -> 3.41 us
    psum x3 -> x0, waiting for transfers between devices: 275 us -> none  [the longest x1 114 us: per_device(): lax.psum((partials[0], partials[1], partials[2], partials[3], partials[4]...]
    psum x1 -> x0, blocking collectives: 44.2 us -> none  [per_device(): numerator, denominator = lax.psum((numerator, denominator), 'sensor')]
    reduce_scatter x5 -> x0, waiting for transfers between devices: 42.2 us -> none  [the longest x1 11.4 us: per_device(): lax.psum_scatter(summed[1], 'tm', scatter_dimension=0, tiled=True)]
    dot_general x23 -> x0, matrix products: 24.5 us -> none  [the longest x3 5.75 us: attend_out(): jnp.dot(asking_unit_vector, pooled_unit_vector.T, precision=largest_energy)]
    all_to_all x0 -> x1, blocking collectives: none -> 21.1 us  [swap(): lax.all_to_all(rows, 'sensor', 0, 0, tiled=True, axis_index_groups=blocks)]
    all_to_all x0 -> x2, waiting for transfers between devices: none -> 17.8 us  [swap(): lax.all_to_all(rows, 'sensor', 0, 0, tiled=True, axis_index_groups=blocks)]
    ppermute x0 -> x4, waiting for transfers between devices: none -> 10.7 us  [the longest x3 9.48 us: others(): lax.ppermute(rows, 'sensor', [(i, (i + step * group) % n_sensor) for i in...]
    pallas_call x0 -> x7, Pallas kernels: none -> 9.77 us  [call(): pl.pallas_call(kernel, out_shape=out_shape, compiler_params=params(), **m...]
  transfers between devices with their start and end apart: 8 -> 6, of which waited for: 7 -> 6; matrix products, arithmetic and copies ran while one was open for 5% -> 0% of each run, Pallas kernels for 0% -> 2%
where the time goes in v2:
time: 78.8 us; the launch traced here: 78.4 us
  waiting for transfers between devices  28.5 us (36%)
  blocking collectives  21.1 us (27%)
  starting transfers between devices  14.8 us (19%)
  Pallas kernels  9.77 us (12%)
  local copies, waits for them, and re-layouts  3.41 us (4%)
    all_to_all x1, blocking collectives, swap(): lax.all_to_all(rows, 'sensor', 0, 0, tiled=True, axis_index_groups=blocks)  21.1 us
    all_to_all x2, waiting for transfers between devices, swap(): lax.all_to_all(rows, 'sensor', 0, 0, tiled=True, axis_index_groups=blocks)  17.8 us
    pallas_call x7, Pallas kernels, call(): pl.pallas_call(kernel, out_shape=out_shape, compiler_params=params(), **m...  9.77 us
    ppermute x3, waiting for transfers between devices, others(): lax.ppermute(rows, 'sensor', [(i, (i + step * group) % n_sensor) for i in...  9.48 us
    all_to_all x2, starting transfers between devices, swap(): lax.all_to_all(rows, 'sensor', 0, 0, tiled=True, axis_index_groups=blocks)  7.38 us
    ppermute x3, starting transfers between devices, others(): lax.ppermute(rows, 'sensor', [(i, (i + step * group) % n_sensor) for i in...  7.32 us
    unnamed x15, local copies, waits for them, and re-layouts  2.71 us
  transfers between devices with their start and end apart: 6, of which 6 were waited for; matrix products, arithmetic and copies ran while one was open for 0% of the time, Pallas kernels for 2%

profile of v2, /device:TPU:0, one launch (start us, length us, event | category | flops | bytes accessed | tf_op | source)
XLA Modules:
  0.0 78.4 jit_solution(12351921253852063478)
XLA Ops:
  0.6 0.8 copy.15.mask_ref
  1.4 0.0 copy-start
  1.4 0.9 %copy-done = bf16[64,16,128]{2,1,0:T(8,128)(2,1)S(1)} copy-done((bf16[64,16,128]{2,1,0:T(8,128)(2,1)S(1)}, bf16[64,16,128]{2,1,0:T(8,128)(2,1)}, u32[]{:S(2)}) %copy-start) | copy-done | bytes 262168
  2.4 0.0 copy-start.1
  2.4 0.9 %copy-done.1 = bf16[64,16,128]{2,1,0:T(8,128)(2,1)S(1)} copy-done((bf16[64,16,128]{2,1,0:T(8,128)(2,1)S(1)}, bf16[64,16,128]{2,1,0:T(8,128)(2,1)}, u32[]{:S(2)}) %copy-start.1) | copy-done | bytes 262168
  3.3 0.6 shard_map.135
  3.9 0.0 copy-start.2
  3.9 0.0 copy-start.3
  4.0 0.0 copy-start.4
  4.0 0.0 copy-start.5
  4.0 0.0 copy-start.6
  4.0 21.1 %all_to_all.15.swapped = f32[8,256,128]{2,1,0:T(8,128)S(1)} all-to-all(f32[8,256,128]{2,1,0:T(8,128)S(1)} %shard_map.135), channel_id=1, replica_groups={{0,2,4,6,8,10,12,14},{16,18,20,22,24,26,28,30},{1,3,5,7,9,11,13,15},{17..., dimensions={0} | all-to-all | bytes 2097152 | tf_op jit(solution)/shard_map/all_to_all | solution.py:262
  25.1 0.0 copy-done.2
  25.1 0.0 copy-done.3
  25.1 0.0 copy-done.4
  25.2 1.1 %shard_map.136.refs_0_ = f32[136,128]{1,0:T(8,128)S(1)} custom-call(f32[8,256,128]{2,1,0:T(8,128)S(1)} %all_to_all.15.swapped, f32[64,128]{1,0:T(8,128)S(1)} %copy-done.2, bf16[128,128]{1,0:T(8,128)(2,1)S(1)} %copy-done.3, bf16[128,128]{1,0:T(8,128)(2,1)S(1)} %copy-done.4), custom_call_target="tpu_custom_call" | custom-call | tf_op jit(solution)/shard_map/pallas_call | solution.py:245
  26.2 2.7 %collective-permute-start = (f32[136,128]{1,0:T(8,128)S(1)}, f32[136,128]{1,0:T(8,128)S(1)}, u32[]{:S(2)}, u32[]{:S(2)}) collective-permute-start(f32[136,128]{1,0:T(8,128)S(1)} %shard_map.136.refs_0_), channel_id=1, source_target_pairs={{0,16},{2,18},{4,20},{6,22},{8,24},{10,26},{12,28},{14,30},{16,0},... | collective-permute-start | bytes 208904 | tf_op jit(solution)/shard_map/ppermute | solution.py:266
  28.9 3.4 %collective-permute-done.refs_1_ = f32[136,128]{1,0:T(8,128)S(1)} collective-permute-done((f32[136,128]{1,0:T(8,128)S(1)}, f32[136,128]{1,0:T(8,128)S(1)}, u32[]{:S(2)}, u32[]{:S(2)}) %collective-permute-start) | collective-permute-done | bytes 69664 | tf_op jit(solution)/shard_map/ppermute | solution.py:266
  32.3 0.0 copy-done.5
  32.3 0.0 copy-done.6
  32.3 2.9 %shard_map.137 = (f32[8,128,128]{2,1,0:T(8,128)S(1)}, f32[128,128]{1,0:T(8,128)S(1)}, bf16[1024,128]{1,0:T(8,128)(2,1)S(1)}, f32[128,128]{1,0:T(8,128)S(1)}) custom-call(f32[8,256,128]{2,1,0:T(8,128)S(1)} %all_to_all.15.swapped, bf16[128,128]{1,0:T(8,128)(2,1)S(1)} %copy-done.5, bf16[128,128]{1,0:T(8,128)(2,1)S(1)} %copy-done.6, ...), custom_call_target="tpu_custom_call" | custom-call | tf_op jit(solution)/shard_map/pallas_call | solution.py:245
  35.2 2.0 %collective-permute-start.1 = (f32[128,128]{1,0:T(8,128)S(1)}, f32[128,128]{1,0:T(8,128)S(1)}, u32[]{:S(2)}, u32[]{:S(2)}) collective-permute-start(f32[128,128]{1,0:T(8,128)S(1)} %get-tuple-element.21.refs_2_), channel_id=1, source_target_pairs={{0,16},{2,18},{4,20},{6,22},{8,24},{10,26},{12,28},{14,30},{16,0},... | collective-permute-start | bytes 196616 | tf_op jit(solution)/shard_map/ppermute | solution.py:266
  37.2 3.9 %collective-permute-done.1.refs_3_ = f32[128,128]{1,0:T(8,128)S(1)} collective-permute-done((f32[128,128]{1,0:T(8,128)S(1)}, f32[128,128]{1,0:T(8,128)S(1)}, u32[]{:S(2)}, u32[]{:S(2)}) %collective-permute-start.1) | collective-permute-done | bytes 65568 | tf_op jit(solution)/shard_map/ppermute | solution.py:266
  41.1 3.0 %shard_map.138 = f32[8,336,128]{2,1,0:T(8,128)} custom-call(f32[8,256,128]{2,1,0:T(8,128)S(1)} %all_to_all.15.swapped, f32[64,128]{1,0:T(8,128)S(1)} %copy-done.2, bf16[128,128]{1,0:T(8,128)(2,1)S(1)} %copy-done.3, bf16[128,128]{1,0:T(8,128)(2,1)S(1)} %copy-done.4, bf16[128,128]{1,0:T(8,128)(2,1)S(1)} %copy-done.5, ...), custom_call_target="tpu_custom_call" | custom-call | tf_op jit(solution)/shard_map/pallas_call | solution.py:245
  44.1 3.6 %all-to-all-start.1 = ((f32[8,336,128]{2,1,0:T(8,128)}), f32[8,336,128]{2,1,0:T(8,128)S(1)}, u32[]{:S(2)}, u32[]{:S(2)}) async-start(f32[8,336,128]{2,1,0:T(8,128)} %shard_map.138), calls=%async_computation.1 | async-start | bytes 2752512 | tf_op jit(solution)/shard_map/all_to_all | solution.py:262
  47.7 13.1 %all-to-all-done.1.rows_ref.parts_ref = f32[8,336,128]{2,1,0:T(8,128)S(1)} async-done(((f32[8,336,128]{2,1,0:T(8,128)}), f32[8,336,128]{2,1,0:T(8,128)S(1)}, u32[]{:S(2)}, u32[]{:S(2)}) %all-to-all-start.1) | async-done | bytes 1376288 | tf_op jit(solution)/shard_map/all_to_all | solution.py:262
  60.9 0.1 collective-permute-start.2
  60.9 1.2 %collective-permute-done.2 = f32[40,128]{1,0:T(8,128)S(1)} collective-permute-done((f32[40,128]{1,0:T(8,128)S(1)}, f32[40,128]{1,0:T(8,128)S(1)}, u32[]{:S(2)}, u32[]{:S(2)}) %collective-permute-start.2) | collective-permute-done | bytes 20512 | tf_op jit(solution)/shard_map/ppermute | solution.py:318
  62.1 2.7 %collective-permute-start.3 = (f32[40,128]{1,0:T(8,128)S(1)}, f32[40,128]{1,0:T(8,128)S(1)}, u32[]{:S(2)}, u32[]{:S(2)}) collective-permute-start(f32[40,128]{1,0:T(8,128)S(1)} %bitcast_add_fusion), channel_id=1, source_target_pairs={{0,16},{2,18},{4,20},{6,22},{8,24},{10,26},{12,28},{14,30},{16,0},... | collective-permute-start | bytes 61448 | tf_op jit(solution)/shard_map/ppermute | solution.py:266
  64.8 2.2 %collective-permute-done.3 = f32[40,128]{1,0:T(8,128)S(1)} collective-permute-done((f32[40,128]{1,0:T(8,128)S(1)}, f32[40,128]{1,0:T(8,128)S(1)}, u32[]{:S(2)}, u32[]{:S(2)}) %collective-permute-start.3) | collective-permute-done | bytes 20512 | tf_op jit(solution)/shard_map/ppermute | solution.py:266
  67.0 0.7 broadcast_in_dim.2
  67.7 3.8 %all-to-all-start.2 = ((f32[8,40,128]{2,1,0:T(8,128)}), f32[8,40,128]{2,1,0:T(8,128)S(1)}, u32[]{:S(2)}, u32[]{:S(2)}) async-start(f32[8,40,128]{2,1,0:T(8,128)} %broadcast_in_dim.2), calls=%async_computation.2 | async-start | bytes 327680 | tf_op jit(solution)/shard_map/all_to_all | solution.py:262
  71.5 1.5 %shard_map.139 = (bf16[64,16,128]{2,1,0:T(8,128)(2,1)}, bf16[64,16,128]{2,1,0:T(8,128)(2,1)}) custom-call(f32[8,336,128]{2,1,0:T(8,128)S(1)} %all-to-all-done.1.rows_ref.parts_ref, s32[64,16]{1,0:T(8,128)S(1)} %copy.15.mask_ref), custom_call_target="tpu_custom_call" | custom-call | tf_op jit(solution)/shard_map/pallas_call | solution.py:245
  72.9 4.8 %all-to-all-done.2 = f32[8,40,128]{2,1,0:T(8,128)S(1)} async-done(((f32[8,40,128]{2,1,0:T(8,128)}), f32[8,40,128]{2,1,0:T(8,128)S(1)}, u32[]{:S(2)}, u32[]{:S(2)}) %all-to-all-start.2) | async-done | bytes 163872 | tf_op jit(solution)/shard_map/all_to_all | solution.py:262
  77.7 0.7 shard_map.141
  (4 shorter events, 0.0 us)
Async XLA Ops:
  1.4 1.0 %copy-start = (bf16[64,16,128]{2,1,0:T(8,128)(2,1)S(1)}, bf16[64,16,128]{2,1,0:T(8,128)(2,1)}, u32[]{:S(2)}) copy-start(bf16[64,16,128]{2,1,0:T(8,128)(2,1)} %inputs_ref.1) | copy-start | bytes 786436
  2.4 0.9 %copy-start.1 = (bf16[64,16,128]{2,1,0:T(8,128)(2,1)S(1)}, bf16[64,16,128]{2,1,0:T(8,128)(2,1)}, u32[]{:S(2)}) copy-start(bf16[64,16,128]{2,1,0:T(8,128)(2,1)} %cotangent_ref.1) | copy-start | bytes 786436
  3.9 21.2 %copy-start.2 = (f32[64,128]{1,0:T(8,128)S(1)}, f32[64,128]{1,0:T(8,128)}, u32[]{:S(2)}) copy-start(f32[64,128]{1,0:T(8,128)} %projector.3) | copy-start | bytes 98308
  3.9 21.2 %copy-start.3 = (bf16[128,128]{1,0:T(8,128)(2,1)S(1)}, bf16[128,128]{1,0:T(8,128)(2,1)}, u32[]{:S(2)}) copy-start(bf16[128,128]{1,0:T(8,128)(2,1)} %wk.3) | copy-start | bytes 98308
  4.0 21.2 %copy-start.4 = (bf16[128,128]{1,0:T(8,128)(2,1)S(1)}, bf16[128,128]{1,0:T(8,128)(2,1)}, u32[]{:S(2)}) copy-start(bf16[128,128]{1,0:T(8,128)(2,1)} %wv.3) | copy-start | bytes 98308
  4.0 28.3 %copy-start.5 = (bf16[128,128]{1,0:T(8,128)(2,1)S(1)}, bf16[128,128]{1,0:T(8,128)(2,1)}, u32[]{:S(2)}) copy-start(bf16[128,128]{1,0:T(8,128)(2,1)} %wq.3) | copy-start | bytes 98308
  4.0 28.3 %copy-start.6 = (bf16[128,128]{1,0:T(8,128)(2,1)S(1)}, bf16[128,128]{1,0:T(8,128)(2,1)}, u32[]{:S(2)}) copy-start(bf16[128,128]{1,0:T(8,128)(2,1)} %wo.1) | copy-start | bytes 98308
  26.2 6.0 %collective-permute-start = (f32[136,128]{1,0:T(8,128)S(1)}, f32[136,128]{1,0:T(8,128)S(1)}, u32[]{:S(2)}, u32[]{:S(2)}) collective-permute-start(f32[136,128]{1,0:T(8,128)S(1)} %shard_map.136.refs_0_), channel_id=1, source_target_pairs={{0,16},{2,18},{4,20},{6,22},{8,24},{10,26},{12,28},{14,30},{16,0},... | collective-permute-start | bytes 208904 | tf_op jit(solution)/shard_map/ppermute | solution.py:266
  35.2 5.9 %collective-permute-start.1 = (f32[128,128]{1,0:T(8,128)S(1)}, f32[128,128]{1,0:T(8,128)S(1)}, u32[]{:S(2)}, u32[]{:S(2)}) collective-permute-start(f32[128,128]{1,0:T(8,128)S(1)} %get-tuple-element.21.refs_2_), channel_id=1, source_target_pairs={{0,16},{2,18},{4,20},{6,22},{8,24},{10,26},{12,28},{14,30},{16,0},... | collective-permute-start | bytes 196616 | tf_op jit(solution)/shard_map/ppermute | solution.py:266
  44.1 16.7 %all-to-all-start.1 = ((f32[8,336,128]{2,1,0:T(8,128)}), f32[8,336,128]{2,1,0:T(8,128)S(1)}, u32[]{:S(2)}, u32[]{:S(2)}) async-start(f32[8,336,128]{2,1,0:T(8,128)} %shard_map.138), calls=%async_computation.1 | async-start | bytes 2752512 | tf_op jit(solution)/shard_map/all_to_all | solution.py:262
  60.9 1.3 %collective-permute-start.2 = (f32[40,128]{1,0:T(8,128)S(1)}, f32[40,128]{1,0:T(8,128)S(1)}, u32[]{:S(2)}, u32[]{:S(2)}) collective-permute-start(f32[40,128]{1,0:T(8,128)S(1)} %dynamic-slice_bitcast_fusion), channel_id=1, source_target_pairs={{0,1},{1,0},{2,3},{3,2},{4,5},{5,4},{6,7},{7,6},{8,9},{9,8},{10,11... | collective-permute-start | bytes 61448 | tf_op jit(solution)/shard_map/ppermute | solution.py:318
  62.1 4.9 %collective-permute-start.3 = (f32[40,128]{1,0:T(8,128)S(1)}, f32[40,128]{1,0:T(8,128)S(1)}, u32[]{:S(2)}, u32[]{:S(2)}) collective-permute-start(f32[40,128]{1,0:T(8,128)S(1)} %bitcast_add_fusion), channel_id=1, source_target_pairs={{0,16},{2,18},{4,20},{6,22},{8,24},{10,26},{12,28},{14,30},{16,0},... | collective-permute-start | bytes 61448 | tf_op jit(solution)/shard_map/ppermute | solution.py:266
  67.7 10.0 %all-to-all-start.2 = ((f32[8,40,128]{2,1,0:T(8,128)}), f32[8,40,128]{2,1,0:T(8,128)S(1)}, u32[]{:S(2)}, u32[]{:S(2)}) async-start(f32[8,40,128]{2,1,0:T(8,128)} %broadcast_in_dim.2), calls=%async_computation.2 | async-start | bytes 327680 | tf_op jit(solution)/shard_map/all_to_all | solution.py:262

commit v3 on v2

v3 whole, which is shorter than its diff:
```python
import functools

import jax
import jax.numpy as jnp
from jax import lax
from jax.experimental import pallas as pl
from jax.experimental.pallas import tpu as pltpu
from jax.sharding import PartitionSpec as P

sharpness_divisor = 12.0
epsilon = 1e-06
f32 = jnp.float32
bf16 = jnp.bfloat16


def params(mebibytes=32):
    return pltpu.CompilerParams(vmem_limit_bytes=mebibytes * 1024 * 1024)


def dot(left, right, left_dim, right_dim):
    return lax.dot_general(
        left, right, (((left_dim,), (right_dim,)), ((), ())), preferred_element_type=f32
    )


def rounded_dot(left, right, left_dim, right_dim):
    return dot(left.astype(bf16), right.astype(bf16), left_dim, right_dim)


def inverse_norm(vector):
    return lax.rsqrt(jnp.mean(vector * vector, axis=-1, keepdims=True) + epsilon)


def normalize_back(inverse, unit, gradient):
    return inverse * (gradient - unit * jnp.mean(unit * gradient, axis=-1, keepdims=True))


def diagonal(tokens):
    rows = lax.broadcasted_iota(jnp.int32, (tokens, tokens), 0)
    return rows == lax.broadcasted_iota(jnp.int32, (tokens, tokens), 1)


def turned_mask(mask_ref):
    sensors = mask_ref.shape[1]
    return dot(diagonal(sensors).astype(f32).astype(bf16), mask_ref[...].astype(f32).astype(bf16), 1, 1)


def outward_kernel(inputs_ref, mask_ref, cotangent_ref, far_ref, near, near_cotangent, wide, out_ref, sems):
    sensors, steps, _ = inputs_ref.shape
    places = out_ref.shape[0]
    share = steps // places
    rows = share * sensors
    first = pltpu.make_async_copy(inputs_ref, near, sems.at[2 * places])
    second = pltpu.make_async_copy(cotangent_ref, near_cotangent, sems.at[2 * places + 1])
    first.start()
    second.start()
    marks = turned_mask(mask_ref)
    sent = []

    def send(place, half):
        block = (place, pl.ds(half * rows, rows))
        copy = pltpu.make_async_copy(
            out_ref.at[block], far_ref.at[block], sems.at[half * places + place]
        )
        copy.start()
        sent.append(copy)

    first.wait()
    wide[...] = near[...].astype(f32)
    for place in range(places):
        for own in range(share):
            t = place * share + own
            out_ref[place, own * sensors : (own + 1) * sensors, :] = (
                wide[:, t, :] * marks[:, t : t + 1]
            )
        send(place, 0)
    second.wait()
    wide[...] = near_cotangent[...].astype(f32)
    for place in range(places):
        for own in range(share):
            at = rows + own * sensors
            out_ref[place, at : at + sensors, :] = wide[:, place * share + own, :]
        send(place, 1)
    for copy in sent:
        copy.wait()


def homeward_kernel(rows_ref, mask_ref, layer_ref, d_inputs_ref, wide, wide_gradient):
    sensors, steps, _ = layer_ref.shape
    share = steps // rows_ref.shape[0]
    marks = turned_mask(mask_ref)
    for t in range(steps):
        place, own = divmod(t, share)
        wide[:, t, :] = rows_ref[place, own * sensors : (own + 1) * sensors, :]
        at = (share + own) * sensors
        wide_gradient[:, t, :] = rows_ref[place, at : at + sensors, :] * marks[:, t : t + 1]
    layer_ref[...] = wide[...].astype(bf16)
    d_inputs_ref[...] = wide_gradient[...].astype(bf16)


def rows_of(ref, block, sensors):
    rows = ref[:, block * sensors : (block + 1) * sensors, :]
    return rows.reshape(rows.shape[0] * sensors, rows.shape[2])


def put_rows(ref, block, sensors, rows):
    ref[:, block * sensors : (block + 1) * sensors, :] = rows.reshape(
        ref.shape[0], sensors, rows.shape[1]
    )


def scale_of(width):
    return sharpness_divisor / width


def weigh_in(key_raw, projector):
    inverse = inverse_norm(key_raw)
    unit = key_raw * inverse
    mapping = projector * inverse_norm(projector)
    scale = scale_of(key_raw.shape[-1])
    return inverse, unit, jnp.exp(scale * rounded_dot(mapping, unit, 1, 1))


def in_kernel(share, sensors, swapped, projector, wk, wv, sums_ref):
    tokens, width = projector.shape
    same = diagonal(tokens)
    tail = share * tokens
    sums_ref[tail:, :] = jnp.zeros((sums_ref.shape[0] - tail, width), f32)
    both_weights = jnp.concatenate([wk[...], wv[...]], axis=1)
    for t in range(share):
        hidden = rows_of(swapped, t, sensors).astype(bf16)
        both = dot(hidden, both_weights, 1, 0)
        _, _, weights = weigh_in(both[:, :width], projector[...])
        sums_ref[t * tokens : (t + 1) * tokens, :] = rounded_dot(weights, both[:, width:], 1, 0)
        den = jnp.sum(weights, axis=1, keepdims=True)
        sums_ref[tail + t : tail + t + 1, :tokens] = jnp.sum(
            jnp.where(same, den, 0.0), axis=0, keepdims=True
        )


def total_of(refs):
    total = refs[0][...]
    for ref in refs[1:]:
        total = total + ref[...]
    return total


def num_den(total, t, share, tokens):
    num = total[t * tokens : (t + 1) * tokens, :]
    at = share * tokens + t
    den = jnp.sum(
        jnp.where(diagonal(tokens), total[at : at + 1, :tokens], 0.0), axis=1, keepdims=True
    )
    return num, den


def ready_kernel(
    share, sensors, swapped, projector, wk, wv, wq, wo,
    in_ref, out_ref,
):
    width = wk.shape[0]
    tokens = projector.shape[0]
    together = jnp.concatenate([wk[...], wv[...], wq[...]], axis=1)
    for t in range(share):
        hidden = rows_of(swapped, t, sensors).astype(bf16)
        at = slice(t * hidden.shape[0], (t + 1) * hidden.shape[0])
        raw = dot(hidden, together, 1, 0)
        inverse, unit, weights = weigh_in(raw[:, :width], projector[...])
        query_raw = raw[:, 2 * width :]
        query_inverse = inverse_norm(query_raw)
        in_ref[0, at, :] = unit
        in_ref[1, at, :] = jnp.broadcast_to(inverse, unit.shape)
        in_ref[2, at, :] = raw[:, width : 2 * width].astype(bf16).astype(f32)
        for block in range(hidden.shape[0] // width):
            to = block * tokens + t * hidden.shape[0]
            in_ref[3, to : to + tokens, :] = weights[:, block * width : (block + 1) * width]
        out_ref[0, at, :] = query_raw * query_inverse
        out_ref[1, at, :] = jnp.broadcast_to(query_inverse, unit.shape)
        cotangent = rows_of(swapped, share + t, sensors).astype(bf16)
        out_ref[2, at, :] = dot(cotangent, wo[...], 1, 1).astype(bf16).astype(f32)


def out_kernel(share, terms, ready_ref, *refs):
    sums, (ds_ref, normed_ref, d_scores_ref) = refs[:terms], refs[terms:]
    width = ready_ref.shape[2]
    tokens = ds_ref.shape[0] // share
    scale = scale_of(width)
    total = total_of(sums)
    n_rows = ready_ref.shape[1] // share
    for t in range(share):
        at = slice(t * n_rows, (t + 1) * n_rows)
        own = slice(t * tokens, (t + 1) * tokens)
        unit = ready_ref[0, at, :]
        num, den = num_den(total, t, share, tokens)
        summary = num / den
        pooled_inverse = inverse_norm(summary)
        pooled = summary * pooled_inverse
        weights = jnp.exp(scale * rounded_dot(pooled, unit, 1, 1))
        attention = weights / jnp.sum(weights, axis=0, keepdims=True)
        blended = rounded_dot(attention, summary, 0, 0)
        blended_inverse = inverse_norm(blended)
        normed = blended * blended_inverse
        normed_ref[at, :] = normed.astype(bf16)
        d_blended = normalize_back(blended_inverse, normed, ready_ref[2, at, :])
        d_attention = rounded_dot(summary, d_blended, 1, 1)
        d_scores = attention * (
            d_attention - jnp.sum(attention * d_attention, axis=0, keepdims=True)
        )
        d_pooled = scale * rounded_dot(d_scores, unit, 1, 0)
        ds_ref[own, :] = rounded_dot(attention, d_blended, 1, 0) + normalize_back(
            pooled_inverse, pooled, d_pooled
        )
        d_scores_ref[own, :] = d_scores


def query_kernel(share, sensors, terms, swapped, wq, wo, ready_ref, normed_ref, d_scores_ref, *refs):
    sums, (lay_ref, dh_ref) = refs[:terms], refs[terms:]
    width = wq.shape[0]
    tokens = d_scores_ref.shape[0] // share
    scale = scale_of(width)
    total = total_of(sums)
    n_rows = ready_ref.shape[1] // share
    grad_rows = share * n_rows
    for t in range(share):
        at = slice(t * n_rows, (t + 1) * n_rows)
        rows = rows_of(swapped, t, sensors)
        cotangent = rows_of(swapped, share + t, sensors)
        normed = normed_ref[at, :]
        layer = (rows + dot(normed, wo[...], 1, 0)).astype(bf16).astype(f32)
        put_rows(lay_ref, t, sensors, layer)
        grad_out = dot(normed, cotangent.astype(bf16), 0, 0)
        num, den = num_den(total, t, share, tokens)
        summary = num / den
        pooled = summary * inverse_norm(summary)
        d_unit = scale * rounded_dot(d_scores_ref[t * tokens : (t + 1) * tokens, :], pooled, 0, 0)
        d_query = normalize_back(ready_ref[1, at, :], ready_ref[0, at, :], d_unit).astype(bf16)
        grad_query = dot(rows.astype(bf16), d_query, 0, 0)
        dh_ref[at, :] = cotangent + dot(d_query, wq[...], 1, 1)
        for i, grad in enumerate((grad_query, grad_out)):
            to = slice(grad_rows + i * width, grad_rows + (i + 1) * width)
            dh_ref[to, :] = grad if t == 0 else dh_ref[to, :] + grad


def put_partials(ref, grads):
    owners, rows, width = ref.shape
    for m in range(owners):
        at = 0
        for grad in grads:
            own = grad.shape[0] // owners
            ref[m, at : at + own, :] = grad[m * own : (m + 1) * own, :]
            at += own
        if at < rows:
            ref[m, at:, :] = jnp.zeros((rows - at, width), f32)


def in_back_kernel(
    share, sensors, terms, swapped, projector, wk, wv, ready_ref, dh_ref, layer_ref, *refs
):
    sums, d_sums = refs[:terms], refs[terms : 2 * terms]
    out_ref, part_ref = refs[2 * terms :]
    out_ref[:, : share * sensors, :] = layer_ref[...]
    tokens, width = projector.shape
    scale = scale_of(width)
    total = total_of(sums)
    d_total = total_of(d_sums)
    mapping_inverse = inverse_norm(projector[...])
    mapping = projector[...] * mapping_inverse
    turned = jnp.concatenate([wk[...], wv[...]], axis=1)
    gradients = None
    n_rows = ready_ref.shape[1] // share
    grad_rows = share * n_rows
    for t in range(share):
        at = slice(t * n_rows, (t + 1) * n_rows)
        own = slice(t * tokens, (t + 1) * tokens)
        hidden = rows_of(swapped, t, sensors).astype(bf16)
        unit = ready_ref[0, at, :]
        weights = jnp.concatenate(
            [
                ready_ref[3, t * n_rows + i * tokens : t * n_rows + (i + 1) * tokens, :]
                for i in range(n_rows // width)
            ],
            axis=1,
        )
        num, den = num_den(total, t, share, tokens)
        d_summary = d_total[own, :]
        d_num = d_summary / den
        d_den = -jnp.sum(d_summary * num, axis=1, keepdims=True) / (den * den)
        d_scores = (rounded_dot(d_num, ready_ref[2, at, :], 1, 1) + d_den) * weights
        d_unit = scale * rounded_dot(d_scores, mapping, 0, 0)
        d_mapping = scale * rounded_dot(d_scores, unit, 1, 0)
        d_key = normalize_back(ready_ref[1, at, :], unit, d_unit).astype(bf16)
        d_values = rounded_dot(weights, d_num, 0, 0).astype(bf16)
        together = jnp.concatenate([d_key, d_values], axis=1)
        d_hidden = dh_ref[at, :] + dot(together, turned, 1, 1)
        put_rows(out_ref, share + t, sensors, d_hidden)
        more = (normalize_back(mapping_inverse, mapping, d_mapping), dot(hidden, together, 0, 0))
        gradients = more if t == 0 else tuple(a + b for a, b in zip(gradients, more))
    parts = [gradients[0], gradients[1][:, :width], gradients[1][:, width:]]
    parts += [dh_ref[grad_rows + i * width : grad_rows + (i + 1) * width, :] for i in range(2)]
    put_partials(part_ref, parts)


def deal_kernel(count, place_ref, *refs):
    chunks, out_refs, rows = refs[:count], refs[count:-1], refs[-1]
    for m, chunk in enumerate(chunks):
        source = lax.bitwise_xor(place_ref[0], m)
        rows[pl.ds(source * chunk.shape[0], chunk.shape[0]), :] = chunk[...]
    at = 0
    for out in out_refs:
        out[...] = rows[at : at + out.shape[0], :]
        at += out.shape[0]


def call(kernel, out_shape, *args, vmem=32, **more):
    return pl.pallas_call(kernel, out_shape=out_shape, compiler_params=params(vmem), **more)(*args)


def group_size(most, *sizes):
    group = 1
    while group < most and all(size % (2 * group) == 0 for size in sizes):
        group *= 2
    return group


def per_device(n_sensor, n_tm, inputs, mask, projector, w_key, w_value, w_query, w_out, cotangent):
    sensors, steps, width = inputs.shape
    tokens = projector.shape[0]
    group = group_size(8, n_sensor, steps)
    rest = n_sensor // group
    share = steps // group
    blocks = [list(range(r * group, (r + 1) * group)) for r in range(rest)]

    def swap(rows):
        return lax.all_to_all(rows, "sensor", 0, 0, tiled=True, axis_index_groups=blocks)

    def others(rows):
        return [
            lax.ppermute(
                rows, "sensor", [(i, (i + step * group) % n_sensor) for i in range(n_sensor)]
            )
            for step in range(1, rest)
        ]

    def shape(*dims, kind=f32):
        return jax.ShapeDtypeStruct(dims, kind)

    wide = pltpu.VMEM(inputs.shape, f32)
    mask = mask.T

    place_spec = pl.BlockSpec(memory_space=pltpu.SMEM)
    far_spec = pl.BlockSpec(memory_space=pltpu.HBM)
    near_spec = pl.BlockSpec(memory_space=pltpu.VMEM)
    swapped = swap(
        call(
            outward_kernel,
            shape(group, 2 * share * sensors, width),
            inputs, mask, cotangent,
            vmem=60,
            in_specs=[far_spec, near_spec, far_spec],
            out_specs=far_spec,
            scratch_shapes=[
                pltpu.VMEM(inputs.shape, bf16),
                pltpu.VMEM(inputs.shape, bf16),
                wide,
                pltpu.VMEM((group, 2 * share * sensors, width), f32),
                pltpu.SemaphoreType.DMA((2 * group + 2,)),
            ],
        )
    )
    n_rows = group * sensors
    sums_rows = share * tokens + -(-share // 8) * 8
    sums = call(
        functools.partial(in_kernel, share, sensors),
        shape(sums_rows, width),
        swapped, projector, w_key, w_value,
    )
    sums = [sums] + others(sums)
    tokens_shape = shape(share * tokens, n_rows)
    owned = [tokens // n_tm] + [width // n_tm] * 4
    quarter = group_size(4, n_sensor)
    chunk = -(-sum(owned) // (8 * quarter)) * 8
    ready_in, ready_out = call(
        functools.partial(ready_kernel, share, sensors),
        (shape(4, share * n_rows, width), shape(3, share * n_rows, width)),
        swapped, projector, w_key, w_value, w_query, w_out,
    )
    d_sums, normed, d_scores = call(
        functools.partial(out_kernel, share, rest),
        (shape(share * tokens, width), shape(share * n_rows, width, kind=bf16), tokens_shape),
        ready_out, *sums,
    )
    d_sums = [d_sums] + others(d_sums)
    layer, d_hidden = call(
        functools.partial(query_kernel, share, sensors, rest),
        (
            shape(group, share * sensors, width),
            shape(share * n_rows + 2 * width, width),
        ),
        swapped, w_query, w_out, ready_out, normed, d_scores, *sums,
    )
    back, part = call(
        functools.partial(in_back_kernel, share, sensors, rest),
        (
            shape(group, 2 * share * sensors, width),
            shape(n_tm, quarter * chunk, width),
        ),
        swapped, projector, w_key, w_value, ready_in, d_hidden, layer, *sums, *d_sums,
    )
    me = lax.axis_index("tm")
    mine = lax.dynamic_index_in_dim(part, me, 0, keepdims=False)
    for step in range(1, n_tm):
        gone = lax.dynamic_index_in_dim(part, lax.rem(me + step, n_tm), 0, keepdims=False)
        ring = [(i, (i + step) % n_tm) for i in range(n_tm)]
        mine = mine + lax.ppermute(gone, "tm", ring)

    def partner(rows, m):
        return lax.ppermute(rows, "sensor", [(i, i ^ m) for i in range(n_sensor)])

    mine = mine.reshape(quarter, chunk, width)
    place = lax.rem(lax.axis_index("sensor"), quarter)
    total = lax.dynamic_index_in_dim(mine, place, 0, keepdims=False)
    for m in range(1, quarter):
        gone = lax.dynamic_index_in_dim(mine, lax.bitwise_xor(place, m), 0, keepdims=False)
        total = total + partner(gone, m)
    home = swap(back)
    output_rows, d_inputs = call(
        homeward_kernel,
        (shape(*inputs.shape, kind=bf16), shape(*inputs.shape, kind=bf16)),
        home, mask,
        scratch_shapes=[wide, wide],
    )
    m = quarter
    while n_sensor % (2 * m) == 0:
        gone = partner(total, m)
        m *= 2
        if n_sensor % (2 * m):
            total, gone, output_rows, d_inputs = lax.optimization_barrier(
                (total, gone, output_rows, d_inputs)
            )
        total = total + gone
    odd = n_sensor // m
    spread = [
        lax.ppermute(total, "sensor", [(i, (i + step * m) % n_sensor) for i in range(n_sensor)])
        for step in range(1, odd)
    ]
    total = sum(spread, total)
    chunks = [total] + [partner(total, m) for m in range(1, quarter)]
    outs = call(
        functools.partial(deal_kernel, quarter),
        tuple(shape(n, width) for n in owned),
        place[None], *chunks,
        in_specs=[place_spec] + [near_spec] * quarter,
        scratch_shapes=[pltpu.VMEM((quarter * chunk, width), f32)],
    )
    return (output_rows, d_inputs, *outs)


def solution(mesh):
    placed = (
        P("sensor", "tm", None),
        P("sensor", "tm"),
        P(),
        P(),
        P(),
        P(),
        P(),
        P("sensor", "tm", None),
    )
    return jax.shard_map(
        functools.partial(per_device, mesh.shape["sensor"], mesh.shape["tm"]),
        mesh=mesh,
        in_specs=placed,
        out_specs=(
            P("sensor", "tm", None),
            P("sensor", "tm", None),
            P("tm", None),
            P("tm", None),
            P("tm", None),
            P("tm", None),
            P("tm", None),
        ),
        check_vma=False,
    )
```

time: 78.8 us -> 73.7 us (0.935)
  waiting for transfers between devices: 28.5 us -> 20.1 us
  starting transfers between devices: 14.8 us -> 18.7 us
  local copies, waits for them, and re-layouts: 3.41 us -> 0.06 us
  Pallas kernels: 9.77 us -> 12.5 us
    all_to_all x2 -> x1, waiting for transfers between devices: 17.8 us -> 0.01 us  [swap(): lax.all_to_all(rows, 'sensor', 0, 0, tiled=True, axis_index_groups=blocks)]
    ppermute x0 -> x8, waiting for transfers between devices: none -> 13.3 us  [partner(): return lax.ppermute(rows, 'sensor', [(i, i ^ m) for i in range(n_sensor)])]
    ppermute x0 -> x8, starting transfers between devices: none -> 10.2 us  [partner(): return lax.ppermute(rows, 'sensor', [(i, i ^ m) for i in range(n_sensor)])]
    ppermute x3 -> x2, waiting for transfers between devices: 9.48 us -> 5.39 us  [others(): lax.ppermute(rows, 'sensor', [(i, (i + step * group) % n_sensor) for i in...]
    all_to_all x2 -> x1, starting transfers between devices: 7.38 us -> 3.69 us  [swap(): lax.all_to_all(rows, 'sensor', 0, 0, tiled=True, axis_index_groups=blocks)]
    pallas_call x7 -> x8, Pallas kernels: 9.77 us -> 12.5 us  [call(): pl.pallas_call(kernel, out_shape=out_shape, compiler_params=params(vmem),...]
    unnamed x15 -> x12, local copies, waits for them, and re-layouts: 2.71 us -> 0.02 us
    ppermute x3 -> x2, starting transfers between devices: 7.32 us -> 4.67 us  [others(): lax.ppermute(rows, 'sensor', [(i, (i + step * group) % n_sensor) for i in...]
  transfers between devices with their start and end apart: 6 -> 12, of which waited for: 6 -> 10; matrix products, arithmetic and copies ran while one was open for 0% -> 0% of each run, Pallas kernels for 2% -> 5%
where the time goes in v3:
time: 73.7 us; the launch traced here: 73.4 us
  blocking collectives  21.2 us (29%)
  waiting for transfers between devices  20.1 us (27%)
  starting transfers between devices  18.7 us (25%)
  Pallas kernels  12.5 us (17%)
  between operations  0.8 us (1%)
    all_to_all x1, blocking collectives, swap(): lax.all_to_all(rows, 'sensor', 0, 0, tiled=True, axis_index_groups=blocks)  21.2 us
    ppermute x8, waiting for transfers between devices, partner(): return lax.ppermute(rows, 'sensor', [(i, i ^ m) for i in range(n_sensor)])  13.3 us
    pallas_call x8, Pallas kernels, call(): pl.pallas_call(kernel, out_shape=out_shape, compiler_params=params(vmem),...  12.5 us
    ppermute x8, starting transfers between devices, partner(): return lax.ppermute(rows, 'sensor', [(i, i ^ m) for i in range(n_sensor)])  10.2 us
    ppermute x2, waiting for transfers between devices, others(): lax.ppermute(rows, 'sensor', [(i, (i + step * group) % n_sensor) for i in...  5.39 us
    ppermute x2, starting transfers between devices, others(): lax.ppermute(rows, 'sensor', [(i, (i + step * group) % n_sensor) for i in...  4.67 us
    all_to_all x1, starting transfers between devices, swap(): lax.all_to_all(rows, 'sensor', 0, 0, tiled=True, axis_index_groups=blocks)  3.69 us
  transfers between devices with their start and end apart: 12, of which 10 were waited for; matrix products, arithmetic and copies ran while one was open for 0% of the time, Pallas kernels for 5%

profile of v3, /device:TPU:0, one launch (start us, length us, event | category | flops | bytes accessed | tf_op | source)
XLA Modules:
  0.0 73.4 jit_solution(11926565457599740453)
XLA Ops:
  0.6 0.0 copy-start
  0.6 0.0 copy-start.1
  0.7 0.0 copy-start.2
  0.7 0.0 copy-start.3
  0.7 0.0 copy-start.4
  0.7 3.1 %shard_map.135 = f32[8,256,128]{2,1,0:T(8,128)} custom-call(bf16[64,16,128]{2,1,0:T(8,128)(2,1)} %inputs_ref.1, s32[16,64]{1,0:T(8,128)} %bitcast.19, bf16[64,16,128]{2,1,0:T(8,128)(2,1)} %cotangent_ref.1), custom_call_target="tpu_custom_call" | custom-call | tf_op jit(solution)/shard_map/pallas_call | solution.py:315
  3.8 21.2 %all_to_all.10.swapped = f32[8,256,128]{2,1,0:T(8,128)S(1)} all-to-all(f32[8,256,128]{2,1,0:T(8,128)} %shard_map.135), channel_id=1, replica_groups={{0,2,4,6,8,10,12,14},{16,18,20,22,24,26,28,30},{1,3,5,7,9,11,13,15},{17..., dimensions={0} | all-to-all | bytes 2097152 | tf_op jit(solution)/shard_map/all_to_all | solution.py:334
  25.0 0.0 copy-done
  25.0 0.0 copy-done.1
  25.0 0.0 copy-done.2
  25.0 1.1 %shard_map.137.refs_0_ = f32[136,128]{1,0:T(8,128)S(1)} custom-call(f32[8,256,128]{2,1,0:T(8,128)S(1)} %all_to_all.10.swapped, f32[64,128]{1,0:T(8,128)S(1)} %copy-done, bf16[128,128]{1,0:T(8,128)(2,1)S(1)} %copy-done.1, bf16[128,128]{1,0:T(8,128)(2,1)S(1)} %copy-done.2), custom_call_target="tpu_custom_call" | custom-call | tf_op jit(solution)/shard_map/pallas_call | solution.py:315
  26.1 2.7 %collective-permute-start = (f32[136,128]{1,0:T(8,128)S(1)}, f32[136,128]{1,0:T(8,128)S(1)}, u32[]{:S(2)}, u32[]{:S(2)}) collective-permute-start(f32[136,128]{1,0:T(8,128)S(1)} %shard_map.137.refs_0_), channel_id=1, source_target_pairs={{0,16},{2,18},{4,20},{6,22},{8,24},{10,26},{12,28},{14,30},{16,0},... | collective-permute-start | bytes 208904 | tf_op jit(solution)/shard_map/ppermute | solution.py:338
  28.8 0.0 copy-done.3
  28.8 0.0 copy-done.4
  28.8 0.9 %shard_map.136 = (f32[4,1024,128]{2,1,0:T(8,128)S(1)}, f32[3,1024,128]{2,1,0:T(8,128)S(1)}) custom-call(f32[8,256,128]{2,1,0:T(8,128)S(1)} %all_to_all.10.swapped, f32[64,128]{1,0:T(8,128)S(1)} %copy-done, bf16[128,128]{1,0:T(8,128)(2,1)S(1)} %copy-done.1, bf16[128,128]{1,0:T(8,128)(2,1)S(1)} %copy-done.2, bf16[128,128]{1,0:T(8,128)(2,1)S(1)} %copy-done.3, ...), custom_call_target="tpu_custom_call" | custom-call | tf_op jit(solution)/shard_map/pallas_call | solution.py:315
  29.7 2.5 %collective-permute-done.refs_1_ = f32[136,128]{1,0:T(8,128)S(1)} collective-permute-done((f32[136,128]{1,0:T(8,128)S(1)}, f32[136,128]{1,0:T(8,128)S(1)}, u32[]{:S(2)}, u32[]{:S(2)}) %collective-permute-start) | collective-permute-done | bytes 69664 | tf_op jit(solution)/shard_map/ppermute | solution.py:338
  32.1 1.9 %shard_map.138 = (f32[128,128]{1,0:T(8,128)S(1)}, bf16[1024,128]{1,0:T(8,128)(2,1)S(1)}, f32[128,512]{1,0:T(8,128)S(1)}) custom-call(f32[3,1024,128]{2,1,0:T(8,128)S(1)} %get-tuple-element.28.ready_ref, f32[136,128]{1,0:T(8,128)S(1)} %shard_map.137.refs_0_, f32[136,128]{1,0:T(8,128)S(1)} %collective-permute-done.refs_1_), custom_call_target="tpu_custom_call" | custom-call | tf_op jit(solution)/shard_map/pallas_call | solution.py:315
  34.0 2.0 %collective-permute-start.1 = (f32[128,128]{1,0:T(8,128)S(1)}, f32[128,128]{1,0:T(8,128)S(1)}, u32[]{:S(2)}, u32[]{:S(2)}) collective-permute-start(f32[128,128]{1,0:T(8,128)S(1)} %get-tuple-element.33.refs_2_), channel_id=1, source_target_pairs={{0,16},{2,18},{4,20},{6,22},{8,24},{10,26},{12,28},{14,30},{16,0},... | collective-permute-start | bytes 196616 | tf_op jit(solution)/shard_map/ppermute | solution.py:338
  36.0 1.0 %shard_map.139 = (f32[8,128,128]{2,1,0:T(8,128)S(1)}, f32[1280,128]{1,0:T(8,128)S(1)}) custom-call(f32[8,256,128]{2,1,0:T(8,128)S(1)} %all_to_all.10.swapped, bf16[128,128]{1,0:T(8,128)(2,1)S(1)} %copy-done.3, bf16[128,128]{1,0:T(8,128)(2,1)S(1)} %copy-done.4, f32[3,1024,128]{2,1,0:T(8,128)S(1)} %get-tuple-element.28.ready_ref, ...), custom_call_target="tpu_custom_call" | custom-call | tf_op jit(solution)/shard_map/pallas_call | solution.py:315
  37.0 2.9 %collective-permute-done.1.refs_3_ = f32[128,128]{1,0:T(8,128)S(1)} collective-permute-done((f32[128,128]{1,0:T(8,128)S(1)}, f32[128,128]{1,0:T(8,128)S(1)}, u32[]{:S(2)}, u32[]{:S(2)}) %collective-permute-start.1) | collective-permute-done | bytes 65568 | tf_op jit(solution)/shard_map/ppermute | solution.py:338
  39.9 2.3 %shard_map.140 = (f32[8,256,128]{2,1,0:T(8,128)}, f32[2,288,128]{2,1,0:T(8,128)S(1)}) custom-call(f32[8,256,128]{2,1,0:T(8,128)S(1)} %all_to_all.10.swapped, f32[64,128]{1,0:T(8,128)S(1)} %copy-done, bf16[128,128]{1,0:T(8,128)(2,1)S(1)} %copy-done.1, bf16[128,128]{1,0:T(8,128)(2,1)S(1)} %copy-done.2, f32[4,1024,128]{2,1,0:T(8,128)S(1)} %get-tuple-element.27.ready_ref, ...), custom_call_target="tpu_custom_call" | custom-call | tf_op jit(solution)/shard_map/pallas_call | solution.py:315
  42.3 0.0 copy-start.5
  42.3 3.7 %all-to-all-start.1 = ((f32[8,256,128]{2,1,0:T(8,128)}), f32[8,256,128]{2,1,0:T(8,128)S(1)}, u32[]{:S(2)}, u32[]{:S(2)}) async-start(f32[8,256,128]{2,1,0:T(8,128)} %get-tuple-element.35), calls=%async_computation.1 | async-start | bytes 2097152 | tf_op jit(solution)/shard_map/all_to_all | solution.py:334
  46.0 0.1 collective-permute-start.2
  46.1 1.3 %collective-permute-done.2 = f32[288,128]{1,0:T(8,128)S(1)} collective-permute-done((f32[288,128]{1,0:T(8,128)S(1)}, f32[288,128]{1,0:T(8,128)S(1)}, u32[]{:S(2)}, u32[]{:S(2)}) %collective-permute-start.2) | collective-permute-done | bytes 147488 | tf_op jit(solution)/shard_map/ppermute | solution.py:414
  47.5 2.9 %collective-permute-start.5 = (f32[72,128]{1,0:T(8,128)S(1)}, f32[72,128]{1,0:T(8,128)S(1)}, u32[]{:S(2)}, u32[]{:S(2)}) collective-permute-start(f32[72,128]{1,0:T(8,128)S(1)} %get-tuple-element.48), channel_id=1, source_target_pairs={{0,6},{2,4},{4,2},{6,0},{8,14},{10,12},{12,10},{14,8},{16,22},{18,... | collective-permute-start | bytes 110600 | tf_op jit(solution)/shard_map/ppermute | solution.py:417
  50.4 0.5 collective-permute-start.4
  50.9 0.1 collective-permute-start.3
  51.1 6.4 %collective-permute-done.5 = f32[72,128]{1,0:T(8,128)S(1)} collective-permute-done((f32[72,128]{1,0:T(8,128)S(1)}, f32[72,128]{1,0:T(8,128)S(1)}, u32[]{:S(2)}, u32[]{:S(2)}) %collective-permute-start.5) | collective-permute-done | bytes 36896 | tf_op jit(solution)/shard_map/ppermute | solution.py:417
  57.4 0.3 collective-permute-done.4
  57.7 0.0 collective-permute-done.3
  57.7 1.2 %collective-permute-start.6 = (f32[72,128]{1,0:T(8,128)S(1)}, f32[72,128]{1,0:T(8,128)S(1)}, u32[]{:S(2)}, u32[]{:S(2)}) collective-permute-start(f32[72,128]{1,0:T(8,128)S(1)} %fusion.1), channel_id=1, source_target_pairs={{0,8},{2,10},{4,12},{6,14},{8,0},{10,2},{12,4},{14,6},{16,24},{18,... | collective-permute-start | bytes 110600 | tf_op jit(solution)/shard_map/ppermute | solution.py:417
  58.9 2.8 %collective-permute-done.6 = f32[72,128]{1,0:T(8,128)S(1)} collective-permute-done((f32[72,128]{1,0:T(8,128)S(1)}, f32[72,128]{1,0:T(8,128)S(1)}, u32[]{:S(2)}, u32[]{:S(2)}) %collective-permute-start.6) | collective-permute-done | bytes 36896 | tf_op jit(solution)/shard_map/ppermute | solution.py:417
  61.8 2.0 %collective-permute-start.7 = (f32[72,128]{1,0:T(8,128)S(1)}, f32[72,128]{1,0:T(8,128)S(1)}, u32[]{:S(2)}, u32[]{:S(2)}) collective-permute-start(f32[72,128]{1,0:T(8,128)S(1)} %add.52), channel_id=1, source_target_pairs={{0,16},{2,18},{4,20},{6,22},{8,24},{10,26},{12,28},{14,30},{16,0},... | collective-permute-start | bytes 110600 | tf_op jit(solution)/shard_map/ppermute | solution.py:417
  63.8 0.0 all-to-all-done.1.rows_ref
  63.8 0.0 copy-done.5
  63.8 1.6 %shard_map.141 = (bf16[64,16,128]{2,1,0:T(8,128)(2,1)}, bf16[64,16,128]{2,1,0:T(8,128)(2,1)}) custom-call(f32[8,256,128]{2,1,0:T(8,128)S(1)} %all-to-all-done.1.rows_ref, s32[16,64]{1,0:T(8,128)S(1)} %bitcast.20), custom_call_target="tpu_custom_call" | custom-call | tf_op jit(solution)/shard_map/pallas_call | solution.py:315
  65.4 1.3 %collective-permute-done.7 = f32[72,128]{1,0:T(8,128)S(1)} collective-permute-done((f32[72,128]{1,0:T(8,128)S(1)}, f32[72,128]{1,0:T(8,128)S(1)}, u32[]{:S(2)}, u32[]{:S(2)}) %collective-permute-start.7) | collective-permute-done | bytes 36896 | tf_op jit(solution)/shard_map/ppermute | solution.py:417
  66.6 0.6 collective-permute-start.8
  67.2 0.6 collective-permute-start.9
  67.8 2.3 %collective-permute-start.10 = (f32[72,128]{1,0:T(8,128)S(1)}, f32[72,128]{1,0:T(8,128)S(1)}, u32[]{:S(2)}, u32[]{:S(2)}) collective-permute-start(f32[72,128]{1,0:T(8,128)S(1)} %add.53.refs_0_), channel_id=1, source_target_pairs={{0,6},{2,4},{4,2},{6,0},{8,14},{10,12},{12,10},{14,8},{16,22},{18,... | collective-permute-start | bytes 110600 | tf_op jit(solution)/shard_map/ppermute | solution.py:417
  70.1 0.5 collective-permute-done.8.refs_1_
  70.6 0.6 collective-permute-done.9.refs_2_
  71.2 1.5 %collective-permute-done.10.refs_3_ = f32[72,128]{1,0:T(8,128)S(1)} collective-permute-done((f32[72,128]{1,0:T(8,128)S(1)}, f32[72,128]{1,0:T(8,128)S(1)}, u32[]{:S(2)}, u32[]{:S(2)}) %collective-permute-start.10) | collective-permute-done | bytes 36896 | tf_op jit(solution)/shard_map/ppermute | solution.py:417
  72.7 0.7 shard_map.142
  (6 shorter events, 0.1 us)
Async XLA Ops:
  0.6 24.4 %copy-start = (f32[64,128]{1,0:T(8,128)S(1)}, f32[64,128]{1,0:T(8,128)}, u32[]{:S(2)}) copy-start(f32[64,128]{1,0:T(8,128)} %projector.5) | copy-start | bytes 98308
  0.6 24.4 %copy-start.1 = (bf16[128,128]{1,0:T(8,128)(2,1)S(1)}, bf16[128,128]{1,0:T(8,128)(2,1)}, u32[]{:S(2)}) copy-start(bf16[128,128]{1,0:T(8,128)(2,1)} %wk.5) | copy-start | bytes 98308
  0.7 24.3 %copy-start.2 = (bf16[128,128]{1,0:T(8,128)(2,1)S(1)}, bf16[128,128]{1,0:T(8,128)(2,1)}, u32[]{:S(2)}) copy-start(bf16[128,128]{1,0:T(8,128)(2,1)} %wv.5) | copy-start | bytes 98308
  0.7 28.1 %copy-start.3 = (bf16[128,128]{1,0:T(8,128)(2,1)S(1)}, bf16[128,128]{1,0:T(8,128)(2,1)}, u32[]{:S(2)}) copy-start(bf16[128,128]{1,0:T(8,128)(2,1)} %wq.3) | copy-start | bytes 98308
  0.7 28.1 %copy-start.4 = (bf16[128,128]{1,0:T(8,128)(2,1)S(1)}, bf16[128,128]{1,0:T(8,128)(2,1)}, u32[]{:S(2)}) copy-start(bf16[128,128]{1,0:T(8,128)(2,1)} %wo.3) | copy-start | bytes 98308
  26.1 6.0 %collective-permute-start = (f32[136,128]{1,0:T(8,128)S(1)}, f32[136,128]{1,0:T(8,128)S(1)}, u32[]{:S(2)}, u32[]{:S(2)}) collective-permute-start(f32[136,128]{1,0:T(8,128)S(1)} %shard_map.137.refs_0_), channel_id=1, source_target_pairs={{0,16},{2,18},{4,20},{6,22},{8,24},{10,26},{12,28},{14,30},{16,0},... | collective-permute-start | bytes 208904 | tf_op jit(solution)/shard_map/ppermute | solution.py:338
  34.0 5.9 %collective-permute-start.1 = (f32[128,128]{1,0:T(8,128)S(1)}, f32[128,128]{1,0:T(8,128)S(1)}, u32[]{:S(2)}, u32[]{:S(2)}) collective-permute-start(f32[128,128]{1,0:T(8,128)S(1)} %get-tuple-element.33.refs_2_), channel_id=1, source_target_pairs={{0,16},{2,18},{4,20},{6,22},{8,24},{10,26},{12,28},{14,30},{16,0},... | collective-permute-start | bytes 196616 | tf_op jit(solution)/shard_map/ppermute | solution.py:338
  42.3 21.5 %copy-start.5 = (s32[64,16]{0,1:T(8,128)S(1)}, s32[64,16]{0,1:T(8,128)}, u32[]{:S(2)}) copy-start(s32[64,16]{0,1:T(8,128)} %param.9) | copy-start | bytes 12292
  42.3 21.5 %all-to-all-start.1 = ((f32[8,256,128]{2,1,0:T(8,128)}), f32[8,256,128]{2,1,0:T(8,128)S(1)}, u32[]{:S(2)}, u32[]{:S(2)}) async-start(f32[8,256,128]{2,1,0:T(8,128)} %get-tuple-element.35), calls=%async_computation.1 | async-start | bytes 2097152 | tf_op jit(solution)/shard_map/all_to_all | solution.py:334
  46.0 1.4 %collective-permute-start.2 = (f32[288,128]{1,0:T(8,128)S(1)}, f32[288,128]{1,0:T(8,128)S(1)}, u32[]{:S(2)}, u32[]{:S(2)}) collective-permute-start(f32[288,128]{1,0:T(8,128)S(1)} %dynamic-slice_bitcast_fusion), channel_id=1, source_target_pairs={{0,1},{1,0},{2,3},{3,2},{4,5},{5,4},{6,7},{7,6},{8,9},{9,8},{10,11... | collective-permute-start | bytes 442376 | tf_op jit(solution)/shard_map/ppermute | solution.py:414
  47.5 9.9 %collective-permute-start.5 = (f32[72,128]{1,0:T(8,128)S(1)}, f32[72,128]{1,0:T(8,128)S(1)}, u32[]{:S(2)}, u32[]{:S(2)}) collective-permute-start(f32[72,128]{1,0:T(8,128)S(1)} %get-tuple-element.48), channel_id=1, source_target_pairs={{0,6},{2,4},{4,2},{6,0},{8,14},{10,12},{12,10},{14,8},{16,22},{18,... | collective-permute-start | bytes 110600 | tf_op jit(solution)/shard_map/ppermute | solution.py:417
  50.4 7.3 %collective-permute-start.4 = (f32[72,128]{1,0:T(8,128)S(1)}, f32[72,128]{1,0:T(8,128)S(1)}, u32[]{:S(2)}, u32[]{:S(2)}) collective-permute-start(f32[72,128]{1,0:T(8,128)S(1)} %get-tuple-element.49), channel_id=1, source_target_pairs={{0,4},{2,6},{4,0},{6,2},{8,12},{10,14},{12,8},{14,10},{16,20},{18,... | collective-permute-start | bytes 110600 | tf_op jit(solution)/shard_map/ppermute | solution.py:417
  50.9 6.8 %collective-permute-start.3 = (f32[72,128]{1,0:T(8,128)S(1)}, f32[72,128]{1,0:T(8,128)S(1)}, u32[]{:S(2)}, u32[]{:S(2)}) collective-permute-start(f32[72,128]{1,0:T(8,128)S(1)} %get-tuple-element.47), channel_id=1, source_target_pairs={{0,2},{2,0},{4,6},{6,4},{8,10},{10,8},{12,14},{14,12},{16,18},{18,... | collective-permute-start | bytes 110600 | tf_op jit(solution)/shard_map/ppermute | solution.py:417
  57.7 4.0 %collective-permute-start.6 = (f32[72,128]{1,0:T(8,128)S(1)}, f32[72,128]{1,0:T(8,128)S(1)}, u32[]{:S(2)}, u32[]{:S(2)}) collective-permute-start(f32[72,128]{1,0:T(8,128)S(1)} %fusion.1), channel_id=1, source_target_pairs={{0,8},{2,10},{4,12},{6,14},{8,0},{10,2},{12,4},{14,6},{16,24},{18,... | collective-permute-start | bytes 110600 | tf_op jit(solution)/shard_map/ppermute | solution.py:417
  61.8 4.9 %collective-permute-start.7 = (f32[72,128]{1,0:T(8,128)S(1)}, f32[72,128]{1,0:T(8,128)S(1)}, u32[]{:S(2)}, u32[]{:S(2)}) collective-permute-start(f32[72,128]{1,0:T(8,128)S(1)} %add.52), channel_id=1, source_target_pairs={{0,16},{2,18},{4,20},{6,22},{8,24},{10,26},{12,28},{14,30},{16,0},... | collective-permute-start | bytes 110600 | tf_op jit(solution)/shard_map/ppermute | solution.py:417
  66.6 4.0 %collective-permute-start.8 = (f32[72,128]{1,0:T(8,128)S(1)}, f32[72,128]{1,0:T(8,128)S(1)}, u32[]{:S(2)}, u32[]{:S(2)}) collective-permute-start(f32[72,128]{1,0:T(8,128)S(1)} %add.53.refs_0_), channel_id=1, source_target_pairs={{0,2},{2,0},{4,6},{6,4},{8,10},{10,8},{12,14},{14,12},{16,18},{18,... | collective-permute-start | bytes 110600 | tf_op jit(solution)/shard_map/ppermute | solution.py:417
  67.2 4.0 %collective-permute-start.9 = (f32[72,128]{1,0:T(8,128)S(1)}, f32[72,128]{1,0:T(8,128)S(1)}, u32[]{:S(2)}, u32[]{:S(2)}) collective-permute-start(f32[72,128]{1,0:T(8,128)S(1)} %add.53.refs_0_), channel_id=1, source_target_pairs={{0,4},{2,6},{4,0},{6,2},{8,12},{10,14},{12,8},{14,10},{16,20},{18,... | collective-permute-start | bytes 110600 | tf_op jit(solution)/shard_map/ppermute | solution.py:417
  67.8 4.9 %collective-permute-start.10 = (f32[72,128]{1,0:T(8,128)S(1)}, f32[72,128]{1,0:T(8,128)S(1)}, u32[]{:S(2)}, u32[]{:S(2)}) collective-permute-start(f32[72,128]{1,0:T(8,128)S(1)} %add.53.refs_0_), channel_id=1, source_target_pairs={{0,6},{2,4},{4,2},{6,0},{8,14},{10,12},{12,10},{14,8},{16,22},{18,... | collective-permute-start | bytes 110600 | tf_op jit(solution)/shard_map/ppermute | solution.py:417

commit v4 on v3

--- a/solution.py
+++ b/solution.py
@@ -25,6 +25,21 @@
 
 def rounded_dot(left, right, left_dim, right_dim):
     return dot(left.astype(bf16), right.astype(bf16), left_dim, right_dim)
+
+
+def split(value):
+    high = value.astype(bf16)
+    return high, (value - high.astype(f32)).astype(bf16)
+
+
+def close_dot(left, right, left_dim, right_dim):
+    high, low = split(left)
+    right_high, right_low = split(right)
+    return (
+        dot(high, right_high, left_dim, right_dim)
+        + dot(high, right_low, left_dim, right_dim)
+        + dot(low, right_high, left_dim, right_dim)
+    )
 
 
 def inverse_norm(vector):
@@ -118,7 +133,7 @@
     unit = key_raw * inverse
     mapping = projector * inverse_norm(projector)
     scale = scale_of(key_raw.shape[-1])
-    return inverse, unit, jnp.exp(scale * rounded_dot(mapping, unit, 1, 1))
+    return inverse, unit, jnp.exp(scale * close_dot(mapping, unit, 1, 1))
 
 
 def in_kernel(share, sensors, swapped, projector, wk, wv, sums_ref):
@@ -127,14 +142,15 @@
     tail = share * tokens
     sums_ref[tail:, :] = jnp.zeros((sums_ref.shape[0] - tail, width), f32)
     both_weights = jnp.concatenate([wk[...], wv[...]], axis=1)
-    for t in range(share):
-        hidden = rows_of(swapped, t, sensors).astype(bf16)
-        both = dot(hidden, both_weights, 1, 0)
-        _, _, weights = weigh_in(both[:, :width], projector[...])
-        sums_ref[t * tokens : (t + 1) * tokens, :] = rounded_dot(weights, both[:, width:], 1, 0)
-        den = jnp.sum(weights, axis=1, keepdims=True)
+    steps = range(share)
+    both = [dot(rows_of(swapped, t, sensors).astype(bf16), both_weights, 1, 0) for t in steps]
+    weights = [weigh_in(raw[:, :width], projector[...])[2] for raw in both]
+    dens = [jnp.sum(weight, axis=1, keepdims=True) for weight in weights]
+    nums = [rounded_dot(weights[t], both[t][:, width:], 1, 0) for t in steps]
+    for t in steps:
+        sums_ref[t * tokens : (t + 1) * tokens, :] = nums[t]
         sums_ref[tail + t : tail + t + 1, :tokens] = jnp.sum(
-            jnp.where(same, den, 0.0), axis=0, keepdims=True
+            jnp.where(same, dens[t], 0.0), axis=0, keepdims=True
         )
 
 
@@ -187,30 +203,38 @@
     scale = scale_of(width)
     total = total_of(sums)
     n_rows = ready_ref.shape[1] // share
-    for t in range(share):
-        at = slice(t * n_rows, (t + 1) * n_rows)
+    steps = range(share)
+    units = [ready_ref[0, t * n_rows : (t + 1) * n_rows, :] for t in steps]
+    summaries = []
+    for t in steps:
+        num, den = num_den(total, t, share, tokens)
+        summaries.append(num / den)
+    inverses = [inverse_norm(summary) for summary in summaries]
+    pooled = [summary * inverse for summary, inverse in zip(summaries, inverses)]
+    weights = [jnp.exp(scale * close_dot(pooled[t], units[t], 1, 1)) for t in steps]
+    attention = [weight / jnp.sum(weight, axis=0, keepdims=True) for weight in weights]
+    blended = [rounded_dot(attention[t], summaries[t], 0, 0) for t in steps]
+    blended_inverses = [inverse_norm(each) for each in blended]
+    normed = [each * inverse for each, inverse in zip(blended, blended_inverses)]
+    d_blended = [
+        normalize_back(
+            blended_inverses[t], normed[t], ready_ref[2, t * n_rows : (t + 1) * n_rows, :]
+        )
+        for t in steps
+    ]
+    d_attention = [close_dot(summaries[t], d_blended[t], 1, 1) for t in steps]
+    d_scores = [
+        attention[t]
+        * (d_attention[t] - jnp.sum(attention[t] * d_attention[t], axis=0, keepdims=True))
+        for t in steps
+    ]
+    d_pooled = [scale * rounded_dot(d_scores[t], units[t], 1, 0) for t in steps]
+    direct = [close_dot(attention[t], d_blended[t], 1, 0) for t in steps]
+    for t in steps:
         own = slice(t * tokens, (t + 1) * tokens)
-        unit = ready_ref[0, at, :]
-        num, den = num_den(total, t, share, tokens)
-        summary = num / den
-        pooled_inverse = inverse_norm(summary)
-        pooled = summary * pooled_inverse
-        weights = jnp.exp(scale * rounded_dot(pooled, unit, 1, 1))
-        attention = weights / jnp.sum(weights, axis=0, keepdims=True)
-        blended = rounded_dot(attention, summary, 0, 0)
-        blended_inverse = inverse_norm(blended)
-        normed = blended * blended_inverse
-        normed_ref[at, :] = normed.astype(bf16)
-        d_blended = normalize_back(blended_inverse, normed, ready_ref[2, at, :])
-        d_attention = rounded_dot(summary, d_blended, 1, 1)
-        d_scores = attention * (
-            d_attention - jnp.sum(attention * d_attention, axis=0, keepdims=True)
-        )
-        d_pooled = scale * rounded_dot(d_scores, unit, 1, 0)
-        ds_ref[own, :] = rounded_dot(attention, d_blended, 1, 0) + normalize_back(
-            pooled_inverse, pooled, d_pooled
-        )
-        d_scores_ref[own, :] = d_scores
+        ds_ref[own, :] = direct[t] + normalize_back(inverses[t], pooled[t], d_pooled[t])
+        d_scores_ref[own, :] = d_scores[t]
+        normed_ref[t * n_rows : (t + 1) * n_rows, :] = normed[t].astype(bf16)
 
 
 def query_kernel(share, sensors, terms, swapped, wq, wo, ready_ref, normed_ref, d_scores_ref, *refs):
@@ -232,7 +256,7 @@
         num, den = num_den(total, t, share, tokens)
         summary = num / den
         pooled = summary * inverse_norm(summary)
-        d_unit = scale * rounded_dot(d_scores_ref[t * tokens : (t + 1) * tokens, :], pooled, 0, 0)
+        d_unit = scale * close_dot(d_scores_ref[t * tokens : (t + 1) * tokens, :], pooled, 0, 0)
         d_query = normalize_back(ready_ref[1, at, :], ready_ref[0, at, :], d_unit).astype(bf16)
         grad_query = dot(rows.astype(bf16), d_query, 0, 0)
         dh_ref[at, :] = cotangent + dot(d_query, wq[...], 1, 1)
@@ -257,8 +281,10 @@
     share, sensors, terms, swapped, projector, wk, wv, ready_ref, dh_ref, layer_ref, *refs
 ):
     sums, d_sums = refs[:terms], refs[terms : 2 * terms]
-    out_ref, part_ref = refs[2 * terms :]
-    out_ref[:, : share * sensors, :] = layer_ref[...]
+    far_ref, part_ref, out_ref, sems = refs[2 * terms :]
+    half = share * sensors
+    sent = [pltpu.make_async_copy(layer_ref, far_ref.at[:, pl.ds(0, half)], sems.at[share])]
+    sent[0].start()
     tokens, width = projector.shape
     scale = scale_of(width)
     total = total_of(sums)
@@ -266,38 +292,57 @@
     mapping_inverse = inverse_norm(projector[...])
     mapping = projector[...] * mapping_inverse
     turned = jnp.concatenate([wk[...], wv[...]], axis=1)
-    gradients = None
     n_rows = ready_ref.shape[1] // share
     grad_rows = share * n_rows
-    for t in range(share):
-        at = slice(t * n_rows, (t + 1) * n_rows)
-        own = slice(t * tokens, (t + 1) * tokens)
-        hidden = rows_of(swapped, t, sensors).astype(bf16)
-        unit = ready_ref[0, at, :]
-        weights = jnp.concatenate(
+    steps = range(share)
+    spans = [slice(t * n_rows, (t + 1) * n_rows) for t in steps]
+    hidden = [rows_of(swapped, t, sensors).astype(bf16) for t in steps]
+    units = [ready_ref[0, span, :] for span in spans]
+    weights = [
+        jnp.concatenate(
             [
                 ready_ref[3, t * n_rows + i * tokens : t * n_rows + (i + 1) * tokens, :]
                 for i in range(n_rows // width)
             ],
             axis=1,
         )
+        for t in steps
+    ]
+    d_nums, d_dens = [], []
+    for t in steps:
         num, den = num_den(total, t, share, tokens)
-        d_summary = d_total[own, :]
-        d_num = d_summary / den
-        d_den = -jnp.sum(d_summary * num, axis=1, keepdims=True) / (den * den)
-        d_scores = (rounded_dot(d_num, ready_ref[2, at, :], 1, 1) + d_den) * weights
-        d_unit = scale * rounded_dot(d_scores, mapping, 0, 0)
-        d_mapping = scale * rounded_dot(d_scores, unit, 1, 0)
-        d_key = normalize_back(ready_ref[1, at, :], unit, d_unit).astype(bf16)
-        d_values = rounded_dot(weights, d_num, 0, 0).astype(bf16)
-        together = jnp.concatenate([d_key, d_values], axis=1)
-        d_hidden = dh_ref[at, :] + dot(together, turned, 1, 1)
-        put_rows(out_ref, share + t, sensors, d_hidden)
-        more = (normalize_back(mapping_inverse, mapping, d_mapping), dot(hidden, together, 0, 0))
-        gradients = more if t == 0 else tuple(a + b for a, b in zip(gradients, more))
-    parts = [gradients[0], gradients[1][:, :width], gradients[1][:, width:]]
+        d_summary = d_total[t * tokens : (t + 1) * tokens, :]
+        d_nums.append(d_summary / den)
+        d_dens.append(-jnp.sum(d_summary * num, axis=1, keepdims=True) / (den * den))
+    d_weights = []
+    for t in steps:
+        high, low = split(d_nums[t])
+        values = ready_ref[2, spans[t], :].astype(bf16)
+        d_weights.append(dot(high, values, 1, 1) + dot(low, values, 1, 1) + d_dens[t])
+    d_scores = [d_weights[t] * weights[t] for t in steps]
+    d_units = [scale * rounded_dot(d_scores[t], mapping, 0, 0) for t in steps]
+    d_values = [rounded_dot(weights[t], d_nums[t], 0, 0).astype(bf16) for t in steps]
+    d_keys = [
+        normalize_back(ready_ref[1, spans[t], :], units[t], d_units[t]).astype(bf16) for t in steps
+    ]
+    together = [jnp.concatenate([d_keys[t], d_values[t]], axis=1) for t in steps]
+    for t in steps:
+        put_rows(out_ref, t, sensors, dh_ref[spans[t], :] + dot(together[t], turned, 1, 1))
+        copy = pltpu.make_async_copy(
+            out_ref.at[:, pl.ds(t * sensors, sensors)],
+            far_ref.at[:, pl.ds(half + t * sensors, sensors)],
+            sems.at[t],
+        )
+        copy.start()
+        sent.append(copy)
+    d_mapping = sum(scale * rounded_dot(d_scores[t], units[t], 1, 0) for t in steps)
+    gradients = sum(dot(hidden[t], together[t], 0, 0) for t in steps)
+    parts = [normalize_back(mapping_inverse, mapping, d_mapping)]
+    parts += [gradients[:, :width], gradients[:, width:]]
     parts += [dh_ref[grad_rows + i * width : grad_rows + (i + 1) * width, :] for i in range(2)]
     put_partials(part_ref, parts)
+    for copy in sent:
+        copy.wait()
 
 
 def deal_kernel(count, place_ref, *refs):
@@ -405,6 +450,11 @@
             shape(n_tm, quarter * chunk, width),
         ),
         swapped, projector, w_key, w_value, ready_in, d_hidden, layer, *sums, *d_sums,
+        out_specs=(far_spec, near_spec),
+        scratch_shapes=[
+            pltpu.VMEM((group, share * sensors, width), f32),
+            pltpu.SemaphoreType.DMA((share + 1,)),
+        ],
     )
     me = lax.axis_index("tm")
     mine = lax.dynamic_index_in_dim(part, me, 0, keepdims=False)

time: 73.7 us -> 72.5 us (0.984)
  Pallas kernels: 12.5 us -> 11.5 us
    pallas_call x8, Pallas kernels: 12.5 us -> 11.5 us  [call(): pl.pallas_call(kernel, out_shape=out_shape, compiler_params=params(vmem),...]
where the time goes in v4:
time: 72.5 us; the launch traced here: 72.1 us
  blocking collectives  21.2 us (29%)
  waiting for transfers between devices  19.9 us (27%)
  starting transfers between devices  18.5 us (26%)
  Pallas kernels  11.5 us (16%)
  between operations  0.81 us (1%)
    all_to_all x1, blocking collectives, swap(): lax.all_to_all(rows, 'sensor', 0, 0, tiled=True, axis_index_groups=blocks)  21.2 us
    ppermute x8, waiting for transfers between devices, partner(): return lax.ppermute(rows, 'sensor', [(i, i ^ m) for i in range(n_sensor)])  13.3 us
    pallas_call x8, Pallas kernels, call(): pl.pallas_call(kernel, out_shape=out_shape, compiler_params=params(vmem),...  11.5 us
    ppermute x8, starting transfers between devices, partner(): return lax.ppermute(rows, 'sensor', [(i, i ^ m) for i in range(n_sensor)])  10.2 us
    ppermute x2, waiting for transfers between devices, others(): lax.ppermute(rows, 'sensor', [(i, (i + step * group) % n_sensor) for i in...  5.21 us
    ppermute x2, starting transfers between devices, others(): lax.ppermute(rows, 'sensor', [(i, (i + step * group) % n_sensor) for i in...  4.66 us
    all_to_all x1, starting transfers between devices, swap(): lax.all_to_all(rows, 'sensor', 0, 0, tiled=True, axis_index_groups=blocks)  3.57 us
  transfers between devices with their start and end apart: 12, of which 10 were waited for; matrix products, arithmetic and copies ran while one was open for 0% of the time, Pallas kernels for 5%

profile of v4, /device:TPU:0, one launch (start us, length us, event | category | flops | bytes accessed | tf_op | source)
XLA Modules:
  0.0 72.1 jit_solution(5574038962576886878)
XLA Ops:
  0.6 0.0 copy-start
  0.6 0.0 copy-start.1
  0.7 0.0 copy-start.2
  0.7 0.0 copy-start.3
  0.7 0.0 copy-start.4
  0.7 3.1 %shard_map.135 = f32[8,256,128]{2,1,0:T(8,128)} custom-call(bf16[64,16,128]{2,1,0:T(8,128)(2,1)} %inputs_ref.1, s32[16,64]{1,0:T(8,128)} %bitcast.19, bf16[64,16,128]{2,1,0:T(8,128)(2,1)} %cotangent_ref.1), custom_call_target="tpu_custom_call" | custom-call | tf_op jit(solution)/shard_map/pallas_call | solution.py:360
  3.8 21.2 %all_to_all.10.swapped = f32[8,256,128]{2,1,0:T(8,128)S(1)} all-to-all(f32[8,256,128]{2,1,0:T(8,128)} %shard_map.135), channel_id=1, replica_groups={{0,2,4,6,8,10,12,14},{16,18,20,22,24,26,28,30},{1,3,5,7,9,11,13,15},{17..., dimensions={0} | all-to-all | bytes 2097152 | tf_op jit(solution)/shard_map/all_to_all | solution.py:379
  25.0 0.0 copy-done
  25.0 0.0 copy-done.1
  25.0 0.0 copy-done.2
  25.0 0.9 %shard_map.137.refs_0_ = f32[136,128]{1,0:T(8,128)S(1)} custom-call(f32[8,256,128]{2,1,0:T(8,128)S(1)} %all_to_all.10.swapped, f32[64,128]{1,0:T(8,128)S(1)} %copy-done, bf16[128,128]{1,0:T(8,128)(2,1)S(1)} %copy-done.1, bf16[128,128]{1,0:T(8,128)(2,1)S(1)} %copy-done.2), custom_call_target="tpu_custom_call" | custom-call | tf_op jit(solution)/shard_map/pallas_call | solution.py:360
  25.9 2.6 %collective-permute-start = (f32[136,128]{1,0:T(8,128)S(1)}, f32[136,128]{1,0:T(8,128)S(1)}, u32[]{:S(2)}, u32[]{:S(2)}) collective-permute-start(f32[136,128]{1,0:T(8,128)S(1)} %shard_map.137.refs_0_), channel_id=1, source_target_pairs={{0,16},{2,18},{4,20},{6,22},{8,24},{10,26},{12,28},{14,30},{16,0},... | collective-permute-start | bytes 208904 | tf_op jit(solution)/shard_map/ppermute | solution.py:383
  28.5 0.0 copy-done.3
  28.5 0.0 copy-done.4
  28.5 0.9 %shard_map.136 = (f32[4,1024,128]{2,1,0:T(8,128)S(1)}, f32[3,1024,128]{2,1,0:T(8,128)S(1)}) custom-call(f32[8,256,128]{2,1,0:T(8,128)S(1)} %all_to_all.10.swapped, f32[64,128]{1,0:T(8,128)S(1)} %copy-done, bf16[128,128]{1,0:T(8,128)(2,1)S(1)} %copy-done.1, bf16[128,128]{1,0:T(8,128)(2,1)S(1)} %copy-done.2, bf16[128,128]{1,0:T(8,128)(2,1)S(1)} %copy-done.3, ...), custom_call_target="tpu_custom_call" | custom-call | tf_op jit(solution)/shard_map/pallas_call | solution.py:360
  29.4 2.5 %collective-permute-done.refs_1_ = f32[136,128]{1,0:T(8,128)S(1)} collective-permute-done((f32[136,128]{1,0:T(8,128)S(1)}, f32[136,128]{1,0:T(8,128)S(1)}, u32[]{:S(2)}, u32[]{:S(2)}) %collective-permute-start) | collective-permute-done | bytes 69664 | tf_op jit(solution)/shard_map/ppermute | solution.py:383
  31.9 1.6 %shard_map.138 = (f32[128,128]{1,0:T(8,128)S(1)}, bf16[1024,128]{1,0:T(8,128)(2,1)S(1)}, f32[128,512]{1,0:T(8,128)S(1)}) custom-call(f32[3,1024,128]{2,1,0:T(8,128)S(1)} %get-tuple-element.28.ready_ref, f32[136,128]{1,0:T(8,128)S(1)} %shard_map.137.refs_0_, f32[136,128]{1,0:T(8,128)S(1)} %collective-permute-done.refs_1_), custom_call_target="tpu_custom_call" | custom-call | tf_op jit(solution)/shard_map/pallas_call | solution.py:360
  33.5 2.0 %collective-permute-start.1 = (f32[128,128]{1,0:T(8,128)S(1)}, f32[128,128]{1,0:T(8,128)S(1)}, u32[]{:S(2)}, u32[]{:S(2)}) collective-permute-start(f32[128,128]{1,0:T(8,128)S(1)} %get-tuple-element.33.refs_2_), channel_id=1, source_target_pairs={{0,16},{2,18},{4,20},{6,22},{8,24},{10,26},{12,28},{14,30},{16,0},... | collective-permute-start | bytes 196616 | tf_op jit(solution)/shard_map/ppermute | solution.py:383
  35.5 1.2 %shard_map.139 = (f32[8,128,128]{2,1,0:T(8,128)S(1)}, f32[1280,128]{1,0:T(8,128)S(1)}) custom-call(f32[8,256,128]{2,1,0:T(8,128)S(1)} %all_to_all.10.swapped, bf16[128,128]{1,0:T(8,128)(2,1)S(1)} %copy-done.3, bf16[128,128]{1,0:T(8,128)(2,1)S(1)} %copy-done.4, f32[3,1024,128]{2,1,0:T(8,128)S(1)} %get-tuple-element.28.ready_ref, ...), custom_call_target="tpu_custom_call" | custom-call | tf_op jit(solution)/shard_map/pallas_call | solution.py:360
  36.7 2.8 %collective-permute-done.1.refs_3_ = f32[128,128]{1,0:T(8,128)S(1)} collective-permute-done((f32[128,128]{1,0:T(8,128)S(1)}, f32[128,128]{1,0:T(8,128)S(1)}, u32[]{:S(2)}, u32[]{:S(2)}) %collective-permute-start.1) | collective-permute-done | bytes 65568 | tf_op jit(solution)/shard_map/ppermute | solution.py:383
  39.4 1.7 %shard_map.140 = (f32[8,256,128]{2,1,0:T(8,128)}, f32[2,288,128]{2,1,0:T(8,128)S(1)}) custom-call(f32[8,256,128]{2,1,0:T(8,128)S(1)} %all_to_all.10.swapped, f32[64,128]{1,0:T(8,128)S(1)} %copy-done, bf16[128,128]{1,0:T(8,128)(2,1)S(1)} %copy-done.1, bf16[128,128]{1,0:T(8,128)(2,1)S(1)} %copy-done.2, f32[4,1024,128]{2,1,0:T(8,128)S(1)} %get-tuple-element.27.ready_ref, ...), custom_call_target="tpu_custom_call" | custom-call | tf_op jit(solution)/shard_map/pallas_call | solution.py:360
  41.1 0.0 copy-start.5
  41.2 3.6 %all-to-all-start.1 = ((f32[8,256,128]{2,1,0:T(8,128)}), f32[8,256,128]{2,1,0:T(8,128)S(1)}, u32[]{:S(2)}, u32[]{:S(2)}) async-start(f32[8,256,128]{2,1,0:T(8,128)} %get-tuple-element.35), calls=%async_computation.1 | async-start | bytes 2097152 | tf_op jit(solution)/shard_map/all_to_all | solution.py:379
  44.8 0.1 collective-permute-start.2
  44.9 1.3 %collective-permute-done.2 = f32[288,128]{1,0:T(8,128)S(1)} collective-permute-done((f32[288,128]{1,0:T(8,128)S(1)}, f32[288,128]{1,0:T(8,128)S(1)}, u32[]{:S(2)}, u32[]{:S(2)}) %collective-permute-start.2) | collective-permute-done | bytes 147488 | tf_op jit(solution)/shard_map/ppermute | solution.py:464
  46.3 2.9 %collective-permute-start.5 = (f32[72,128]{1,0:T(8,128)S(1)}, f32[72,128]{1,0:T(8,128)S(1)}, u32[]{:S(2)}, u32[]{:S(2)}) collective-permute-start(f32[72,128]{1,0:T(8,128)S(1)} %get-tuple-element.48), channel_id=1, source_target_pairs={{0,6},{2,4},{4,2},{6,0},{8,14},{10,12},{12,10},{14,8},{16,22},{18,... | collective-permute-start | bytes 110600 | tf_op jit(solution)/shard_map/ppermute | solution.py:467
  49.1 0.5 collective-permute-start.4
  49.7 0.1 collective-permute-start.3
  49.8 6.4 %collective-permute-done.5 = f32[72,128]{1,0:T(8,128)S(1)} collective-permute-done((f32[72,128]{1,0:T(8,128)S(1)}, f32[72,128]{1,0:T(8,128)S(1)}, u32[]{:S(2)}, u32[]{:S(2)}) %collective-permute-start.5) | collective-permute-done | bytes 36896 | tf_op jit(solution)/shard_map/ppermute | solution.py:467
  56.2 0.3 collective-permute-done.4
  56.5 0.0 collective-permute-done.3
  56.5 1.2 %collective-permute-start.6 = (f32[72,128]{1,0:T(8,128)S(1)}, f32[72,128]{1,0:T(8,128)S(1)}, u32[]{:S(2)}, u32[]{:S(2)}) collective-permute-start(f32[72,128]{1,0:T(8,128)S(1)} %fusion.1), channel_id=1, source_target_pairs={{0,8},{2,10},{4,12},{6,14},{8,0},{10,2},{12,4},{14,6},{16,24},{18,... | collective-permute-start | bytes 110600 | tf_op jit(solution)/shard_map/ppermute | solution.py:467
  57.7 2.8 %collective-permute-done.6 = f32[72,128]{1,0:T(8,128)S(1)} collective-permute-done((f32[72,128]{1,0:T(8,128)S(1)}, f32[72,128]{1,0:T(8,128)S(1)}, u32[]{:S(2)}, u32[]{:S(2)}) %collective-permute-start.6) | collective-permute-done | bytes 36896 | tf_op jit(solution)/shard_map/ppermute | solution.py:467
  60.5 2.0 %collective-permute-start.7 = (f32[72,128]{1,0:T(8,128)S(1)}, f32[72,128]{1,0:T(8,128)S(1)}, u32[]{:S(2)}, u32[]{:S(2)}) collective-permute-start(f32[72,128]{1,0:T(8,128)S(1)} %add.52), channel_id=1, source_target_pairs={{0,16},{2,18},{4,20},{6,22},{8,24},{10,26},{12,28},{14,30},{16,0},... | collective-permute-start | bytes 110600 | tf_op jit(solution)/shard_map/ppermute | solution.py:467
  62.5 0.0 all-to-all-done.1.rows_ref
  62.5 0.0 copy-done.5
  62.5 1.6 %shard_map.141 = (bf16[64,16,128]{2,1,0:T(8,128)(2,1)}, bf16[64,16,128]{2,1,0:T(8,128)(2,1)}) custom-call(f32[8,256,128]{2,1,0:T(8,128)S(1)} %all-to-all-done.1.rows_ref, s32[16,64]{1,0:T(8,128)S(1)} %bitcast.20), custom_call_target="tpu_custom_call" | custom-call | tf_op jit(solution)/shard_map/pallas_call | solution.py:360
  64.1 1.3 %collective-permute-done.7 = f32[72,128]{1,0:T(8,128)S(1)} collective-permute-done((f32[72,128]{1,0:T(8,128)S(1)}, f32[72,128]{1,0:T(8,128)S(1)}, u32[]{:S(2)}, u32[]{:S(2)}) %collective-permute-start.7) | collective-permute-done | bytes 36896 | tf_op jit(solution)/shard_map/ppermute | solution.py:467
  65.4 0.6 collective-permute-start.8
  66.0 0.6 collective-permute-start.9
  66.6 2.3 %collective-permute-start.10 = (f32[72,128]{1,0:T(8,128)S(1)}, f32[72,128]{1,0:T(8,128)S(1)}, u32[]{:S(2)}, u32[]{:S(2)}) collective-permute-start(f32[72,128]{1,0:T(8,128)S(1)} %add.53.refs_0_), channel_id=1, source_target_pairs={{0,6},{2,4},{4,2},{6,0},{8,14},{10,12},{12,10},{14,8},{16,22},{18,... | collective-permute-start | bytes 110600 | tf_op jit(solution)/shard_map/ppermute | solution.py:467
  68.9 0.5 collective-permute-done.8.refs_1_
  69.3 0.6 collective-permute-done.9.refs_2_
  69.9 1.5 %collective-permute-done.10.refs_3_ = f32[72,128]{1,0:T(8,128)S(1)} collective-permute-done((f32[72,128]{1,0:T(8,128)S(1)}, f32[72,128]{1,0:T(8,128)S(1)}, u32[]{:S(2)}, u32[]{:S(2)}) %collective-permute-start.10) | collective-permute-done | bytes 36896 | tf_op jit(solution)/shard_map/ppermute | solution.py:467
  71.4 0.7 shard_map.142
  (6 shorter events, 0.1 us)
Async XLA Ops:
  0.6 24.4 %copy-start = (f32[64,128]{1,0:T(8,128)S(1)}, f32[64,128]{1,0:T(8,128)}, u32[]{:S(2)}) copy-start(f32[64,128]{1,0:T(8,128)} %projector.5) | copy-start | bytes 98308
  0.6 24.4 %copy-start.1 = (bf16[128,128]{1,0:T(8,128)(2,1)S(1)}, bf16[128,128]{1,0:T(8,128)(2,1)}, u32[]{:S(2)}) copy-start(bf16[128,128]{1,0:T(8,128)(2,1)} %wk.5) | copy-start | bytes 98308
  0.7 24.3 %copy-start.2 = (bf16[128,128]{1,0:T(8,128)(2,1)S(1)}, bf16[128,128]{1,0:T(8,128)(2,1)}, u32[]{:S(2)}) copy-start(bf16[128,128]{1,0:T(8,128)(2,1)} %wv.5) | copy-start | bytes 98308
  0.7 27.9 %copy-start.3 = (bf16[128,128]{1,0:T(8,128)(2,1)S(1)}, bf16[128,128]{1,0:T(8,128)(2,1)}, u32[]{:S(2)}) copy-start(bf16[128,128]{1,0:T(8,128)(2,1)} %wq.3) | copy-start | bytes 98308
  0.7 27.9 %copy-start.4 = (bf16[128,128]{1,0:T(8,128)(2,1)S(1)}, bf16[128,128]{1,0:T(8,128)(2,1)}, u32[]{:S(2)}) copy-start(bf16[128,128]{1,0:T(8,128)(2,1)} %wo.3) | copy-start | bytes 98308
  25.9 6.0 %collective-permute-start = (f32[136,128]{1,0:T(8,128)S(1)}, f32[136,128]{1,0:T(8,128)S(1)}, u32[]{:S(2)}, u32[]{:S(2)}) collective-permute-start(f32[136,128]{1,0:T(8,128)S(1)} %shard_map.137.refs_0_), channel_id=1, source_target_pairs={{0,16},{2,18},{4,20},{6,22},{8,24},{10,26},{12,28},{14,30},{16,0},... | collective-permute-start | bytes 208904 | tf_op jit(solution)/shard_map/ppermute | solution.py:383
  33.5 5.9 %collective-permute-start.1 = (f32[128,128]{1,0:T(8,128)S(1)}, f32[128,128]{1,0:T(8,128)S(1)}, u32[]{:S(2)}, u32[]{:S(2)}) collective-permute-start(f32[128,128]{1,0:T(8,128)S(1)} %get-tuple-element.33.refs_2_), channel_id=1, source_target_pairs={{0,16},{2,18},{4,20},{6,22},{8,24},{10,26},{12,28},{14,30},{16,0},... | collective-permute-start | bytes 196616 | tf_op jit(solution)/shard_map/ppermute | solution.py:383
  41.1 21.4 %copy-start.5 = (s32[64,16]{0,1:T(8,128)S(1)}, s32[64,16]{0,1:T(8,128)}, u32[]{:S(2)}) copy-start(s32[64,16]{0,1:T(8,128)} %param.9) | copy-start | bytes 12292
  41.2 21.4 %all-to-all-start.1 = ((f32[8,256,128]{2,1,0:T(8,128)}), f32[8,256,128]{2,1,0:T(8,128)S(1)}, u32[]{:S(2)}, u32[]{:S(2)}) async-start(f32[8,256,128]{2,1,0:T(8,128)} %get-tuple-element.35), calls=%async_computation.1 | async-start | bytes 2097152 | tf_op jit(solution)/shard_map/all_to_all | solution.py:379
  44.8 1.4 %collective-permute-start.2 = (f32[288,128]{1,0:T(8,128)S(1)}, f32[288,128]{1,0:T(8,128)S(1)}, u32[]{:S(2)}, u32[]{:S(2)}) collective-permute-start(f32[288,128]{1,0:T(8,128)S(1)} %dynamic-slice_bitcast_fusion), channel_id=1, source_target_pairs={{0,1},{1,0},{2,3},{3,2},{4,5},{5,4},{6,7},{7,6},{8,9},{9,8},{10,11... | collective-permute-start | bytes 442376 | tf_op jit(solution)/shard_map/ppermute | solution.py:464
  46.3 9.9 %collective-permute-start.5 = (f32[72,128]{1,0:T(8,128)S(1)}, f32[72,128]{1,0:T(8,128)S(1)}, u32[]{:S(2)}, u32[]{:S(2)}) collective-permute-start(f32[72,128]{1,0:T(8,128)S(1)} %get-tuple-element.48), channel_id=1, source_target_pairs={{0,6},{2,4},{4,2},{6,0},{8,14},{10,12},{12,10},{14,8},{16,22},{18,... | collective-permute-start | bytes 110600 | tf_op jit(solution)/shard_map/ppermute | solution.py:467
  49.1 7.3 %collective-permute-start.4 = (f32[72,128]{1,0:T(8,128)S(1)}, f32[72,128]{1,0:T(8,128)S(1)}, u32[]{:S(2)}, u32[]{:S(2)}) collective-permute-start(f32[72,128]{1,0:T(8,128)S(1)} %get-tuple-element.49), channel_id=1, source_target_pairs={{0,4},{2,6},{4,0},{6,2},{8,12},{10,14},{12,8},{14,10},{16,20},{18,... | collective-permute-start | bytes 110600 | tf_op jit(solution)/shard_map/ppermute | solution.py:467
  49.7 6.8 %collective-permute-start.3 = (f32[72,128]{1,0:T(8,128)S(1)}, f32[72,128]{1,0:T(8,128)S(1)}, u32[]{:S(2)}, u32[]{:S(2)}) collective-permute-start(f32[72,128]{1,0:T(8,128)S(1)} %get-tuple-element.47), channel_id=1, source_target_pairs={{0,2},{2,0},{4,6},{6,4},{8,10},{10,8},{12,14},{14,12},{16,18},{18,... | collective-permute-start | bytes 110600 | tf_op jit(solution)/shard_map/ppermute | solution.py:467
  56.5 4.0 %collective-permute-start.6 = (f32[72,128]{1,0:T(8,128)S(1)}, f32[72,128]{1,0:T(8,128)S(1)}, u32[]{:S(2)}, u32[]{:S(2)}) collective-permute-start(f32[72,128]{1,0:T(8,128)S(1)} %fusion.1), channel_id=1, source_target_pairs={{0,8},{2,10},{4,12},{6,14},{8,0},{10,2},{12,4},{14,6},{16,24},{18,... | collective-permute-start | bytes 110600 | tf_op jit(solution)/shard_map/ppermute | solution.py:467
  60.5 4.9 %collective-permute-start.7 = (f32[72,128]{1,0:T(8,128)S(1)}, f32[72,128]{1,0:T(8,128)S(1)}, u32[]{:S(2)}, u32[]{:S(2)}) collective-permute-start(f32[72,128]{1,0:T(8,128)S(1)} %add.52), channel_id=1, source_target_pairs={{0,16},{2,18},{4,20},{6,22},{8,24},{10,26},{12,28},{14,30},{16,0},... | collective-permute-start | bytes 110600 | tf_op jit(solution)/shard_map/ppermute | solution.py:467
  65.4 4.0 %collective-permute-start.8 = (f32[72,128]{1,0:T(8,128)S(1)}, f32[72,128]{1,0:T(8,128)S(1)}, u32[]{:S(2)}, u32[]{:S(2)}) collective-permute-start(f32[72,128]{1,0:T(8,128)S(1)} %add.53.refs_0_), channel_id=1, source_target_pairs={{0,2},{2,0},{4,6},{6,4},{8,10},{10,8},{12,14},{14,12},{16,18},{18,... | collective-permute-start | bytes 110600 | tf_op jit(solution)/shard_map/ppermute | solution.py:467
  66.0 4.0 %collective-permute-start.9 = (f32[72,128]{1,0:T(8,128)S(1)}, f32[72,128]{1,0:T(8,128)S(1)}, u32[]{:S(2)}, u32[]{:S(2)}) collective-permute-start(f32[72,128]{1,0:T(8,128)S(1)} %add.53.refs_0_), channel_id=1, source_target_pairs={{0,4},{2,6},{4,0},{6,2},{8,12},{10,14},{12,8},{14,10},{16,20},{18,... | collective-permute-start | bytes 110600 | tf_op jit(solution)/shard_map/ppermute | solution.py:467
  66.6 4.9 %collective-permute-start.10 = (f32[72,128]{1,0:T(8,128)S(1)}, f32[72,128]{1,0:T(8,128)S(1)}, u32[]{:S(2)}, u32[]{:S(2)}) collective-permute-start(f32[72,128]{1,0:T(8,128)S(1)} %add.53.refs_0_), channel_id=1, source_target_pairs={{0,6},{2,4},{4,2},{6,0},{8,14},{10,12},{12,10},{14,8},{16,22},{18,... | collective-permute-start | bytes 110600 | tf_op jit(solution)/shard_map/ppermute | solution.py:467

commit v5 on v4

--- a/solution.py
+++ b/solution.py
@@ -60,16 +60,19 @@
     return dot(diagonal(sensors).astype(f32).astype(bf16), mask_ref[...].astype(f32).astype(bf16), 1, 1)
 
 
-def outward_kernel(inputs_ref, mask_ref, cotangent_ref, far_ref, near, near_cotangent, wide, out_ref, sems):
+def outward_kernel(
+    inputs_ref, mask_ref, cotangent_ref, far_ref, near, near_mask, near_cotangent, wide, out_ref, sems
+):
     sensors, steps, _ = inputs_ref.shape
     places = out_ref.shape[0]
     share = steps // places
     rows = share * sensors
     first = pltpu.make_async_copy(inputs_ref, near, sems.at[2 * places])
     second = pltpu.make_async_copy(cotangent_ref, near_cotangent, sems.at[2 * places + 1])
+    third = pltpu.make_async_copy(mask_ref, near_mask, sems.at[2 * places + 2])
     first.start()
+    third.start()
     second.start()
-    marks = turned_mask(mask_ref)
     sent = []
 
     def send(place, half):
@@ -80,6 +83,8 @@
         copy.start()
         sent.append(copy)
 
+    third.wait()
+    marks = turned_mask(near_mask)
     first.wait()
     wide[...] = near[...].astype(f32)
     for place in range(places):
@@ -401,14 +406,15 @@
             shape(group, 2 * share * sensors, width),
             inputs, mask, cotangent,
             vmem=60,
-            in_specs=[far_spec, near_spec, far_spec],
+            in_specs=[far_spec, far_spec, far_spec],
             out_specs=far_spec,
             scratch_shapes=[
                 pltpu.VMEM(inputs.shape, bf16),
+                pltpu.VMEM(mask.shape, mask.dtype),
                 pltpu.VMEM(inputs.shape, bf16),
                 wide,
                 pltpu.VMEM((group, 2 * share * sensors, width), f32),
-                pltpu.SemaphoreType.DMA((2 * group + 2,)),
+                pltpu.SemaphoreType.DMA((2 * group + 3,)),
             ],
         )
     )

time: 72.5 us -> 71.7 us (0.989)
  no operation moved by 1% of the time
where the time goes in v5:
time: 71.7 us; the launch traced here: 71.4 us
  blocking collectives  21.2 us (30%)
  waiting for transfers between devices  19.9 us (28%)
  starting transfers between devices  18.5 us (26%)
  Pallas kernels  10.9 us (15%)
  between operations  0.81 us (1%)
    all_to_all x1, blocking collectives, swap(): lax.all_to_all(rows, 'sensor', 0, 0, tiled=True, axis_index_groups=blocks)  21.2 us
    ppermute x8, waiting for transfers between devices, partner(): return lax.ppermute(rows, 'sensor', [(i, i ^ m) for i in range(n_sensor)])  13.3 us
    pallas_call x8, Pallas kernels, call(): pl.pallas_call(kernel, out_shape=out_shape, compiler_params=params(vmem),...  10.9 us
    ppermute x8, starting transfers between devices, partner(): return lax.ppermute(rows, 'sensor', [(i, i ^ m) for i in range(n_sensor)])  10.2 us
    ppermute x2, waiting for transfers between devices, others(): lax.ppermute(rows, 'sensor', [(i, (i + step * group) % n_sensor) for i in...  5.21 us
    ppermute x2, starting transfers between devices, others(): lax.ppermute(rows, 'sensor', [(i, (i + step * group) % n_sensor) for i in...  4.65 us
    all_to_all x1, starting transfers between devices, swap(): lax.all_to_all(rows, 'sensor', 0, 0, tiled=True, axis_index_groups=blocks)  3.57 us
  transfers between devices with their start and end apart: 12, of which 10 were waited for; matrix products, arithmetic and copies ran while one was open for 0% of the time, Pallas kernels for 5%

profile of v5, /device:TPU:0, one launch (start us, length us, event | category | flops | bytes accessed | tf_op | source)
XLA Modules:
  0.0 71.4 jit_solution(10479219612735839292)
XLA Ops:
  0.6 0.0 copy-start
  0.6 0.0 copy-start.1
  0.7 0.0 copy-start.2
  0.7 0.0 copy-start.3
  0.7 0.0 copy-start.4
  0.7 2.4 %shard_map.135 = f32[8,256,128]{2,1,0:T(8,128)} custom-call(bf16[64,16,128]{2,1,0:T(8,128)(2,1)} %inputs_ref.1, s32[16,64]{1,0:T(8,128)} %bitcast.19, bf16[64,16,128]{2,1,0:T(8,128)(2,1)} %cotangent_ref.1), custom_call_target="tpu_custom_call" | custom-call | tf_op jit(solution)/shard_map/pallas_call | solution.py:365
  3.1 21.2 %all_to_all.10.swapped = f32[8,256,128]{2,1,0:T(8,128)S(1)} all-to-all(f32[8,256,128]{2,1,0:T(8,128)} %shard_map.135), channel_id=1, replica_groups={{0,2,4,6,8,10,12,14},{16,18,20,22,24,26,28,30},{1,3,5,7,9,11,13,15},{17..., dimensions={0} | all-to-all | bytes 2097152 | tf_op jit(solution)/shard_map/all_to_all | solution.py:384
  24.3 0.0 copy-done
  24.3 0.0 copy-done.1
  24.3 0.0 copy-done.2
  24.3 0.9 %shard_map.137.refs_0_ = f32[136,128]{1,0:T(8,128)S(1)} custom-call(f32[8,256,128]{2,1,0:T(8,128)S(1)} %all_to_all.10.swapped, f32[64,128]{1,0:T(8,128)S(1)} %copy-done, bf16[128,128]{1,0:T(8,128)(2,1)S(1)} %copy-done.1, bf16[128,128]{1,0:T(8,128)(2,1)S(1)} %copy-done.2), custom_call_target="tpu_custom_call" | custom-call | tf_op jit(solution)/shard_map/pallas_call | solution.py:365
  25.2 2.6 %collective-permute-start = (f32[136,128]{1,0:T(8,128)S(1)}, f32[136,128]{1,0:T(8,128)S(1)}, u32[]{:S(2)}, u32[]{:S(2)}) collective-permute-start(f32[136,128]{1,0:T(8,128)S(1)} %shard_map.137.refs_0_), channel_id=1, source_target_pairs={{0,16},{2,18},{4,20},{6,22},{8,24},{10,26},{12,28},{14,30},{16,0},... | collective-permute-start | bytes 208904 | tf_op jit(solution)/shard_map/ppermute | solution.py:388
  27.8 0.0 copy-done.3
  27.8 0.0 copy-done.4
  27.8 0.9 %shard_map.136 = (f32[4,1024,128]{2,1,0:T(8,128)S(1)}, f32[3,1024,128]{2,1,0:T(8,128)S(1)}) custom-call(f32[8,256,128]{2,1,0:T(8,128)S(1)} %all_to_all.10.swapped, f32[64,128]{1,0:T(8,128)S(1)} %copy-done, bf16[128,128]{1,0:T(8,128)(2,1)S(1)} %copy-done.1, bf16[128,128]{1,0:T(8,128)(2,1)S(1)} %copy-done.2, bf16[128,128]{1,0:T(8,128)(2,1)S(1)} %copy-done.3, ...), custom_call_target="tpu_custom_call" | custom-call | tf_op jit(solution)/shard_map/pallas_call | solution.py:365
  28.8 2.5 %collective-permute-done.refs_1_ = f32[136,128]{1,0:T(8,128)S(1)} collective-permute-done((f32[136,128]{1,0:T(8,128)S(1)}, f32[136,128]{1,0:T(8,128)S(1)}, u32[]{:S(2)}, u32[]{:S(2)}) %collective-permute-start) | collective-permute-done | bytes 69664 | tf_op jit(solution)/shard_map/ppermute | solution.py:388
  31.2 1.6 %shard_map.138 = (f32[128,128]{1,0:T(8,128)S(1)}, bf16[1024,128]{1,0:T(8,128)(2,1)S(1)}, f32[128,512]{1,0:T(8,128)S(1)}) custom-call(f32[3,1024,128]{2,1,0:T(8,128)S(1)} %get-tuple-element.28.ready_ref, f32[136,128]{1,0:T(8,128)S(1)} %shard_map.137.refs_0_, f32[136,128]{1,0:T(8,128)S(1)} %collective-permute-done.refs_1_), custom_call_target="tpu_custom_call" | custom-call | tf_op jit(solution)/shard_map/pallas_call | solution.py:365
  32.8 2.0 %collective-permute-start.1 = (f32[128,128]{1,0:T(8,128)S(1)}, f32[128,128]{1,0:T(8,128)S(1)}, u32[]{:S(2)}, u32[]{:S(2)}) collective-permute-start(f32[128,128]{1,0:T(8,128)S(1)} %get-tuple-element.33.refs_2_), channel_id=1, source_target_pairs={{0,16},{2,18},{4,20},{6,22},{8,24},{10,26},{12,28},{14,30},{16,0},... | collective-permute-start | bytes 196616 | tf_op jit(solution)/shard_map/ppermute | solution.py:388
  34.8 1.2 %shard_map.139 = (f32[8,128,128]{2,1,0:T(8,128)S(1)}, f32[1280,128]{1,0:T(8,128)S(1)}) custom-call(f32[8,256,128]{2,1,0:T(8,128)S(1)} %all_to_all.10.swapped, bf16[128,128]{1,0:T(8,128)(2,1)S(1)} %copy-done.3, bf16[128,128]{1,0:T(8,128)(2,1)S(1)} %copy-done.4, f32[3,1024,128]{2,1,0:T(8,128)S(1)} %get-tuple-element.28.ready_ref, ...), custom_call_target="tpu_custom_call" | custom-call | tf_op jit(solution)/shard_map/pallas_call | solution.py:365
  36.0 2.8 %collective-permute-done.1.refs_3_ = f32[128,128]{1,0:T(8,128)S(1)} collective-permute-done((f32[128,128]{1,0:T(8,128)S(1)}, f32[128,128]{1,0:T(8,128)S(1)}, u32[]{:S(2)}, u32[]{:S(2)}) %collective-permute-start.1) | collective-permute-done | bytes 65568 | tf_op jit(solution)/shard_map/ppermute | solution.py:388
  38.7 1.7 %shard_map.140 = (f32[8,256,128]{2,1,0:T(8,128)}, f32[2,288,128]{2,1,0:T(8,128)S(1)}) custom-call(f32[8,256,128]{2,1,0:T(8,128)S(1)} %all_to_all.10.swapped, f32[64,128]{1,0:T(8,128)S(1)} %copy-done, bf16[128,128]{1,0:T(8,128)(2,1)S(1)} %copy-done.1, bf16[128,128]{1,0:T(8,128)(2,1)S(1)} %copy-done.2, f32[4,1024,128]{2,1,0:T(8,128)S(1)} %get-tuple-element.27.ready_ref, ...), custom_call_target="tpu_custom_call" | custom-call | tf_op jit(solution)/shard_map/pallas_call | solution.py:365
  40.5 0.0 copy-start.5
  40.5 3.6 %all-to-all-start.1 = ((f32[8,256,128]{2,1,0:T(8,128)}), f32[8,256,128]{2,1,0:T(8,128)S(1)}, u32[]{:S(2)}, u32[]{:S(2)}) async-start(f32[8,256,128]{2,1,0:T(8,128)} %get-tuple-element.35), calls=%async_computation.1 | async-start | bytes 2097152 | tf_op jit(solution)/shard_map/all_to_all | solution.py:384
  44.1 0.1 collective-permute-start.2
  44.2 1.3 %collective-permute-done.2 = f32[288,128]{1,0:T(8,128)S(1)} collective-permute-done((f32[288,128]{1,0:T(8,128)S(1)}, f32[288,128]{1,0:T(8,128)S(1)}, u32[]{:S(2)}, u32[]{:S(2)}) %collective-permute-start.2) | collective-permute-done | bytes 147488 | tf_op jit(solution)/shard_map/ppermute | solution.py:470
  45.6 2.9 %collective-permute-start.5 = (f32[72,128]{1,0:T(8,128)S(1)}, f32[72,128]{1,0:T(8,128)S(1)}, u32[]{:S(2)}, u32[]{:S(2)}) collective-permute-start(f32[72,128]{1,0:T(8,128)S(1)} %get-tuple-element.48), channel_id=1, source_target_pairs={{0,6},{2,4},{4,2},{6,0},{8,14},{10,12},{12,10},{14,8},{16,22},{18,... | collective-permute-start | bytes 110600 | tf_op jit(solution)/shard_map/ppermute | solution.py:473
  48.4 0.5 collective-permute-start.4
  49.0 0.1 collective-permute-start.3
  49.1 6.4 %collective-permute-done.5 = f32[72,128]{1,0:T(8,128)S(1)} collective-permute-done((f32[72,128]{1,0:T(8,128)S(1)}, f32[72,128]{1,0:T(8,128)S(1)}, u32[]{:S(2)}, u32[]{:S(2)}) %collective-permute-start.5) | collective-permute-done | bytes 36896 | tf_op jit(solution)/shard_map/ppermute | solution.py:473
  55.5 0.3 collective-permute-done.4
  55.8 0.0 collective-permute-done.3
  55.8 1.2 %collective-permute-start.6 = (f32[72,128]{1,0:T(8,128)S(1)}, f32[72,128]{1,0:T(8,128)S(1)}, u32[]{:S(2)}, u32[]{:S(2)}) collective-permute-start(f32[72,128]{1,0:T(8,128)S(1)} %fusion.1), channel_id=1, source_target_pairs={{0,8},{2,10},{4,12},{6,14},{8,0},{10,2},{12,4},{14,6},{16,24},{18,... | collective-permute-start | bytes 110600 | tf_op jit(solution)/shard_map/ppermute | solution.py:473
  57.0 2.8 %collective-permute-done.6 = f32[72,128]{1,0:T(8,128)S(1)} collective-permute-done((f32[72,128]{1,0:T(8,128)S(1)}, f32[72,128]{1,0:T(8,128)S(1)}, u32[]{:S(2)}, u32[]{:S(2)}) %collective-permute-start.6) | collective-permute-done | bytes 36896 | tf_op jit(solution)/shard_map/ppermute | solution.py:473
  59.8 2.0 %collective-permute-start.7 = (f32[72,128]{1,0:T(8,128)S(1)}, f32[72,128]{1,0:T(8,128)S(1)}, u32[]{:S(2)}, u32[]{:S(2)}) collective-permute-start(f32[72,128]{1,0:T(8,128)S(1)} %add.52), channel_id=1, source_target_pairs={{0,16},{2,18},{4,20},{6,22},{8,24},{10,26},{12,28},{14,30},{16,0},... | collective-permute-start | bytes 110600 | tf_op jit(solution)/shard_map/ppermute | solution.py:473
  61.8 0.0 all-to-all-done.1.rows_ref
  61.8 0.0 copy-done.5
  61.8 1.6 %shard_map.141 = (bf16[64,16,128]{2,1,0:T(8,128)(2,1)}, bf16[64,16,128]{2,1,0:T(8,128)(2,1)}) custom-call(f32[8,256,128]{2,1,0:T(8,128)S(1)} %all-to-all-done.1.rows_ref, s32[16,64]{1,0:T(8,128)S(1)} %bitcast.20), custom_call_target="tpu_custom_call" | custom-call | tf_op jit(solution)/shard_map/pallas_call | solution.py:365
  63.4 1.3 %collective-permute-done.7 = f32[72,128]{1,0:T(8,128)S(1)} collective-permute-done((f32[72,128]{1,0:T(8,128)S(1)}, f32[72,128]{1,0:T(8,128)S(1)}, u32[]{:S(2)}, u32[]{:S(2)}) %collective-permute-start.7) | collective-permute-done | bytes 36896 | tf_op jit(solution)/shard_map/ppermute | solution.py:473
  64.7 0.6 collective-permute-start.8
  65.3 0.6 collective-permute-start.9
  65.9 2.3 %collective-permute-start.10 = (f32[72,128]{1,0:T(8,128)S(1)}, f32[72,128]{1,0:T(8,128)S(1)}, u32[]{:S(2)}, u32[]{:S(2)}) collective-permute-start(f32[72,128]{1,0:T(8,128)S(1)} %add.53.refs_0_), channel_id=1, source_target_pairs={{0,6},{2,4},{4,2},{6,0},{8,14},{10,12},{12,10},{14,8},{16,22},{18,... | collective-permute-start | bytes 110600 | tf_op jit(solution)/shard_map/ppermute | solution.py:473
  68.2 0.5 collective-permute-done.8.refs_1_
  68.6 0.6 collective-permute-done.9.refs_2_
  69.3 1.5 %collective-permute-done.10.refs_3_ = f32[72,128]{1,0:T(8,128)S(1)} collective-permute-done((f32[72,128]{1,0:T(8,128)S(1)}, f32[72,128]{1,0:T(8,128)S(1)}, u32[]{:S(2)}, u32[]{:S(2)}) %collective-permute-start.10) | collective-permute-done | bytes 36896 | tf_op jit(solution)/shard_map/ppermute | solution.py:473
  70.8 0.7 shard_map.142
  (6 shorter events, 0.1 us)
Async XLA Ops:
  0.6 23.7 %copy-start = (f32[64,128]{1,0:T(8,128)S(1)}, f32[64,128]{1,0:T(8,128)}, u32[]{:S(2)}) copy-start(f32[64,128]{1,0:T(8,128)} %projector.5) | copy-start | bytes 98308
  0.6 23.7 %copy-start.1 = (bf16[128,128]{1,0:T(8,128)(2,1)S(1)}, bf16[128,128]{1,0:T(8,128)(2,1)}, u32[]{:S(2)}) copy-start(bf16[128,128]{1,0:T(8,128)(2,1)} %wk.5) | copy-start | bytes 98308
  0.7 23.7 %copy-start.2 = (bf16[128,128]{1,0:T(8,128)(2,1)S(1)}, bf16[128,128]{1,0:T(8,128)(2,1)}, u32[]{:S(2)}) copy-start(bf16[128,128]{1,0:T(8,128)(2,1)} %wv.5) | copy-start | bytes 98308
  0.7 27.2 %copy-start.3 = (bf16[128,128]{1,0:T(8,128)(2,1)S(1)}, bf16[128,128]{1,0:T(8,128)(2,1)}, u32[]{:S(2)}) copy-start(bf16[128,128]{1,0:T(8,128)(2,1)} %wq.3) | copy-start | bytes 98308
  0.7 27.2 %copy-start.4 = (bf16[128,128]{1,0:T(8,128)(2,1)S(1)}, bf16[128,128]{1,0:T(8,128)(2,1)}, u32[]{:S(2)}) copy-start(bf16[128,128]{1,0:T(8,128)(2,1)} %wo.3) | copy-start | bytes 98308
  25.2 6.0 %collective-permute-start = (f32[136,128]{1,0:T(8,128)S(1)}, f32[136,128]{1,0:T(8,128)S(1)}, u32[]{:S(2)}, u32[]{:S(2)}) collective-permute-start(f32[136,128]{1,0:T(8,128)S(1)} %shard_map.137.refs_0_), channel_id=1, source_target_pairs={{0,16},{2,18},{4,20},{6,22},{8,24},{10,26},{12,28},{14,30},{16,0},... | collective-permute-start | bytes 208904 | tf_op jit(solution)/shard_map/ppermute | solution.py:388
  32.8 5.9 %collective-permute-start.1 = (f32[128,128]{1,0:T(8,128)S(1)}, f32[128,128]{1,0:T(8,128)S(1)}, u32[]{:S(2)}, u32[]{:S(2)}) collective-permute-start(f32[128,128]{1,0:T(8,128)S(1)} %get-tuple-element.33.refs_2_), channel_id=1, source_target_pairs={{0,16},{2,18},{4,20},{6,22},{8,24},{10,26},{12,28},{14,30},{16,0},... | collective-permute-start | bytes 196616 | tf_op jit(solution)/shard_map/ppermute | solution.py:388
  40.5 21.4 %copy-start.5 = (s32[64,16]{0,1:T(8,128)S(1)}, s32[64,16]{0,1:T(8,128)}, u32[]{:S(2)}) copy-start(s32[64,16]{0,1:T(8,128)} %param.9) | copy-start | bytes 12292
  40.5 21.4 %all-to-all-start.1 = ((f32[8,256,128]{2,1,0:T(8,128)}), f32[8,256,128]{2,1,0:T(8,128)S(1)}, u32[]{:S(2)}, u32[]{:S(2)}) async-start(f32[8,256,128]{2,1,0:T(8,128)} %get-tuple-element.35), calls=%async_computation.1 | async-start | bytes 2097152 | tf_op jit(solution)/shard_map/all_to_all | solution.py:384
  44.1 1.4 %collective-permute-start.2 = (f32[288,128]{1,0:T(8,128)S(1)}, f32[288,128]{1,0:T(8,128)S(1)}, u32[]{:S(2)}, u32[]{:S(2)}) collective-permute-start(f32[288,128]{1,0:T(8,128)S(1)} %dynamic-slice_bitcast_fusion), channel_id=1, source_target_pairs={{0,1},{1,0},{2,3},{3,2},{4,5},{5,4},{6,7},{7,6},{8,9},{9,8},{10,11... | collective-permute-start | bytes 442376 | tf_op jit(solution)/shard_map/ppermute | solution.py:470
  45.6 9.9 %collective-permute-start.5 = (f32[72,128]{1,0:T(8,128)S(1)}, f32[72,128]{1,0:T(8,128)S(1)}, u32[]{:S(2)}, u32[]{:S(2)}) collective-permute-start(f32[72,128]{1,0:T(8,128)S(1)} %get-tuple-element.48), channel_id=1, source_target_pairs={{0,6},{2,4},{4,2},{6,0},{8,14},{10,12},{12,10},{14,8},{16,22},{18,... | collective-permute-start | bytes 110600 | tf_op jit(solution)/shard_map/ppermute | solution.py:473
  48.4 7.3 %collective-permute-start.4 = (f32[72,128]{1,0:T(8,128)S(1)}, f32[72,128]{1,0:T(8,128)S(1)}, u32[]{:S(2)}, u32[]{:S(2)}) collective-permute-start(f32[72,128]{1,0:T(8,128)S(1)} %get-tuple-element.49), channel_id=1, source_target_pairs={{0,4},{2,6},{4,0},{6,2},{8,12},{10,14},{12,8},{14,10},{16,20},{18,... | collective-permute-start | bytes 110600 | tf_op jit(solution)/shard_map/ppermute | solution.py:473
  49.0 6.8 %collective-permute-start.3 = (f32[72,128]{1,0:T(8,128)S(1)}, f32[72,128]{1,0:T(8,128)S(1)}, u32[]{:S(2)}, u32[]{:S(2)}) collective-permute-start(f32[72,128]{1,0:T(8,128)S(1)} %get-tuple-element.47), channel_id=1, source_target_pairs={{0,2},{2,0},{4,6},{6,4},{8,10},{10,8},{12,14},{14,12},{16,18},{18,... | collective-permute-start | bytes 110600 | tf_op jit(solution)/shard_map/ppermute | solution.py:473
  55.8 4.0 %collective-permute-start.6 = (f32[72,128]{1,0:T(8,128)S(1)}, f32[72,128]{1,0:T(8,128)S(1)}, u32[]{:S(2)}, u32[]{:S(2)}) collective-permute-start(f32[72,128]{1,0:T(8,128)S(1)} %fusion.1), channel_id=1, source_target_pairs={{0,8},{2,10},{4,12},{6,14},{8,0},{10,2},{12,4},{14,6},{16,24},{18,... | collective-permute-start | bytes 110600 | tf_op jit(solution)/shard_map/ppermute | solution.py:473
  59.8 4.9 %collective-permute-start.7 = (f32[72,128]{1,0:T(8,128)S(1)}, f32[72,128]{1,0:T(8,128)S(1)}, u32[]{:S(2)}, u32[]{:S(2)}) collective-permute-start(f32[72,128]{1,0:T(8,128)S(1)} %add.52), channel_id=1, source_target_pairs={{0,16},{2,18},{4,20},{6,22},{8,24},{10,26},{12,28},{14,30},{16,0},... | collective-permute-start | bytes 110600 | tf_op jit(solution)/shard_map/ppermute | solution.py:473
  64.7 4.0 %collective-permute-start.8 = (f32[72,128]{1,0:T(8,128)S(1)}, f32[72,128]{1,0:T(8,128)S(1)}, u32[]{:S(2)}, u32[]{:S(2)}) collective-permute-start(f32[72,128]{1,0:T(8,128)S(1)} %add.53.refs_0_), channel_id=1, source_target_pairs={{0,2},{2,0},{4,6},{6,4},{8,10},{10,8},{12,14},{14,12},{16,18},{18,... | collective-permute-start | bytes 110600 | tf_op jit(solution)/shard_map/ppermute | solution.py:473
  65.3 4.0 %collective-permute-start.9 = (f32[72,128]{1,0:T(8,128)S(1)}, f32[72,128]{1,0:T(8,128)S(1)}, u32[]{:S(2)}, u32[]{:S(2)}) collective-permute-start(f32[72,128]{1,0:T(8,128)S(1)} %add.53.refs_0_), channel_id=1, source_target_pairs={{0,4},{2,6},{4,0},{6,2},{8,12},{10,14},{12,8},{14,10},{16,20},{18,... | collective-permute-start | bytes 110600 | tf_op jit(solution)/shard_map/ppermute | solution.py:473
  65.9 4.9 %collective-permute-start.10 = (f32[72,128]{1,0:T(8,128)S(1)}, f32[72,128]{1,0:T(8,128)S(1)}, u32[]{:S(2)}, u32[]{:S(2)}) collective-permute-start(f32[72,128]{1,0:T(8,128)S(1)} %add.53.refs_0_), channel_id=1, source_target_pairs={{0,6},{2,4},{4,2},{6,0},{8,14},{10,12},{12,10},{14,8},{16,22},{18,... | collective-permute-start | bytes 110600 | tf_op jit(solution)/shard_map/ppermute | solution.py:473

commit v6 on v5

--- a/solution.py
+++ b/solution.py
@@ -35,10 +35,11 @@
 def close_dot(left, right, left_dim, right_dim):
     high, low = split(left)
     right_high, right_low = split(right)
-    return (
-        dot(high, right_high, left_dim, right_dim)
-        + dot(high, right_low, left_dim, right_dim)
-        + dot(low, right_high, left_dim, right_dim)
+    return dot(
+        jnp.concatenate([high, high, low], axis=left_dim),
+        jnp.concatenate([right_high, right_low, right_high], axis=right_dim),
+        left_dim,
+        right_dim,
     )
 
 

time: 71.7 us -> 71.5 us (level)
  no operation moved by 1% of the time
where the time goes in v6:
time: 71.5 us; the launch traced here: 71.3 us
  blocking collectives  21.2 us (30%)
  waiting for transfers between devices  19.8 us (28%)
  starting transfers between devices  18.6 us (26%)
  Pallas kernels  10.7 us (15%)
  between operations  0.81 us (1%)
    all_to_all x1, blocking collectives, swap(): lax.all_to_all(rows, 'sensor', 0, 0, tiled=True, axis_index_groups=blocks)  21.2 us
    ppermute x8, waiting for transfers between devices, partner(): return lax.ppermute(rows, 'sensor', [(i, i ^ m) for i in range(n_sensor)])  13.3 us
    pallas_call x8, Pallas kernels, call(): pl.pallas_call(kernel, out_shape=out_shape, compiler_params=params(vmem),...  10.7 us
    ppermute x8, starting transfers between devices, partner(): return lax.ppermute(rows, 'sensor', [(i, i ^ m) for i in range(n_sensor)])  10.3 us
    ppermute x2, waiting for transfers between devices, others(): lax.ppermute(rows, 'sensor', [(i, (i + step * group) % n_sensor) for i in...  5.15 us
    ppermute x2, starting transfers between devices, others(): lax.ppermute(rows, 'sensor', [(i, (i + step * group) % n_sensor) for i in...  4.67 us
    all_to_all x1, starting transfers between devices, swap(): lax.all_to_all(rows, 'sensor', 0, 0, tiled=True, axis_index_groups=blocks)  3.57 us
  transfers between devices with their start and end apart: 12, of which 10 were waited for; matrix products, arithmetic and copies ran while one was open for 0% of the time, Pallas kernels for 5%

profile of v6, /device:TPU:0, one launch (start us, length us, event | category | flops | bytes accessed | tf_op | source)
XLA Modules:
  0.0 71.3 jit_solution(16106645883280949659)
XLA Ops:
  0.6 0.0 copy-start
  0.6 0.0 copy-start.1
  0.7 0.0 copy-start.2
  0.7 0.0 copy-start.3
  0.7 0.0 copy-start.4
  0.7 2.4 %shard_map.135 = f32[8,256,128]{2,1,0:T(8,128)} custom-call(bf16[64,16,128]{2,1,0:T(8,128)(2,1)} %inputs_ref.1, s32[16,64]{1,0:T(8,128)} %bitcast.19, bf16[64,16,128]{2,1,0:T(8,128)(2,1)} %cotangent_ref.1), custom_call_target="tpu_custom_call" | custom-call | tf_op jit(solution)/shard_map/pallas_call | solution.py:366
  3.1 21.2 %all_to_all.10.swapped = f32[8,256,128]{2,1,0:T(8,128)S(1)} all-to-all(f32[8,256,128]{2,1,0:T(8,128)} %shard_map.135), channel_id=1, replica_groups={{0,2,4,6,8,10,12,14},{16,18,20,22,24,26,28,30},{1,3,5,7,9,11,13,15},{17..., dimensions={0} | all-to-all | bytes 2097152 | tf_op jit(solution)/shard_map/all_to_all | solution.py:385
  24.3 0.0 copy-done
  24.3 0.0 copy-done.1
  24.3 0.0 copy-done.2
  24.3 0.8 %shard_map.137.refs_0_ = f32[136,128]{1,0:T(8,128)S(1)} custom-call(f32[8,256,128]{2,1,0:T(8,128)S(1)} %all_to_all.10.swapped, f32[64,128]{1,0:T(8,128)S(1)} %copy-done, bf16[128,128]{1,0:T(8,128)(2,1)S(1)} %copy-done.1, bf16[128,128]{1,0:T(8,128)(2,1)S(1)} %copy-done.2), custom_call_target="tpu_custom_call" | custom-call | tf_op jit(solution)/shard_map/pallas_call | solution.py:366
  25.1 2.7 %collective-permute-start = (f32[136,128]{1,0:T(8,128)S(1)}, f32[136,128]{1,0:T(8,128)S(1)}, u32[]{:S(2)}, u32[]{:S(2)}) collective-permute-start(f32[136,128]{1,0:T(8,128)S(1)} %shard_map.137.refs_0_), channel_id=1, source_target_pairs={{0,16},{2,18},{4,20},{6,22},{8,24},{10,26},{12,28},{14,30},{16,0},... | collective-permute-start | bytes 208904 | tf_op jit(solution)/shard_map/ppermute | solution.py:389
  27.8 0.0 copy-done.3
  27.8 0.0 copy-done.4
  27.8 1.0 %shard_map.136 = (f32[4,1024,128]{2,1,0:T(8,128)S(1)}, f32[3,1024,128]{2,1,0:T(8,128)S(1)}) custom-call(f32[8,256,128]{2,1,0:T(8,128)S(1)} %all_to_all.10.swapped, f32[64,128]{1,0:T(8,128)S(1)} %copy-done, bf16[128,128]{1,0:T(8,128)(2,1)S(1)} %copy-done.1, bf16[128,128]{1,0:T(8,128)(2,1)S(1)} %copy-done.2, bf16[128,128]{1,0:T(8,128)(2,1)S(1)} %copy-done.3, ...), custom_call_target="tpu_custom_call" | custom-call | tf_op jit(solution)/shard_map/pallas_call | solution.py:366
  28.8 2.4 %collective-permute-done.refs_1_ = f32[136,128]{1,0:T(8,128)S(1)} collective-permute-done((f32[136,128]{1,0:T(8,128)S(1)}, f32[136,128]{1,0:T(8,128)S(1)}, u32[]{:S(2)}, u32[]{:S(2)}) %collective-permute-start) | collective-permute-done | bytes 69664 | tf_op jit(solution)/shard_map/ppermute | solution.py:389
  31.1 1.5 %shard_map.138 = (f32[128,128]{1,0:T(8,128)S(1)}, bf16[1024,128]{1,0:T(8,128)(2,1)S(1)}, f32[128,512]{1,0:T(8,128)S(1)}) custom-call(f32[3,1024,128]{2,1,0:T(8,128)S(1)} %get-tuple-element.28.ready_ref, f32[136,128]{1,0:T(8,128)S(1)} %shard_map.137.refs_0_, f32[136,128]{1,0:T(8,128)S(1)} %collective-permute-done.refs_1_), custom_call_target="tpu_custom_call" | custom-call | tf_op jit(solution)/shard_map/pallas_call | solution.py:366
  32.6 2.0 %collective-permute-start.1 = (f32[128,128]{1,0:T(8,128)S(1)}, f32[128,128]{1,0:T(8,128)S(1)}, u32[]{:S(2)}, u32[]{:S(2)}) collective-permute-start(f32[128,128]{1,0:T(8,128)S(1)} %get-tuple-element.33.refs_2_), channel_id=1, source_target_pairs={{0,16},{2,18},{4,20},{6,22},{8,24},{10,26},{12,28},{14,30},{16,0},... | collective-permute-start | bytes 196616 | tf_op jit(solution)/shard_map/ppermute | solution.py:389
  34.7 1.1 %shard_map.139 = (f32[8,128,128]{2,1,0:T(8,128)S(1)}, f32[1280,128]{1,0:T(8,128)S(1)}) custom-call(f32[8,256,128]{2,1,0:T(8,128)S(1)} %all_to_all.10.swapped, bf16[128,128]{1,0:T(8,128)(2,1)S(1)} %copy-done.3, bf16[128,128]{1,0:T(8,128)(2,1)S(1)} %copy-done.4, f32[3,1024,128]{2,1,0:T(8,128)S(1)} %get-tuple-element.28.ready_ref, ...), custom_call_target="tpu_custom_call" | custom-call | tf_op jit(solution)/shard_map/pallas_call | solution.py:366
  35.8 2.8 %collective-permute-done.1.refs_3_ = f32[128,128]{1,0:T(8,128)S(1)} collective-permute-done((f32[128,128]{1,0:T(8,128)S(1)}, f32[128,128]{1,0:T(8,128)S(1)}, u32[]{:S(2)}, u32[]{:S(2)}) %collective-permute-start.1) | collective-permute-done | bytes 65568 | tf_op jit(solution)/shard_map/ppermute | solution.py:389
  38.6 1.7 %shard_map.140 = (f32[8,256,128]{2,1,0:T(8,128)}, f32[2,288,128]{2,1,0:T(8,128)S(1)}) custom-call(f32[8,256,128]{2,1,0:T(8,128)S(1)} %all_to_all.10.swapped, f32[64,128]{1,0:T(8,128)S(1)} %copy-done, bf16[128,128]{1,0:T(8,128)(2,1)S(1)} %copy-done.1, bf16[128,128]{1,0:T(8,128)(2,1)S(1)} %copy-done.2, f32[4,1024,128]{2,1,0:T(8,128)S(1)} %get-tuple-element.27.ready_ref, ...), custom_call_target="tpu_custom_call" | custom-call | tf_op jit(solution)/shard_map/pallas_call | solution.py:366
  40.3 0.0 copy-start.5
  40.3 3.6 %all-to-all-start.1 = ((f32[8,256,128]{2,1,0:T(8,128)}), f32[8,256,128]{2,1,0:T(8,128)S(1)}, u32[]{:S(2)}, u32[]{:S(2)}) async-start(f32[8,256,128]{2,1,0:T(8,128)} %get-tuple-element.35), calls=%async_computation.1 | async-start | bytes 2097152 | tf_op jit(solution)/shard_map/all_to_all | solution.py:385
  43.9 0.1 collective-permute-start.2
  44.0 1.3 %collective-permute-done.2 = f32[288,128]{1,0:T(8,128)S(1)} collective-permute-done((f32[288,128]{1,0:T(8,128)S(1)}, f32[288,128]{1,0:T(8,128)S(1)}, u32[]{:S(2)}, u32[]{:S(2)}) %collective-permute-start.2) | collective-permute-done | bytes 147488 | tf_op jit(solution)/shard_map/ppermute | solution.py:471
  45.4 2.9 %collective-permute-start.5 = (f32[72,128]{1,0:T(8,128)S(1)}, f32[72,128]{1,0:T(8,128)S(1)}, u32[]{:S(2)}, u32[]{:S(2)}) collective-permute-start(f32[72,128]{1,0:T(8,128)S(1)} %get-tuple-element.48), channel_id=1, source_target_pairs={{0,6},{2,4},{4,2},{6,0},{8,14},{10,12},{12,10},{14,8},{16,22},{18,... | collective-permute-start | bytes 110600 | tf_op jit(solution)/shard_map/ppermute | solution.py:474
  48.3 0.5 collective-permute-start.4
  48.8 0.1 collective-permute-start.3
  49.0 6.4 %collective-permute-done.5 = f32[72,128]{1,0:T(8,128)S(1)} collective-permute-done((f32[72,128]{1,0:T(8,128)S(1)}, f32[72,128]{1,0:T(8,128)S(1)}, u32[]{:S(2)}, u32[]{:S(2)}) %collective-permute-start.5) | collective-permute-done | bytes 36896 | tf_op jit(solution)/shard_map/ppermute | solution.py:474
  55.3 0.3 collective-permute-done.4
  55.6 0.0 collective-permute-done.3
  55.6 1.2 %collective-permute-start.6 = (f32[72,128]{1,0:T(8,128)S(1)}, f32[72,128]{1,0:T(8,128)S(1)}, u32[]{:S(2)}, u32[]{:S(2)}) collective-permute-start(f32[72,128]{1,0:T(8,128)S(1)} %fusion.1), channel_id=1, source_target_pairs={{0,8},{2,10},{4,12},{6,14},{8,0},{10,2},{12,4},{14,6},{16,24},{18,... | collective-permute-start | bytes 110600 | tf_op jit(solution)/shard_map/ppermute | solution.py:474
  56.8 2.8 %collective-permute-done.6 = f32[72,128]{1,0:T(8,128)S(1)} collective-permute-done((f32[72,128]{1,0:T(8,128)S(1)}, f32[72,128]{1,0:T(8,128)S(1)}, u32[]{:S(2)}, u32[]{:S(2)}) %collective-permute-start.6) | collective-permute-done | bytes 36896 | tf_op jit(solution)/shard_map/ppermute | solution.py:474
  59.7 2.0 %collective-permute-start.7 = (f32[72,128]{1,0:T(8,128)S(1)}, f32[72,128]{1,0:T(8,128)S(1)}, u32[]{:S(2)}, u32[]{:S(2)}) collective-permute-start(f32[72,128]{1,0:T(8,128)S(1)} %add.52), channel_id=1, source_target_pairs={{0,16},{2,18},{4,20},{6,22},{8,24},{10,26},{12,28},{14,30},{16,0},... | collective-permute-start | bytes 110600 | tf_op jit(solution)/shard_map/ppermute | solution.py:474
  61.7 0.0 all-to-all-done.1.rows_ref
  61.7 0.0 copy-done.5
  61.7 1.6 %shard_map.141 = (bf16[64,16,128]{2,1,0:T(8,128)(2,1)}, bf16[64,16,128]{2,1,0:T(8,128)(2,1)}) custom-call(f32[8,256,128]{2,1,0:T(8,128)S(1)} %all-to-all-done.1.rows_ref, s32[16,64]{1,0:T(8,128)S(1)} %bitcast.20), custom_call_target="tpu_custom_call" | custom-call | tf_op jit(solution)/shard_map/pallas_call | solution.py:366
  63.3 1.2 %collective-permute-done.7 = f32[72,128]{1,0:T(8,128)S(1)} collective-permute-done((f32[72,128]{1,0:T(8,128)S(1)}, f32[72,128]{1,0:T(8,128)S(1)}, u32[]{:S(2)}, u32[]{:S(2)}) %collective-permute-start.7) | collective-permute-done | bytes 36896 | tf_op jit(solution)/shard_map/ppermute | solution.py:474
  64.5 0.6 collective-permute-start.8
  65.1 0.6 collective-permute-start.9
  65.7 2.3 %collective-permute-start.10 = (f32[72,128]{1,0:T(8,128)S(1)}, f32[72,128]{1,0:T(8,128)S(1)}, u32[]{:S(2)}, u32[]{:S(2)}) collective-permute-start(f32[72,128]{1,0:T(8,128)S(1)} %add.53.refs_0_), channel_id=1, source_target_pairs={{0,6},{2,4},{4,2},{6,0},{8,14},{10,12},{12,10},{14,8},{16,22},{18,... | collective-permute-start | bytes 110600 | tf_op jit(solution)/shard_map/ppermute | solution.py:474
  68.0 0.5 collective-permute-done.8.refs_1_
  68.5 0.6 collective-permute-done.9.refs_2_
  69.1 1.5 %collective-permute-done.10.refs_3_ = f32[72,128]{1,0:T(8,128)S(1)} collective-permute-done((f32[72,128]{1,0:T(8,128)S(1)}, f32[72,128]{1,0:T(8,128)S(1)}, u32[]{:S(2)}, u32[]{:S(2)}) %collective-permute-start.10) | collective-permute-done | bytes 36896 | tf_op jit(solution)/shard_map/ppermute | solution.py:474
  70.6 0.7 shard_map.142
  (6 shorter events, 0.1 us)
Async XLA Ops:
  0.6 23.7 %copy-start = (f32[64,128]{1,0:T(8,128)S(1)}, f32[64,128]{1,0:T(8,128)}, u32[]{:S(2)}) copy-start(f32[64,128]{1,0:T(8,128)} %projector.5) | copy-start | bytes 98308
  0.6 23.7 %copy-start.1 = (bf16[128,128]{1,0:T(8,128)(2,1)S(1)}, bf16[128,128]{1,0:T(8,128)(2,1)}, u32[]{:S(2)}) copy-start(bf16[128,128]{1,0:T(8,128)(2,1)} %wk.5) | copy-start | bytes 98308
  0.7 23.7 %copy-start.2 = (bf16[128,128]{1,0:T(8,128)(2,1)S(1)}, bf16[128,128]{1,0:T(8,128)(2,1)}, u32[]{:S(2)}) copy-start(bf16[128,128]{1,0:T(8,128)(2,1)} %wv.5) | copy-start | bytes 98308
  0.7 27.1 %copy-start.3 = (bf16[128,128]{1,0:T(8,128)(2,1)S(1)}, bf16[128,128]{1,0:T(8,128)(2,1)}, u32[]{:S(2)}) copy-start(bf16[128,128]{1,0:T(8,128)(2,1)} %wq.3) | copy-start | bytes 98308
  0.7 27.1 %copy-start.4 = (bf16[128,128]{1,0:T(8,128)(2,1)S(1)}, bf16[128,128]{1,0:T(8,128)(2,1)}, u32[]{:S(2)}) copy-start(bf16[128,128]{1,0:T(8,128)(2,1)} %wo.3) | copy-start | bytes 98308
  25.1 6.0 %collective-permute-start = (f32[136,128]{1,0:T(8,128)S(1)}, f32[136,128]{1,0:T(8,128)S(1)}, u32[]{:S(2)}, u32[]{:S(2)}) collective-permute-start(f32[136,128]{1,0:T(8,128)S(1)} %shard_map.137.refs_0_), channel_id=1, source_target_pairs={{0,16},{2,18},{4,20},{6,22},{8,24},{10,26},{12,28},{14,30},{16,0},... | collective-permute-start | bytes 208904 | tf_op jit(solution)/shard_map/ppermute | solution.py:389
  32.6 5.9 %collective-permute-start.1 = (f32[128,128]{1,0:T(8,128)S(1)}, f32[128,128]{1,0:T(8,128)S(1)}, u32[]{:S(2)}, u32[]{:S(2)}) collective-permute-start(f32[128,128]{1,0:T(8,128)S(1)} %get-tuple-element.33.refs_2_), channel_id=1, source_target_pairs={{0,16},{2,18},{4,20},{6,22},{8,24},{10,26},{12,28},{14,30},{16,0},... | collective-permute-start | bytes 196616 | tf_op jit(solution)/shard_map/ppermute | solution.py:389
  40.3 21.4 %copy-start.5 = (s32[64,16]{0,1:T(8,128)S(1)}, s32[64,16]{0,1:T(8,128)}, u32[]{:S(2)}) copy-start(s32[64,16]{0,1:T(8,128)} %param.9) | copy-start | bytes 12292
  40.3 21.4 %all-to-all-start.1 = ((f32[8,256,128]{2,1,0:T(8,128)}), f32[8,256,128]{2,1,0:T(8,128)S(1)}, u32[]{:S(2)}, u32[]{:S(2)}) async-start(f32[8,256,128]{2,1,0:T(8,128)} %get-tuple-element.35), calls=%async_computation.1 | async-start | bytes 2097152 | tf_op jit(solution)/shard_map/all_to_all | solution.py:385
  43.9 1.4 %collective-permute-start.2 = (f32[288,128]{1,0:T(8,128)S(1)}, f32[288,128]{1,0:T(8,128)S(1)}, u32[]{:S(2)}, u32[]{:S(2)}) collective-permute-start(f32[288,128]{1,0:T(8,128)S(1)} %dynamic-slice_bitcast_fusion), channel_id=1, source_target_pairs={{0,1},{1,0},{2,3},{3,2},{4,5},{5,4},{6,7},{7,6},{8,9},{9,8},{10,11... | collective-permute-start | bytes 442376 | tf_op jit(solution)/shard_map/ppermute | solution.py:471
  45.4 9.9 %collective-permute-start.5 = (f32[72,128]{1,0:T(8,128)S(1)}, f32[72,128]{1,0:T(8,128)S(1)}, u32[]{:S(2)}, u32[]{:S(2)}) collective-permute-start(f32[72,128]{1,0:T(8,128)S(1)} %get-tuple-element.48), channel_id=1, source_target_pairs={{0,6},{2,4},{4,2},{6,0},{8,14},{10,12},{12,10},{14,8},{16,22},{18,... | collective-permute-start | bytes 110600 | tf_op jit(solution)/shard_map/ppermute | solution.py:474
  48.3 7.3 %collective-permute-start.4 = (f32[72,128]{1,0:T(8,128)S(1)}, f32[72,128]{1,0:T(8,128)S(1)}, u32[]{:S(2)}, u32[]{:S(2)}) collective-permute-start(f32[72,128]{1,0:T(8,128)S(1)} %get-tuple-element.49), channel_id=1, source_target_pairs={{0,4},{2,6},{4,0},{6,2},{8,12},{10,14},{12,8},{14,10},{16,20},{18,... | collective-permute-start | bytes 110600 | tf_op jit(solution)/shard_map/ppermute | solution.py:474
  48.8 6.8 %collective-permute-start.3 = (f32[72,128]{1,0:T(8,128)S(1)}, f32[72,128]{1,0:T(8,128)S(1)}, u32[]{:S(2)}, u32[]{:S(2)}) collective-permute-start(f32[72,128]{1,0:T(8,128)S(1)} %get-tuple-element.47), channel_id=1, source_target_pairs={{0,2},{2,0},{4,6},{6,4},{8,10},{10,8},{12,14},{14,12},{16,18},{18,... | collective-permute-start | bytes 110600 | tf_op jit(solution)/shard_map/ppermute | solution.py:474
  55.6 4.0 %collective-permute-start.6 = (f32[72,128]{1,0:T(8,128)S(1)}, f32[72,128]{1,0:T(8,128)S(1)}, u32[]{:S(2)}, u32[]{:S(2)}) collective-permute-start(f32[72,128]{1,0:T(8,128)S(1)} %fusion.1), channel_id=1, source_target_pairs={{0,8},{2,10},{4,12},{6,14},{8,0},{10,2},{12,4},{14,6},{16,24},{18,... | collective-permute-start | bytes 110600 | tf_op jit(solution)/shard_map/ppermute | solution.py:474
  59.7 4.9 %collective-permute-start.7 = (f32[72,128]{1,0:T(8,128)S(1)}, f32[72,128]{1,0:T(8,128)S(1)}, u32[]{:S(2)}, u32[]{:S(2)}) collective-permute-start(f32[72,128]{1,0:T(8,128)S(1)} %add.52), channel_id=1, source_target_pairs={{0,16},{2,18},{4,20},{6,22},{8,24},{10,26},{12,28},{14,30},{16,0},... | collective-permute-start | bytes 110600 | tf_op jit(solution)/shard_map/ppermute | solution.py:474
  64.5 4.0 %collective-permute-start.8 = (f32[72,128]{1,0:T(8,128)S(1)}, f32[72,128]{1,0:T(8,128)S(1)}, u32[]{:S(2)}, u32[]{:S(2)}) collective-permute-start(f32[72,128]{1,0:T(8,128)S(1)} %add.53.refs_0_), channel_id=1, source_target_pairs={{0,2},{2,0},{4,6},{6,4},{8,10},{10,8},{12,14},{14,12},{16,18},{18,... | collective-permute-start | bytes 110600 | tf_op jit(solution)/shard_map/ppermute | solution.py:474
  65.1 4.0 %collective-permute-start.9 = (f32[72,128]{1,0:T(8,128)S(1)}, f32[72,128]{1,0:T(8,128)S(1)}, u32[]{:S(2)}, u32[]{:S(2)}) collective-permute-start(f32[72,128]{1,0:T(8,128)S(1)} %add.53.refs_0_), channel_id=1, source_target_pairs={{0,4},{2,6},{4,0},{6,2},{8,12},{10,14},{12,8},{14,10},{16,20},{18,... | collective-permute-start | bytes 110600 | tf_op jit(solution)/shard_map/ppermute | solution.py:474
  65.7 4.9 %collective-permute-start.10 = (f32[72,128]{1,0:T(8,128)S(1)}, f32[72,128]{1,0:T(8,128)S(1)}, u32[]{:S(2)}, u32[]{:S(2)}) collective-permute-start(f32[72,128]{1,0:T(8,128)S(1)} %add.53.refs_0_), channel_id=1, source_target_pairs={{0,6},{2,4},{4,2},{6,0},{8,14},{10,12},{12,10},{14,8},{16,22},{18,... | collective-permute-start | bytes 110600 | tf_op jit(solution)/shard_map/ppermute | solution.py:474

commit v7 on v6

--- a/solution.py
+++ b/solution.py
@@ -324,7 +324,9 @@
     for t in steps:
         high, low = split(d_nums[t])
         values = ready_ref[2, spans[t], :].astype(bf16)
-        d_weights.append(dot(high, values, 1, 1) + dot(low, values, 1, 1) + d_dens[t])
+        parts = jnp.concatenate([high, low], axis=1)
+        twice = jnp.concatenate([values, values], axis=1)
+        d_weights.append(dot(parts, twice, 1, 1) + d_dens[t])
     d_scores = [d_weights[t] * weights[t] for t in steps]
     d_units = [scale * rounded_dot(d_scores[t], mapping, 0, 0) for t in steps]
     d_values = [rounded_dot(weights[t], d_nums[t], 0, 0).astype(bf16) for t in steps]

time: 71.5 us -> 71.5 us (level)
  no operation moved by 1% of the time
where the time goes in v7:
time: 71.5 us; the launch traced here: 71.2 us
  blocking collectives  21.2 us (30%)
  waiting for transfers between devices  19.8 us (28%)
  starting transfers between devices  18.6 us (26%)
  Pallas kernels  10.7 us (15%)
  between operations  0.81 us (1%)
    all_to_all x1, blocking collectives, swap(): lax.all_to_all(rows, 'sensor', 0, 0, tiled=True, axis_index_groups=blocks)  21.2 us
    ppermute x8, waiting for transfers between devices, partner(): return lax.ppermute(rows, 'sensor', [(i, i ^ m) for i in range(n_sensor)])  13.3 us
    pallas_call x8, Pallas kernels, call(): pl.pallas_call(kernel, out_shape=out_shape, compiler_params=params(vmem),...  10.7 us
    ppermute x8, starting transfers between devices, partner(): return lax.ppermute(rows, 'sensor', [(i, i ^ m) for i in range(n_sensor)])  10.3 us
    ppermute x2, waiting for transfers between devices, others(): lax.ppermute(rows, 'sensor', [(i, (i + step * group) % n_sensor) for i in...  5.15 us
    ppermute x2, starting transfers between devices, others(): lax.ppermute(rows, 'sensor', [(i, (i + step * group) % n_sensor) for i in...  4.67 us
    all_to_all x1, starting transfers between devices, swap(): lax.all_to_all(rows, 'sensor', 0, 0, tiled=True, axis_index_groups=blocks)  3.57 us
  transfers between devices with their start and end apart: 12, of which 10 were waited for; matrix products, arithmetic and copies ran while one was open for 0% of the time, Pallas kernels for 5%

profile of v7, /device:TPU:0, one launch (start us, length us, event | category | flops | bytes accessed | tf_op | source)
XLA Modules:
  0.0 71.2 jit_solution(12728590986183430408)
XLA Ops:
  0.6 0.0 copy-start
  0.6 0.0 copy-start.1
  0.7 0.0 copy-start.2
  0.7 0.0 copy-start.3
  0.7 0.0 copy-start.4
  0.7 2.4 %shard_map.135 = f32[8,256,128]{2,1,0:T(8,128)} custom-call(bf16[64,16,128]{2,1,0:T(8,128)(2,1)} %inputs_ref.1, s32[16,64]{1,0:T(8,128)} %bitcast.19, bf16[64,16,128]{2,1,0:T(8,128)(2,1)} %cotangent_ref.1), custom_call_target="tpu_custom_call" | custom-call | tf_op jit(solution)/shard_map/pallas_call | solution.py:368
  3.1 21.2 %all_to_all.10.swapped = f32[8,256,128]{2,1,0:T(8,128)S(1)} all-to-all(f32[8,256,128]{2,1,0:T(8,128)} %shard_map.135), channel_id=1, replica_groups={{0,2,4,6,8,10,12,14},{16,18,20,22,24,26,28,30},{1,3,5,7,9,11,13,15},{17..., dimensions={0} | all-to-all | bytes 2097152 | tf_op jit(solution)/shard_map/all_to_all | solution.py:387
  24.3 0.0 copy-done
  24.3 0.0 copy-done.1
  24.3 0.0 copy-done.2
  24.3 0.8 %shard_map.137.refs_0_ = f32[136,128]{1,0:T(8,128)S(1)} custom-call(f32[8,256,128]{2,1,0:T(8,128)S(1)} %all_to_all.10.swapped, f32[64,128]{1,0:T(8,128)S(1)} %copy-done, bf16[128,128]{1,0:T(8,128)(2,1)S(1)} %copy-done.1, bf16[128,128]{1,0:T(8,128)(2,1)S(1)} %copy-done.2), custom_call_target="tpu_custom_call" | custom-call | tf_op jit(solution)/shard_map/pallas_call | solution.py:368
  25.1 2.7 %collective-permute-start = (f32[136,128]{1,0:T(8,128)S(1)}, f32[136,128]{1,0:T(8,128)S(1)}, u32[]{:S(2)}, u32[]{:S(2)}) collective-permute-start(f32[136,128]{1,0:T(8,128)S(1)} %shard_map.137.refs_0_), channel_id=1, source_target_pairs={{0,16},{2,18},{4,20},{6,22},{8,24},{10,26},{12,28},{14,30},{16,0},... | collective-permute-start | bytes 208904 | tf_op jit(solution)/shard_map/ppermute | solution.py:391
  27.8 0.0 copy-done.3
  27.8 0.0 copy-done.4
  27.8 1.0 %shard_map.136 = (f32[4,1024,128]{2,1,0:T(8,128)S(1)}, f32[3,1024,128]{2,1,0:T(8,128)S(1)}) custom-call(f32[8,256,128]{2,1,0:T(8,128)S(1)} %all_to_all.10.swapped, f32[64,128]{1,0:T(8,128)S(1)} %copy-done, bf16[128,128]{1,0:T(8,128)(2,1)S(1)} %copy-done.1, bf16[128,128]{1,0:T(8,128)(2,1)S(1)} %copy-done.2, bf16[128,128]{1,0:T(8,128)(2,1)S(1)} %copy-done.3, ...), custom_call_target="tpu_custom_call" | custom-call | tf_op jit(solution)/shard_map/pallas_call | solution.py:368
  28.8 2.4 %collective-permute-done.refs_1_ = f32[136,128]{1,0:T(8,128)S(1)} collective-permute-done((f32[136,128]{1,0:T(8,128)S(1)}, f32[136,128]{1,0:T(8,128)S(1)}, u32[]{:S(2)}, u32[]{:S(2)}) %collective-permute-start) | collective-permute-done | bytes 69664 | tf_op jit(solution)/shard_map/ppermute | solution.py:391
  31.1 1.5 %shard_map.138 = (f32[128,128]{1,0:T(8,128)S(1)}, bf16[1024,128]{1,0:T(8,128)(2,1)S(1)}, f32[128,512]{1,0:T(8,128)S(1)}) custom-call(f32[3,1024,128]{2,1,0:T(8,128)S(1)} %get-tuple-element.28.ready_ref, f32[136,128]{1,0:T(8,128)S(1)} %shard_map.137.refs_0_, f32[136,128]{1,0:T(8,128)S(1)} %collective-permute-done.refs_1_), custom_call_target="tpu_custom_call" | custom-call | tf_op jit(solution)/shard_map/pallas_call | solution.py:368
  32.6 2.0 %collective-permute-start.1 = (f32[128,128]{1,0:T(8,128)S(1)}, f32[128,128]{1,0:T(8,128)S(1)}, u32[]{:S(2)}, u32[]{:S(2)}) collective-permute-start(f32[128,128]{1,0:T(8,128)S(1)} %get-tuple-element.33.refs_2_), channel_id=1, source_target_pairs={{0,16},{2,18},{4,20},{6,22},{8,24},{10,26},{12,28},{14,30},{16,0},... | collective-permute-start | bytes 196616 | tf_op jit(solution)/shard_map/ppermute | solution.py:391
  34.7 1.1 %shard_map.139 = (f32[8,128,128]{2,1,0:T(8,128)S(1)}, f32[1280,128]{1,0:T(8,128)S(1)}) custom-call(f32[8,256,128]{2,1,0:T(8,128)S(1)} %all_to_all.10.swapped, bf16[128,128]{1,0:T(8,128)(2,1)S(1)} %copy-done.3, bf16[128,128]{1,0:T(8,128)(2,1)S(1)} %copy-done.4, f32[3,1024,128]{2,1,0:T(8,128)S(1)} %get-tuple-element.28.ready_ref, ...), custom_call_target="tpu_custom_call" | custom-call | tf_op jit(solution)/shard_map/pallas_call | solution.py:368
  35.8 2.8 %collective-permute-done.1.refs_3_ = f32[128,128]{1,0:T(8,128)S(1)} collective-permute-done((f32[128,128]{1,0:T(8,128)S(1)}, f32[128,128]{1,0:T(8,128)S(1)}, u32[]{:S(2)}, u32[]{:S(2)}) %collective-permute-start.1) | collective-permute-done | bytes 65568 | tf_op jit(solution)/shard_map/ppermute | solution.py:391
  38.6 1.7 %shard_map.140 = (f32[8,256,128]{2,1,0:T(8,128)}, f32[2,288,128]{2,1,0:T(8,128)S(1)}) custom-call(f32[8,256,128]{2,1,0:T(8,128)S(1)} %all_to_all.10.swapped, f32[64,128]{1,0:T(8,128)S(1)} %copy-done, bf16[128,128]{1,0:T(8,128)(2,1)S(1)} %copy-done.1, bf16[128,128]{1,0:T(8,128)(2,1)S(1)} %copy-done.2, f32[4,1024,128]{2,1,0:T(8,128)S(1)} %get-tuple-element.27.ready_ref, ...), custom_call_target="tpu_custom_call" | custom-call | tf_op jit(solution)/shard_map/pallas_call | solution.py:368
  40.3 0.0 copy-start.5
  40.3 3.6 %all-to-all-start.1 = ((f32[8,256,128]{2,1,0:T(8,128)}), f32[8,256,128]{2,1,0:T(8,128)S(1)}, u32[]{:S(2)}, u32[]{:S(2)}) async-start(f32[8,256,128]{2,1,0:T(8,128)} %get-tuple-element.35), calls=%async_computation.1 | async-start | bytes 2097152 | tf_op jit(solution)/shard_map/all_to_all | solution.py:387
  43.9 0.1 collective-permute-start.2
  44.0 1.3 %collective-permute-done.2 = f32[288,128]{1,0:T(8,128)S(1)} collective-permute-done((f32[288,128]{1,0:T(8,128)S(1)}, f32[288,128]{1,0:T(8,128)S(1)}, u32[]{:S(2)}, u32[]{:S(2)}) %collective-permute-start.2) | collective-permute-done | bytes 147488 | tf_op jit(solution)/shard_map/ppermute | solution.py:473
  45.4 2.9 %collective-permute-start.5 = (f32[72,128]{1,0:T(8,128)S(1)}, f32[72,128]{1,0:T(8,128)S(1)}, u32[]{:S(2)}, u32[]{:S(2)}) collective-permute-start(f32[72,128]{1,0:T(8,128)S(1)} %get-tuple-element.48), channel_id=1, source_target_pairs={{0,6},{2,4},{4,2},{6,0},{8,14},{10,12},{12,10},{14,8},{16,22},{18,... | collective-permute-start | bytes 110600 | tf_op jit(solution)/shard_map/ppermute | solution.py:476
  48.2 0.5 collective-permute-start.4
  48.8 0.1 collective-permute-start.3
  48.9 6.4 %collective-permute-done.5 = f32[72,128]{1,0:T(8,128)S(1)} collective-permute-done((f32[72,128]{1,0:T(8,128)S(1)}, f32[72,128]{1,0:T(8,128)S(1)}, u32[]{:S(2)}, u32[]{:S(2)}) %collective-permute-start.5) | collective-permute-done | bytes 36896 | tf_op jit(solution)/shard_map/ppermute | solution.py:476
  55.3 0.3 collective-permute-done.4
  55.6 0.0 collective-permute-done.3
  55.6 1.2 %collective-permute-start.6 = (f32[72,128]{1,0:T(8,128)S(1)}, f32[72,128]{1,0:T(8,128)S(1)}, u32[]{:S(2)}, u32[]{:S(2)}) collective-permute-start(f32[72,128]{1,0:T(8,128)S(1)} %fusion.1), channel_id=1, source_target_pairs={{0,8},{2,10},{4,12},{6,14},{8,0},{10,2},{12,4},{14,6},{16,24},{18,... | collective-permute-start | bytes 110600 | tf_op jit(solution)/shard_map/ppermute | solution.py:476
  56.8 2.8 %collective-permute-done.6 = f32[72,128]{1,0:T(8,128)S(1)} collective-permute-done((f32[72,128]{1,0:T(8,128)S(1)}, f32[72,128]{1,0:T(8,128)S(1)}, u32[]{:S(2)}, u32[]{:S(2)}) %collective-permute-start.6) | collective-permute-done | bytes 36896 | tf_op jit(solution)/shard_map/ppermute | solution.py:476
  59.6 2.0 %collective-permute-start.7 = (f32[72,128]{1,0:T(8,128)S(1)}, f32[72,128]{1,0:T(8,128)S(1)}, u32[]{:S(2)}, u32[]{:S(2)}) collective-permute-start(f32[72,128]{1,0:T(8,128)S(1)} %add.52), channel_id=1, source_target_pairs={{0,16},{2,18},{4,20},{6,22},{8,24},{10,26},{12,28},{14,30},{16,0},... | collective-permute-start | bytes 110600 | tf_op jit(solution)/shard_map/ppermute | solution.py:476
  61.6 0.0 all-to-all-done.1.rows_ref
  61.7 0.0 copy-done.5
  61.7 1.6 %shard_map.141 = (bf16[64,16,128]{2,1,0:T(8,128)(2,1)}, bf16[64,16,128]{2,1,0:T(8,128)(2,1)}) custom-call(f32[8,256,128]{2,1,0:T(8,128)S(1)} %all-to-all-done.1.rows_ref, s32[16,64]{1,0:T(8,128)S(1)} %bitcast.20), custom_call_target="tpu_custom_call" | custom-call | tf_op jit(solution)/shard_map/pallas_call | solution.py:368
  63.2 1.3 %collective-permute-done.7 = f32[72,128]{1,0:T(8,128)S(1)} collective-permute-done((f32[72,128]{1,0:T(8,128)S(1)}, f32[72,128]{1,0:T(8,128)S(1)}, u32[]{:S(2)}, u32[]{:S(2)}) %collective-permute-start.7) | collective-permute-done | bytes 36896 | tf_op jit(solution)/shard_map/ppermute | solution.py:476
  64.5 0.6 collective-permute-start.8
  65.1 0.6 collective-permute-start.9
  65.7 2.3 %collective-permute-start.10 = (f32[72,128]{1,0:T(8,128)S(1)}, f32[72,128]{1,0:T(8,128)S(1)}, u32[]{:S(2)}, u32[]{:S(2)}) collective-permute-start(f32[72,128]{1,0:T(8,128)S(1)} %add.53.refs_0_), channel_id=1, source_target_pairs={{0,6},{2,4},{4,2},{6,0},{8,14},{10,12},{12,10},{14,8},{16,22},{18,... | collective-permute-start | bytes 110600 | tf_op jit(solution)/shard_map/ppermute | solution.py:476
  68.0 0.5 collective-permute-done.8.refs_1_
  68.4 0.6 collective-permute-done.9.refs_2_
  69.0 1.5 %collective-permute-done.10.refs_3_ = f32[72,128]{1,0:T(8,128)S(1)} collective-permute-done((f32[72,128]{1,0:T(8,128)S(1)}, f32[72,128]{1,0:T(8,128)S(1)}, u32[]{:S(2)}, u32[]{:S(2)}) %collective-permute-start.10) | collective-permute-done | bytes 36896 | tf_op jit(solution)/shard_map/ppermute | solution.py:476
  70.5 0.7 shard_map.142
  (6 shorter events, 0.1 us)
Async XLA Ops:
  0.6 23.7 %copy-start = (f32[64,128]{1,0:T(8,128)S(1)}, f32[64,128]{1,0:T(8,128)}, u32[]{:S(2)}) copy-start(f32[64,128]{1,0:T(8,128)} %projector.5) | copy-start | bytes 98308
  0.6 23.7 %copy-start.1 = (bf16[128,128]{1,0:T(8,128)(2,1)S(1)}, bf16[128,128]{1,0:T(8,128)(2,1)}, u32[]{:S(2)}) copy-start(bf16[128,128]{1,0:T(8,128)(2,1)} %wk.5) | copy-start | bytes 98308
  0.7 23.7 %copy-start.2 = (bf16[128,128]{1,0:T(8,128)(2,1)S(1)}, bf16[128,128]{1,0:T(8,128)(2,1)}, u32[]{:S(2)}) copy-start(bf16[128,128]{1,0:T(8,128)(2,1)} %wv.5) | copy-start | bytes 98308
  0.7 27.1 %copy-start.3 = (bf16[128,128]{1,0:T(8,128)(2,1)S(1)}, bf16[128,128]{1,0:T(8,128)(2,1)}, u32[]{:S(2)}) copy-start(bf16[128,128]{1,0:T(8,128)(2,1)} %wq.3) | copy-start | bytes 98308
  0.7 27.1 %copy-start.4 = (bf16[128,128]{1,0:T(8,128)(2,1)S(1)}, bf16[128,128]{1,0:T(8,128)(2,1)}, u32[]{:S(2)}) copy-start(bf16[128,128]{1,0:T(8,128)(2,1)} %wo.3) | copy-start | bytes 98308
  25.1 6.0 %collective-permute-start = (f32[136,128]{1,0:T(8,128)S(1)}, f32[136,128]{1,0:T(8,128)S(1)}, u32[]{:S(2)}, u32[]{:S(2)}) collective-permute-start(f32[136,128]{1,0:T(8,128)S(1)} %shard_map.137.refs_0_), channel_id=1, source_target_pairs={{0,16},{2,18},{4,20},{6,22},{8,24},{10,26},{12,28},{14,30},{16,0},... | collective-permute-start | bytes 208904 | tf_op jit(solution)/shard_map/ppermute | solution.py:391
  32.6 5.9 %collective-permute-start.1 = (f32[128,128]{1,0:T(8,128)S(1)}, f32[128,128]{1,0:T(8,128)S(1)}, u32[]{:S(2)}, u32[]{:S(2)}) collective-permute-start(f32[128,128]{1,0:T(8,128)S(1)} %get-tuple-element.33.refs_2_), channel_id=1, source_target_pairs={{0,16},{2,18},{4,20},{6,22},{8,24},{10,26},{12,28},{14,30},{16,0},... | collective-permute-start | bytes 196616 | tf_op jit(solution)/shard_map/ppermute | solution.py:391
  40.3 21.4 %copy-start.5 = (s32[64,16]{0,1:T(8,128)S(1)}, s32[64,16]{0,1:T(8,128)}, u32[]{:S(2)}) copy-start(s32[64,16]{0,1:T(8,128)} %param.9) | copy-start | bytes 12292
  40.3 21.4 %all-to-all-start.1 = ((f32[8,256,128]{2,1,0:T(8,128)}), f32[8,256,128]{2,1,0:T(8,128)S(1)}, u32[]{:S(2)}, u32[]{:S(2)}) async-start(f32[8,256,128]{2,1,0:T(8,128)} %get-tuple-element.35), calls=%async_computation.1 | async-start | bytes 2097152 | tf_op jit(solution)/shard_map/all_to_all | solution.py:387
  43.9 1.4 %collective-permute-start.2 = (f32[288,128]{1,0:T(8,128)S(1)}, f32[288,128]{1,0:T(8,128)S(1)}, u32[]{:S(2)}, u32[]{:S(2)}) collective-permute-start(f32[288,128]{1,0:T(8,128)S(1)} %dynamic-slice_bitcast_fusion), channel_id=1, source_target_pairs={{0,1},{1,0},{2,3},{3,2},{4,5},{5,4},{6,7},{7,6},{8,9},{9,8},{10,11... | collective-permute-start | bytes 442376 | tf_op jit(solution)/shard_map/ppermute | solution.py:473
  45.4 9.9 %collective-permute-start.5 = (f32[72,128]{1,0:T(8,128)S(1)}, f32[72,128]{1,0:T(8,128)S(1)}, u32[]{:S(2)}, u32[]{:S(2)}) collective-permute-start(f32[72,128]{1,0:T(8,128)S(1)} %get-tuple-element.48), channel_id=1, source_target_pairs={{0,6},{2,4},{4,2},{6,0},{8,14},{10,12},{12,10},{14,8},{16,22},{18,... | collective-permute-start | bytes 110600 | tf_op jit(solution)/shard_map/ppermute | solution.py:476
  48.2 7.3 %collective-permute-start.4 = (f32[72,128]{1,0:T(8,128)S(1)}, f32[72,128]{1,0:T(8,128)S(1)}, u32[]{:S(2)}, u32[]{:S(2)}) collective-permute-start(f32[72,128]{1,0:T(8,128)S(1)} %get-tuple-element.49), channel_id=1, source_target_pairs={{0,4},{2,6},{4,0},{6,2},{8,12},{10,14},{12,8},{14,10},{16,20},{18,... | collective-permute-start | bytes 110600 | tf_op jit(solution)/shard_map/ppermute | solution.py:476
  48.8 6.8 %collective-permute-start.3 = (f32[72,128]{1,0:T(8,128)S(1)}, f32[72,128]{1,0:T(8,128)S(1)}, u32[]{:S(2)}, u32[]{:S(2)}) collective-permute-start(f32[72,128]{1,0:T(8,128)S(1)} %get-tuple-element.47), channel_id=1, source_target_pairs={{0,2},{2,0},{4,6},{6,4},{8,10},{10,8},{12,14},{14,12},{16,18},{18,... | collective-permute-start | bytes 110600 | tf_op jit(solution)/shard_map/ppermute | solution.py:476
  55.6 4.0 %collective-permute-start.6 = (f32[72,128]{1,0:T(8,128)S(1)}, f32[72,128]{1,0:T(8,128)S(1)}, u32[]{:S(2)}, u32[]{:S(2)}) collective-permute-start(f32[72,128]{1,0:T(8,128)S(1)} %fusion.1), channel_id=1, source_target_pairs={{0,8},{2,10},{4,12},{6,14},{8,0},{10,2},{12,4},{14,6},{16,24},{18,... | collective-permute-start | bytes 110600 | tf_op jit(solution)/shard_map/ppermute | solution.py:476
  59.6 4.9 %collective-permute-start.7 = (f32[72,128]{1,0:T(8,128)S(1)}, f32[72,128]{1,0:T(8,128)S(1)}, u32[]{:S(2)}, u32[]{:S(2)}) collective-permute-start(f32[72,128]{1,0:T(8,128)S(1)} %add.52), channel_id=1, source_target_pairs={{0,16},{2,18},{4,20},{6,22},{8,24},{10,26},{12,28},{14,30},{16,0},... | collective-permute-start | bytes 110600 | tf_op jit(solution)/shard_map/ppermute | solution.py:476
  64.5 4.0 %collective-permute-start.8 = (f32[72,128]{1,0:T(8,128)S(1)}, f32[72,128]{1,0:T(8,128)S(1)}, u32[]{:S(2)}, u32[]{:S(2)}) collective-permute-start(f32[72,128]{1,0:T(8,128)S(1)} %add.53.refs_0_), channel_id=1, source_target_pairs={{0,2},{2,0},{4,6},{6,4},{8,10},{10,8},{12,14},{14,12},{16,18},{18,... | collective-permute-start | bytes 110600 | tf_op jit(solution)/shard_map/ppermute | solution.py:476
  65.1 4.0 %collective-permute-start.9 = (f32[72,128]{1,0:T(8,128)S(1)}, f32[72,128]{1,0:T(8,128)S(1)}, u32[]{:S(2)}, u32[]{:S(2)}) collective-permute-start(f32[72,128]{1,0:T(8,128)S(1)} %add.53.refs_0_), channel_id=1, source_target_pairs={{0,4},{2,6},{4,0},{6,2},{8,12},{10,14},{12,8},{14,10},{16,20},{18,... | collective-permute-start | bytes 110600 | tf_op jit(solution)/shard_map/ppermute | solution.py:476
  65.7 4.9 %collective-permute-start.10 = (f32[72,128]{1,0:T(8,128)S(1)}, f32[72,128]{1,0:T(8,128)S(1)}, u32[]{:S(2)}, u32[]{:S(2)}) collective-permute-start(f32[72,128]{1,0:T(8,128)S(1)} %add.53.refs_0_), channel_id=1, source_target_pairs={{0,6},{2,4},{4,2},{6,0},{8,14},{10,12},{12,10},{14,8},{16,22},{18,... | collective-permute-start | bytes 110600 | tf_op jit(solution)/shard_map/ppermute | solution.py:476
